TPU v7x, 256 devices: a whole 4x4x8 slice. The times are simulated.
256 devices in a mesh: grp: 4 (over y), shard: 64 (over z, x, core).
Axes of the slice: x: 4, y: 4, z: 8, core: 2. Of those that a mesh axis runs over, the one named last changes fastest.
Arguments:
- head_vecs: bfloat16 [131072, 512], P(('grp', 'shard')), may hold values from -2 to 2
- tail_vecs: bfloat16 [131072, 512], P(('grp', 'shard')), may hold values from -2 to 2
- rel_id: int32 [131072], P(('grp', 'shard')), may hold values from 0 to 3
- head_owner: int32 [131072, 1], P(('grp', 'shard')), may hold values from 0 to 63; in each aligned block of 512 rows (0 to 511, 512 to 1023, ...) at most 16 rows name the same one
- head_row: int32 [131072], P(('grp', 'shard')), may hold values from 0 to 2047
- tail_owner: int32 [131072, 1], P(('grp', 'shard')), may hold values from 0 to 63; in each aligned block of 512 rows (0 to 511, 512 to 1023, ...) at most 16 rows name the same one
- tail_row: int32 [131072], P(('grp', 'shard')), may hold values from 0 to 2047
- neg_vecs: bfloat16 [4096, 512], P(('grp', 'shard')), may hold values from -2 to 2
- neg_owner: int32 [4096, 1], P(('grp', 'shard')), may hold values from 0 to 63; in each aligned block of 16 rows (0 to 15, 16 to 31, ...) at most 2 rows name the same one
- neg_row: int32 [4096], P(('grp', 'shard')), may hold values from 0 to 2047
- counts: int32 [4, 64], P('grp', 'shard'), may hold values from 1 to 512, 20480 in all within a row
- relations: bfloat16 [4, 512, 512], replicated, may hold values from -0.1 to 1.1
Outputs:
- entity_grad: float32 [4, 131072, 512], P('grp', 'shard')
- relation_grad: float32 [2048, 512], P(('grp', 'shard'))
Inputs may be any that keep to these rules, and one draw needn't show every extreme that they name: `head_owner`: no owner holds the heads of more than 16 triples of one device's 512 slots; some owner holds exactly 16. `tail_owner`: no owner holds the tails of more than 16 triples of one device's 512 slots; some owner holds exactly 16. `neg_owner`: no owner holds more than 2 of one device's 16 negatives; some owner holds exactly 2. Each group's counts sum to 20480, and some device of each group is full.
All inputs are finite; a program needn't handle non-finite values.
Results may differ from a plain program's by a relative error of at most 0.0045.
Values may be sent and summed in bfloat16 or wider, within the bound.
No kernel may reach another device: no remote copies, remote signals or barrier semaphores. Data moves between devices by JAX's collectives and lax.ppermute only.
A program may use at most 64 MiB of HBM per device.

v0:
```python
import jax
import jax.numpy as jnp
from jax import lax
from jax.sharding import PartitionSpec as P

CLS_DEV = 2048


def relation_apply(vectors, relation_ids, relations, transpose):
    result = jnp.zeros((vectors.shape[0], relations.shape[2]), jnp.float32)
    for index in range(relations.shape[0]):
        contract = 1 if transpose else 0
        product = lax.dot_general(
            vectors,
            relations[index],
            (((1,), (contract,)), ((), ())),
            preferred_element_type=jnp.float32,
        )
        result = result + jnp.where((relation_ids == index)[:, None], product, 0.0)
    return result


def pack_rows(values, owners, row_ids, capacity, owner_count, empty_id):
    onehot = (owners[:, None] == jnp.arange(owner_count, dtype=jnp.int32)[None, :]).astype(
        jnp.int32
    )
    rank = jnp.sum(jnp.cumsum(onehot, axis=0) * onehot, axis=1) - 1
    buffer = (
        jnp.zeros((owner_count, capacity, values.shape[1]), jnp.float32)
        .at[owners, rank]
        .set(values)
    )
    labels = jnp.full((owner_count, capacity), empty_id, jnp.int32).at[owners, rank].set(row_ids)
    return (buffer, labels)


def on_device(
    head_vecs,
    tail_vecs,
    rel_id,
    head_owner,
    head_row,
    tail_owner,
    tail_row,
    neg_vecs,
    neg_owner,
    neg_row,
    counts,
    relations,
):
    owner_count = lax.axis_size("shard")
    width = head_vecs.shape[1]
    slots = head_vecs.shape[0]
    negatives = lax.all_gather(neg_vecs, "shard", axis=0, tiled=True)
    query = relation_apply(head_vecs, rel_id, relations, False).astype(jnp.bfloat16)
    live = jnp.arange(slots, dtype=jnp.int32) < counts[0, 0]
    positive = jnp.sum(query.astype(jnp.float32) * tail_vecs.astype(jnp.float32), axis=1)
    scores = lax.dot_general(
        query, negatives, (((1,), (1,)), ((), ())), preferred_element_type=jnp.float32
    )
    top = jnp.maximum(positive, jnp.max(scores, axis=1))
    pos_exp = jnp.exp(positive - top)
    neg_exp = jnp.exp(scores - top[:, None])
    total = pos_exp + jnp.sum(neg_exp, axis=1)
    gpos = jnp.where(live, pos_exp / total - 1.0, 0.0)
    gneg = jnp.where(live[:, None], neg_exp / total[:, None], 0.0).astype(jnp.bfloat16)
    dquery = (
        gpos[:, None] * tail_vecs.astype(jnp.float32)
        + jnp.dot(gneg, negatives, preferred_element_type=jnp.float32)
    ).astype(jnp.bfloat16)
    dtail = gpos[:, None] * query.astype(jnp.float32)
    dhead = relation_apply(dquery, rel_id, relations, True)
    neg_terms = lax.dot_general(
        gneg, query, (((0,), (0,)), ((), ())), preferred_element_type=jnp.float32
    )
    blocks = []
    for index in range(relations.shape[0]):
        masked = jnp.where((rel_id == index)[:, None], dquery, jnp.zeros_like(dquery))
        blocks.append(
            lax.dot_general(
                head_vecs, masked, (((0,), (0,)), ((), ())), preferred_element_type=jnp.float32
            )
        )
    relation_terms = jnp.concatenate(blocks, axis=0)
    relation_grad = lax.psum_scatter(
        relation_terms, ("grp", "shard"), scatter_dimension=0, tiled=True
    )
    neg_grad = lax.psum_scatter(neg_terms, "shard", scatter_dimension=0, tiled=True)
    triple_vals = jnp.concatenate([dhead, dtail], axis=0)
    triple_owner = jnp.concatenate([head_owner[:, 0], tail_owner[:, 0]], axis=0)
    triple_ids = jnp.concatenate([head_row, tail_row], axis=0)
    cap_rows = max(2, 2 * slots // owner_count)
    cap_negs = max(2, 2 * neg_vecs.shape[0] // owner_count)
    tri_buffer, tri_labels = pack_rows(
        triple_vals, triple_owner, triple_ids, 2 * cap_rows, owner_count, CLS_DEV
    )
    neg_buffer, neg_labels = pack_rows(
        neg_grad, neg_owner[:, 0], neg_row, cap_negs, owner_count, CLS_DEV
    )
    send_vals = jnp.concatenate([tri_buffer, neg_buffer], axis=1)
    send_ids = jnp.concatenate([tri_labels, neg_labels], axis=1)
    got_vals, got_ids = (
        lax.all_to_all(send_vals, "shard", split_axis=0, concat_axis=0, tiled=True),
        lax.all_to_all(send_ids, "shard", split_axis=0, concat_axis=0, tiled=True),
    )
    flat_vals = got_vals.reshape(-1, width)
    flat_ids = got_ids.reshape(-1)
    owned = jax.ops.segment_sum(flat_vals, flat_ids, num_segments=CLS_DEV + 1)[:CLS_DEV]
    return (owned[None], relation_grad)


def solution(mesh):
    return jax.shard_map(
        on_device,
        mesh=mesh,
        in_specs=(
            P(("grp", "shard"), None),
            P(("grp", "shard"), None),
            P(("grp", "shard")),
            P(("grp", "shard"), None),
            P(("grp", "shard")),
            P(("grp", "shard"), None),
            P(("grp", "shard")),
            P(("grp", "shard"), None),
            P(("grp", "shard"), None),
            P(("grp", "shard")),
            P("grp", "shard"),
            P(),
        ),
        out_specs=(P("grp", "shard", None), P(("grp", "shard"), None)),
        check_vma=False,
    )
```

profile of v0, /device:TPU:2, one launch (start us, length us, event | category | flops | bytes accessed | tf_op | source)
XLA Modules:
  0.0 1543.3 jit_solution(3801368591167345655)
XLA Ops:
  7.2 0.7 all-gather.2.cloned.1.call-update
  8.6 0.7 constant_dynamic-update-slice_fusion.1
  9.3 0.7 pad_add_fusion.2
  10.0 18.0 %reduce-window.6 = s32[64,8,128]{2,1,0:T(8,128)S(1)} reduce-window(s32[64,8,128]{2,1,0:T(8,128)S(1)} %fusion.47, s32[]{:T(128)} %constant.14.clone.1), window={size=1x1x128 pad=0_0x0_0x127_0}, to_apply=%region_0.1 | reduce-window | flops 8323072 | bytes 524292 | tf_op jit(solution)/shard_map/reduce-window
  28.2 0.1 copy.20
  28.5 0.7 constant_dynamic-update-slice_fusion
  29.2 0.7 fusion.48
  29.9 0.7 pad_add_fusion.1
  30.6 0.7 pad_add_fusion.3
  31.6 0.4 convolution_select_fusion.4
  32.1 0.4 convolution_select_fusion.5
  32.5 0.4 convolution_select_fusion.6
  32.9 0.1 copy-done.1
  33.1 0.7 fusion.16
  33.8 55.5 %all-gather.2.cloned.1.call-done = bf16[1024,512]{1,0:T(8,128)(2,1)} async-done(((bf16[16,512]{1,0:T(8,128)(2,1)}), bf16[1024,512]{1,0:T(8,128)(2,1)}) %all-gather.2.cloned.1.call-update) | async-done | bytes 1048592 | tf_op jit(solution)/shard_map/all_gather | solution.py:54
  89.2 2.0 fusion.58
  91.3 0.5 fusion.7
  91.8 0.6 select_convert_fusion
  92.5 2.1 fusion.59
  94.9 4.3 scatter_custom_fusion.3
  99.3 0.2 select_reduce_fusion
  99.5 1.3 scatter_fusion
  100.8 0.7 copy.22
  101.5 7.9 all-to-all-start
  109.4 0.1 convert_multiply_fusion.2
  109.6 2.2 fusion.14
  111.8 0.5 convolution_select_fusion.1
  112.3 0.5 convolution_select_fusion.2
  112.8 0.5 convolution_select_fusion
  113.3 0.5 fusion.13
  113.8 7.4 scatter_custom_fusion.4
  121.1 0.5 convolution_bitcast_fusion
  121.6 111.7 %reduce-scatter.3.cloned.1.call-done = f32[16,512]{1,0:T(8,128)} async-done(((f32[1024,512]{1,0:T(8,128)}), f32[16,512]{1,0:T(8,128)}) %reduce-scatter.3.cloned.1.call-update) | async-done | bytes 32784 | tf_op jit(solution)/shard_map/reduce_scatter | solution.py:88
  233.4 1.8 scatter_fusion.1
  235.2 5.4 pad_maximum_fusion
  240.6 8.6 all-to-all-start.1
  249.2 0.5 convolution_bitcast_fusion.1
  249.8 0.5 convolution_bitcast_fusion.2
  250.3 0.5 convolution_bitcast_fusion.3
  250.8 2.5 pad_maximum_fusion.1
  253.4 0.5 broadcast.256
  253.9 0.7 reduce.10
  254.6 0.1 reshape.194
  254.7 113.0 %all-to-all-done.1 = f32[64,34,512]{2,1,0:T(8,128)} async-done(((f32[64,34,512]{2,1,0:T(8,128)}), f32[64,34,512]{2,1,0:T(8,128)}, u32[]{:S(2)}, u32[]{:S(2)}) %all-to-all-start.1) | async-done | bytes 4456480 | tf_op jit(solution)/shard_map/all_to_all | solution.py:103
  367.8 5.2 reshape.196
  373.0 19.1 %scatter_custom_fusion.2 = f32[2049,512]{1,0:T(8,128)} fusion(s32[2176]{0:T(1024)S(1)} %reshape.194, f32[2176,512]{1,0:T(8,128)} %reshape.196, f32[]{:T(128)} %constant.12.clone.1), kind=kCustom, calls=%fused_computation.8 | custom fusion | flops 1114112 | bytes 4196864 | tf_op jit(solution)/shard_map/scatter-add | solution.py:108
  392.1 4.7 slice_bitcast_fusion
  396.8 1140.0 %reduce-scatter.5.cloned.1.call-done = f32[8,512]{1,0:T(8,128)} async-done(((f32[2048,512]{1,0:T(8,128)}), f32[8,512]{1,0:T(8,128)}) %reduce-scatter.5.cloned.1.call-update) | async-done | bytes 16400 | tf_op jit(solution)/shard_map/reduce_scatter | solution.py:85
  (47 shorter events, 1.1 us)
Async XLA Ops:
  7.2 24.4 %copy-start = (bf16[512,512]{1,0:T(8,128)(2,1)S(1)}, bf16[512,512]{1,0:T(8,128)(2,1)}, u32[]{:S(2)}) copy-start(bf16[512,512]{1,0:T(8,128)(2,1)} %param.12) | copy-start | bytes 1572868
  7.2 24.4 %copy-start.5 = (s32[512]{0:T(512)S(1)}, s32[512]{0:T(512)}, u32[]{:S(2)}) copy-start(s32[512]{0:T(512)} %param.14) | copy-start | bytes 6148
  7.2 24.4 %copy-start.2 = (bf16[4,512,512]{2,1,0:T(8,128)(2,1)S(1)}, bf16[4,512,512]{2,1,0:T(8,128)(2,1)}, u32[]{:S(2)}) copy-start(bf16[4,512,512]{2,1,0:T(8,128)(2,1)} %param.23) | copy-start | bytes 6291460
  7.2 82.0 %all-gather.2.cloned.1.call-start = ((), (), s32[]{:S(2)}) async-start(), calls=%async_computation.4 | async-start | bytes 1064960 | tf_op jit(solution)/shard_map/all_gather | solution.py:54
  7.9 225.4 %reduce-scatter.3.cloned.1.call-start = ((), (), s32[]{:S(2)}) async-start(), calls=%async_computation.5 | async-start | bytes 2129920 | tf_op jit(solution)/shard_map/reduce_scatter | solution.py:88
  32.0 1.0 copy-start.1
  92.4 2.2 copy-start.9
  92.4 2.3 copy-start.7
  92.5 2.3 copy-start.8
  92.5 6.8 copy-start.4
  92.5 7.0 copy-start.6
  101.5 139.1 %all-to-all-start = ((s32[64,1,34]{2,1,0:T(1,128)}), s32[64,1,34]{2,1,0:T(1,128)S(1)}, u32[]{:S(2)}, u32[]{:S(2)}) async-start(s32[64,1,34]{2,1,0:T(1,128)} %copy.22), calls=%async_computation | async-start | bytes 65536 | tf_op jit(solution)/shard_map/all_to_all | solution.py:104
  109.6 2.3 copy-start.3
  240.6 127.2 %all-to-all-start.1 = ((f32[64,34,512]{2,1,0:T(8,128)}), f32[64,34,512]{2,1,0:T(8,128)}, u32[]{:S(2)}, u32[]{:S(2)}) async-start(f32[64,34,512]{2,1,0:T(8,128)} %pad_maximum_fusion), calls=%async_computation.2 | async-start | bytes 10485760 | tf_op jit(solution)/shard_map/all_to_all | solution.py:103
  249.2 1287.6 %reduce-scatter.5.cloned.1.call-start = ((), (), s32[]{:S(2)}) async-start(), calls=%async_computation.6 | async-start | bytes 4210688 | tf_op jit(solution)/shard_map/reduce_scatter | solution.py:85
Sparse Core Ops, SparseCore 0:
  10.8 78.3 all-gather.1
  94.8 138.5 reduce-scatter.2
  253.5 1283.2 reduce-scatter.4
where the time goes:
time: 1550 us; the launch traced here: 1540 us
  waiting for transfers between devices  1420 us (92%)
  other arithmetic  57.9 us (4%)
  local copies, waits for them, and re-layouts  20.7 us (1%)
  starting transfers between devices  16.6 us (1%)
    reduce_scatter x1, waiting for transfers between devices, on_device(): lax.psum_scatter(relation_terms, ('grp', 'shard'), scatter_dimension=0, t...  1140 us
    all_to_all x1, waiting for transfers between devices, on_device(): lax.all_to_all(send_vals, 'shard', split_axis=0, concat_axis=0, tiled=True)  113 us
    reduce_scatter x1, waiting for transfers between devices, on_device(): lax.psum_scatter(neg_terms, 'shard', scatter_dimension=0, tiled=True)  112 us
    all_gather x1, waiting for transfers between devices, on_device(): negatives = lax.all_gather(neg_vecs, 'shard', axis=0, tiled=True)  55.5 us
  transfers between devices with their start and end apart: 5, of which 4 were waited for; matrix products, arithmetic and copies ran while one was open for 6% of the time, Pallas kernels for 0%

commit v1 on v0

v1 whole, which is shorter than its diff:
```python
import jax
import jax.numpy as jnp
from jax import lax
from jax.experimental import pallas as pl
from jax.experimental.pallas import tpu as pltpu
from jax.sharding import Mesh, PartitionSpec as P

CLS_DEV = 2048
CAP = 16
CAP_N = 2
SIZES = {"y": 4, "z": 8, "x": 4, "c": 2}
SHARD = ("z", "x", "c")
ALL = ("y",) + SHARD
BF = jnp.bfloat16
F32 = jnp.float32


def swap(a, axis, flip):
    return lax.ppermute(a, axis, [(i, i ^ flip) for i in range(SIZES[axis])])


def ring_halves(blocks, axis, dtypes):
    me = lax.axis_index(axis)
    inner = (me == 1) | (me == 2)
    outer_set = jnp.stack([blocks[0], blocks[3]])
    inner_set = jnp.stack([blocks[1], blocks[2]])
    keep = jnp.where(inner, inner_set, outer_set)
    send = jnp.where(inner, outer_set, inner_set).astype(dtypes[0])
    keep = keep + swap(send, axis, 1).astype(F32)
    low = me < 2
    send = jnp.where(low, keep[1], keep[0]).astype(dtypes[1])
    return jnp.where(low, keep[0], keep[1]) + swap(send, axis, 3).astype(F32)


def cube_halves(blocks):
    me = lax.axis_index("z")
    for flip in (4, 2, 1):
        half = blocks.shape[0] // 2
        high = (me & flip) != 0
        send = jnp.where(high, blocks[:half], blocks[half:])
        keep = jnp.where(high, blocks[half:], blocks[:half])
        blocks = keep + swap(send, "z", flip)
    return blocks[0]


def slots_of(owners, cap):
    n = owners.shape[0]
    column = owners
    row = owners.reshape(1, n)
    before = lax.broadcasted_iota(jnp.int32, (n, n), 0) < lax.broadcasted_iota(jnp.int32, (n, n), 1)
    rank = jnp.sum(jnp.where((column == row) & before, 1, 0), axis=0, keepdims=True)
    return row * cap + rank


def onehot_of(slots, count):
    return lax.broadcasted_iota(jnp.int32, (count, slots.shape[1]), 0) == slots


def pick(hot, values):
    return jnp.sum(jnp.where(hot, values.reshape(1, -1), 0), axis=1)


def combine_kernel(tail_ref, head_ref, neg_ref, tl_ref, hl_ref, nl_ref, gp_ref, out_ref):
    rows = out_ref.shape[0]
    first = pl.program_id(0) * rows

    def hot(labels, weights):
        ids = lax.broadcasted_iota(jnp.int32, (rows, labels.shape[1]), 0) + first
        return jnp.where(ids == labels, weights, 0.0).astype(BF)

    total = jnp.dot(hot(tl_ref[...], gp_ref[...]), tail_ref[...], preferred_element_type=F32)
    total += jnp.dot(hot(hl_ref[...], 1.0), head_ref[...], preferred_element_type=F32)
    total += jnp.dot(hot(nl_ref[...], 1.0), neg_ref[...], preferred_element_type=F32)
    out_ref[...] = total


def combine(tails, heads, negs, tail_ids, head_ids, neg_ids, gpos):
    tile = 256
    args = (tails, heads, negs, tail_ids, head_ids, neg_ids, gpos)
    whole = lambda a: pl.BlockSpec(a.shape, lambda i: (0, 0))
    return pl.pallas_call(
        combine_kernel,
        grid=(CLS_DEV // tile,),
        in_specs=[whole(a) for a in args],
        out_specs=pl.BlockSpec((tile, tails.shape[1]), lambda i: (i, 0)),
        out_shape=jax.ShapeDtypeStruct((CLS_DEV, tails.shape[1]), F32),
        compiler_params=pltpu.CompilerParams(vmem_limit_bytes=40 * 2**20),
        name="combine",
    )(*args)


def on_device(
    head_vecs, tail_vecs, rel_id, head_owner, head_row, tail_owner, tail_row,
    neg_vecs, neg_owner, neg_row, counts, relations,
):
    n, width = head_vecs.shape
    rels = relations.shape[0]
    owners = SIZES["z"] * SIZES["x"] * SIZES["c"]
    core = lax.axis_index("c")

    with jax.named_scope("gather_negatives"):
        wide = jnp.broadcast_to(neg_vecs[None], (owners // 2,) + neg_vecs.shape)
        near = lax.all_to_all(wide, ("z", "x"), 0, 0, tiled=True).reshape(-1, width)
        negatives = jnp.concatenate([near, swap(near, "c", 1)], axis=0)

    with jax.named_scope("query"):
        of_rel = [(rel_id == r)[:, None] for r in range(rels)]
        spread = lambda v: jnp.concatenate([jnp.where(m, v, jnp.zeros_like(v)) for m in of_rel], axis=1)
        query = jnp.dot(spread(head_vecs), relations.reshape(rels * width, width), preferred_element_type=F32).astype(BF)
    with jax.named_scope("pack_tails"):
        tail_hot = onehot_of(slots_of(tail_owner, CAP), owners * CAP)
        tail_rows = jnp.dot(tail_hot.astype(BF), query, preferred_element_type=F32).astype(BF)
        got_tails = lax.all_to_all(tail_rows.reshape(owners, CAP, width), SHARD, 0, 0, tiled=True)

    with jax.named_scope("weights"):
        live = jnp.arange(n, dtype=jnp.int32) < counts[0, 0]
        positive = jnp.sum(query.astype(F32) * tail_vecs.astype(F32), axis=1)
        scores = lax.dot_general(query, negatives, (((1,), (1,)), ((), ())), preferred_element_type=F32)
        top = jnp.maximum(positive, jnp.max(scores, axis=1))
        pos_exp = jnp.exp(positive - top)
        neg_exp = jnp.exp(scores - top[:, None])
        total = pos_exp + jnp.sum(neg_exp, axis=1)
        gpos = jnp.where(live, pos_exp / total - 1.0, 0.0)
        gneg = jnp.where(live[:, None], neg_exp / total[:, None], 0.0).astype(BF)
    with jax.named_scope("dquery"):
        dquery = (
            gpos[:, None] * tail_vecs.astype(F32) + jnp.dot(gneg, negatives, preferred_element_type=F32)
        ).astype(BF)
        by_rel = spread(dquery)
    with jax.named_scope("pack_heads"):
        dhead = lax.dot_general(
            by_rel.reshape(n, rels, width), relations, (((1, 2), (0, 2)), ((), ())), preferred_element_type=F32
        ).astype(BF)
        head_hot = onehot_of(slots_of(head_owner, CAP), owners * CAP)
        head_rows = jnp.dot(head_hot.astype(BF), dhead, preferred_element_type=F32).astype(BF)
        got_heads = lax.all_to_all(head_rows.reshape(owners, CAP, width), SHARD, 0, 0, tiled=True)

    with jax.named_scope("neg_terms"):
        neg_terms = lax.dot_general(gneg, query, (((0,), (0,)), ((), ())), preferred_element_type=F32)
        half = neg_terms.shape[0] // 2
        own = neg_terms[:half] + swap(neg_terms[half:].astype(BF), "c", 1).astype(F32)
        own = own.reshape(8, 4, -1, width).transpose(1, 0, 2, 3)
        neg_grad = cube_halves(ring_halves(own, "x", (BF, F32)))
    with jax.named_scope("rel_terms"):
        rel_terms = lax.dot_general(head_vecs, by_rel, (((0,), (0,)), ((), ())), preferred_element_type=F32)
        cut = rel_terms.reshape(8, 4, 2, 8, rels * width)
        first, second = cut[:, :, 0], cut[:, :, 1]
        mine = jnp.where(core == 0, first, second)
        other = jnp.where(core == 0, second, first).astype(BF)
        mine = mine + swap(other, "c", 1).astype(F32)
        mine = jnp.stack([mine[..., r * width:(r + 1) * width] for r in range(rels)])
        mine = ring_halves(mine, "y", (BF, BF))
        relation_grad = cube_halves(ring_halves(mine.transpose(1, 0, 2, 3), "x", (F32, F32)))

    with jax.named_scope("small"):
        neg_hot = onehot_of(slots_of(neg_owner, CAP_N), owners * CAP_N)
        neg_rows = jnp.dot(neg_hot.astype(BF), neg_grad.astype(BF), preferred_element_type=F32).astype(BF)
        ids = [
            pick(hot, rows + 1).reshape(owners, -1)
            for hot, rows in ((tail_hot, tail_row), (head_hot, head_row), (neg_hot, neg_row))
        ]
        gp = pick(tail_hot, gpos).reshape(owners, CAP)
        gp_top = gp.astype(BF)
        extras = [(i >> 7).astype(BF) for i in ids] + [(i & 127).astype(BF) for i in ids]
        extras += [gp_top, (gp - gp_top.astype(F32)).astype(BF)]
        sizes = [e.shape[1] for e in extras]
        line = jnp.concatenate(extras, axis=1)
        line = jnp.pad(line, ((0, 0), (0, 1024 - line.shape[1])))
        packed = jnp.concatenate([neg_rows.reshape(owners, 8, 128), line.reshape(owners, 8, 128)], axis=1)
        got = lax.all_to_all(packed, SHARD, 0, 0, tiled=True)
        got_negs = got[:, :8].reshape(owners * CAP_N, width)
        line = got[:, 8:10].reshape(owners, 256).astype(F32)
        parts, at = [], 0
        for s in sizes:
            parts.append(line[:, at:at + s].reshape(1, -1))
            at += s
        got_ids = [(parts[i] * 128 + parts[i + 3]).astype(jnp.int32) - 1 for i in range(3)]
        got_gpos = parts[6] + parts[7]
    with jax.named_scope("combine"):
        owned = combine(
            got_tails.reshape(-1, width), got_heads.reshape(-1, width), got_negs,
            got_ids[0], got_ids[1], got_ids[2], got_gpos,
        )
    return owned[None], relation_grad


def solution(mesh):
    fine = Mesh(mesh.devices.reshape(*SIZES.values()), tuple(SIZES))
    whole = P(ALL)
    wide = P(ALL, None)
    return jax.shard_map(
        on_device,
        mesh=fine,
        in_specs=(
            wide, wide, whole, wide, whole, wide, whole, wide, wide, whole, P("y", SHARD), P(),
        ),
        out_specs=(P("y", SHARD, None), wide),
        check_vma=False,
    )
```

time: 1550 us -> 184 us (0.12)
  waiting for transfers between devices: 1420 us -> 61.6 us
  starting transfers between devices: 16.6 us -> 62.4 us
  other arithmetic: 57.9 us -> 21 us
    reduce_scatter x2 -> x0, waiting for transfers between devices: 1250 us -> none  [the longest x1 1140 us: on_device(): lax.psum_scatter(relation_terms, ('grp', 'shard'), scatter_dimension=0, t...]
    all_to_all x2 -> x4, waiting for transfers between devices: 113 us -> 11 us  [the longest x1 6.51 us: on_device(): near = lax.all_to_all(wide, ('z', 'x'), 0, 0, tiled=True).reshape(-1, width)]
    all_gather x1 -> x0, waiting for transfers between devices: 55.5 us -> none  [on_device(): negatives = lax.all_gather(neg_vecs, 'shard', axis=0, tiled=True)]
    ppermute x0 -> x15, waiting for transfers between devices: none -> 50.6 us  [swap(): return lax.ppermute(a, axis, [(i, i ^ flip) for i in range(SIZES[axis])])]
    ppermute x0 -> x15, starting transfers between devices: none -> 29.5 us  [swap(): return lax.ppermute(a, axis, [(i, i ^ flip) for i in range(SIZES[axis])])]
    scatter-add x1 -> x0, other arithmetic: 19.1 us -> none  [on_device(): jax.ops.segment_sum(flat_vals, flat_ids, num_segments=CLS_DEV + 1)[:CLS_DEV]]
    another operation x4 -> x0, other arithmetic: 18.2 us -> none
    all_to_all x2 -> x4, starting transfers between devices: 16.5 us -> 32.8 us  [the longest x1 11.7 us: on_device(): near = lax.all_to_all(wide, ('z', 'x'), 0, 0, tiled=True).reshape(-1, width)]
  transfers between devices with their start and end apart: 5 -> 19, of which waited for: 4 -> 11; matrix products, arithmetic and copies ran while one was open for 6% -> 23% of each run, Pallas kernels for 0% -> 5%
where the time goes in v1:
time: 184 us; the launch traced here: 183 us
  starting transfers between devices  62.4 us (34%)
  waiting for transfers between devices  61.6 us (33%)
  other arithmetic  21 us (11%)
  matrix products  15.8 us (9%)
  local copies, waits for them, and re-layouts  12.3 us (7%)
  Pallas kernels  8.29 us (5%)
  between operations  2.07 us (1%)
    ppermute x15, waiting for transfers between devices, swap(): return lax.ppermute(a, axis, [(i, i ^ flip) for i in range(SIZES[axis])])  50.6 us
    ppermute x15, starting transfers between devices, swap(): return lax.ppermute(a, axis, [(i, i ^ flip) for i in range(SIZES[axis])])  29.5 us
    all_to_all x1, starting transfers between devices, on_device(): near = lax.all_to_all(wide, ('z', 'x'), 0, 0, tiled=True).reshape(-1, width)  11.7 us
    all_to_all x1, starting transfers between devices, on_device(): got = lax.all_to_all(packed, SHARD, 0, 0, tiled=True)  9 us
    pallas_call x1, Pallas kernels, combine(): pl.pallas_call(combine_kernel, grid=(CLS_DEV // tile,), in_specs=[whole(a...  8.29 us
    all_to_all x1, waiting for transfers between devices, on_device(): near = lax.all_to_all(wide, ('z', 'x'), 0, 0, tiled=True).reshape(-1, width)  6.51 us
    all_to_all x1, starting transfers between devices, on_device(): lax.all_to_all(head_rows.reshape(owners, CAP, width), SHARD, 0, 0, tiled=...  6.19 us
    unnamed x71, local copies, waits for them, and re-layouts  5.97 us
  transfers between devices with their start and end apart: 19, of which 11 were waited for; matrix products, arithmetic and copies ran while one was open for 23% of the time, Pallas kernels for 5%

profile of v1, /device:TPU:2, one launch (start us, length us, event | category | flops | bytes accessed | tf_op | source)
XLA Modules:
  0.0 183.4 jit_solution(870680875546385792)
XLA Ops:
  0.7 1.7 broadcast_in_dim.137
  2.4 11.7 %all-to-all-start.1 = ((bf16[32,16,512]{2,1,0:T(8,128)(2,1)}), bf16[32,16,512]{2,1,0:T(8,128)(2,1)}, u32[]{:S(2)}, u32[]{:S(2)}) async-start(bf16[32,16,512]{2,1,0:T(8,128)(2,1)} %broadcast_in_dim.137), calls=%async_computation.1 | async-start | bytes 1048576 | tf_op jit(solution)/shard_map/gather_negatives/all_to_all | solution.py:103
  14.9 1.3 copy.36
  17.0 1.4 broadcast_select_fusion.7
  18.7 1.0 copy.40
  19.7 3.0 %fusion.18 = (f32[512]{0:T(512)S(1)}, bf16[512,512]{0,1:T(8,128)(2,1)S(1)}) fusion(bf16[512,512]{0,1:T(8,128)(2,1)} %copy.40, bf16[2048,512]{1,0:T(8,128)(2,1)S(1)} %bitcast.90, bf16[512,512]{0,1:T(8,128)(2,1)} %get-tuple-element.19, bf16[512,512]{0,1:T(8,128)(2,1)} %get-tuple-element.20, bf16[512,512]{0,1:T(8,128)(2,1)} %get-tuple-element.21, ...), kind=kOutput, calls=%fused_computation.31 | convolution fusion | flops 1083440640 | bytes 5244928 | tf_op jit(solution)/shard_map/query/dot_general | solution.py:109
  22.7 1.7 fusion.11
  24.5 6.5 %all-to-all-done.1 = bf16[32,16,512]{2,1,0:T(8,128)(2,1)} async-done(((bf16[32,16,512]{2,1,0:T(8,128)(2,1)}), bf16[32,16,512]{2,1,0:T(8,128)(2,1)}, u32[]{:S(2)}, u32[]{:S(2)}) %all-to-all-start.1) | async-done | bytes 524320 | tf_op jit(solution)/shard_map/gather_negatives/all_to_all | solution.py:103
  31.0 6.0 %all-to-all-start = ((bf16[64,16,512]{2,1,0:T(8,128)(2,1)}), bf16[64,16,512]{2,1,0:T(8,128)(2,1)S(1)}, u32[]{:S(2)}, u32[]{:S(2)}) async-start(bf16[64,16,512]{2,1,0:T(8,128)(2,1)} %bitcast.101), calls=%async_computation | async-start | bytes 2097152 | tf_op jit(solution)/shard_map/pack_tails/all_to_all | solution.py:113
  39.3 2.2 %fusion.48 = (f32[512]{0:T(512)S(1)}, f32[512,1024]{1,0:T(8,128)S(1)}) fusion(bf16[512,512]{0,1:T(8,128)(2,1)} %copy-done.10, bf16[512,512]{1,0:T(8,128)(2,1)} %collective-permute-done, bf16[512,512]{1,0:T(8,128)(2,1)} %bitcast.6), kind=kOutput, calls=%fused_computation.141 | convolution fusion | flops 539491840 | bytes 3672064 | tf_op jit(solution)/shard_map/weights/dot_general | solution.py:118
  44.1 2.1 %broadcast_select_fusion.6 = (bf16[512,512]{0,1:T(8,128)(2,1)S(1)}, bf16[512,512]{0,1:T(8,128)(2,1)S(1)}, bf16[512,512]{0,1:T(8,128)(2,1)S(1)}, bf16[512,512]{0,1:T(8,128)(2,1)S(1)}) fusion(pred[512]{0:T(512)(128)(4,1)S(1)} %get-tuple-element.30, pred[512]{0:T(512)(128)(4,1)S(1)} %get-tuple-element.32, pred[512]{0:T(512)(128)(4,1)S(1)} %get-tuple-element.33, ...), kind=kOutput, calls=%fused_computation.64 | convolution fusion | flops 541065216 | bytes 4722688 | tf_op jit(solution)/shard_map/dquery/dot_general | solution.py:127
  46.2 1.3 fusion.44
  48.6 1.6 fusion.19
  50.6 0.9 copy-done.6
  51.5 0.8 select_convert_fusion.4
  53.8 0.8 concatenate.18
  54.7 9.1 %collective-permute-done.2 = bf16[2,8,16,512]{3,2,0,1:T(8,128)(2,1)} collective-permute-done((bf16[2,8,16,512]{3,2,0,1:T(8,128)(2,1)}, bf16[2,8,16,512]{3,2,0,1:T(8,128)(2,1)}, u32[]{:S(2)}, u32[]{:S(2)}) %collective-permute-start.2) | collective-permute-done | bytes 262176 | tf_op jit(solution)/shard_map/neg_terms/ppermute | solution.py:19
  63.8 1.3 convert_add_fusion.1
  65.2 2.4 %collective-permute-start.3 = (f32[8,16,512]{2,1,0:T(8,128)S(1)}, f32[8,16,512]{2,1,0:T(8,128)S(1)}, u32[]{:S(2)}, u32[]{:S(2)}) collective-permute-start(f32[8,16,512]{2,1,0:T(8,128)S(1)} %select_bitcast_fusion), channel_id=1, source_target_pairs={{0,6},{2,4},{4,2},{6,0},{1,7},{3,5},{5,3},{7,1},{8,14},{10,12},{12... | collective-permute-start | bytes 786440 | tf_op jit(solution)/shard_map/neg_terms/ppermute | solution.py:19
  67.6 1.5 pad_maximum_fusion
  69.0 4.6 %collective-permute-done.3 = f32[8,16,512]{2,1,0:T(8,128)S(1)} collective-permute-done((f32[8,16,512]{2,1,0:T(8,128)S(1)}, f32[8,16,512]{2,1,0:T(8,128)S(1)}, u32[]{:S(2)}, u32[]{:S(2)}) %collective-permute-start.3) | collective-permute-done | bytes 262176 | tf_op jit(solution)/shard_map/neg_terms/ppermute | solution.py:19
  73.7 4.8 %collective-permute-start.4 = (f32[4,16,512]{2,1,0:T(8,128)S(1)}, f32[4,16,512]{2,1,0:T(8,128)S(1)}, u32[]{:S(2)}, u32[]{:S(2)}) collective-permute-start(f32[4,16,512]{2,1,0:T(8,128)S(1)} %slice_select_fusion.1), channel_id=1, source_target_pairs={{0,32},{8,40},{16,48},{24,56},{32,0},{40,8},{48,16},{56,24},{1,33}... | collective-permute-start | bytes 393224 | tf_op jit(solution)/shard_map/neg_terms/ppermute | solution.py:19
  78.5 1.7 bitcast_add_fusion
  80.6 1.6 collective-permute-start.8
  82.8 3.5 %collective-permute-start.5 = (f32[2,16,512]{2,1,0:T(8,128)S(1)}, f32[2,16,512]{2,1,0:T(8,128)S(1)}, u32[]{:S(2)}, u32[]{:S(2)}) collective-permute-start(f32[2,16,512]{2,1,0:T(8,128)S(1)} %slice_select_fusion.3), channel_id=1, source_target_pairs={{0,16},{8,24},{16,0},{24,8},{32,48},{40,56},{48,32},{56,40},{1,17}... | collective-permute-start | bytes 196616 | tf_op jit(solution)/shard_map/neg_terms/ppermute | solution.py:19
  86.4 2.3 %collective-permute-done.5 = f32[2,16,512]{2,1,0:T(8,128)S(1)} collective-permute-done((f32[2,16,512]{2,1,0:T(8,128)S(1)}, f32[2,16,512]{2,1,0:T(8,128)S(1)}, u32[]{:S(2)}, u32[]{:S(2)}) %collective-permute-start.5) | collective-permute-done | bytes 65568 | tf_op jit(solution)/shard_map/neg_terms/ppermute | solution.py:19
  88.7 3.3 %collective-permute-start.6 = (f32[1,16,512]{2,1,0:T(8,128)S(1)}, f32[1,16,512]{2,1,0:T(8,128)S(1)}, u32[]{:S(2)}, u32[]{:S(2)}) collective-permute-start(f32[1,16,512]{2,1,0:T(8,128)S(1)} %slice_select_fusion.5), channel_id=1, source_target_pairs={{0,8},{8,0},{16,24},{24,16},{32,40},{40,32},{48,56},{56,48},{1,9},... | collective-permute-start | bytes 98312 | tf_op jit(solution)/shard_map/neg_terms/ppermute | solution.py:19
  92.1 0.9 collective-permute-done.8
  93.3 1.0 copy-done.5
  94.3 0.8 fusion.26
  95.1 3.0 %collective-permute-start.9 = (bf16[8,4,8,512]{3,2,0,1:T(8,128)(2,1)}, bf16[8,4,8,512]{3,2,0,1:T(8,128)(2,1)}, u32[]{:S(2)}, u32[]{:S(2)}) collective-permute-start(bf16[8,4,8,512]{3,2,0,1:T(8,128)(2,1)} %fusion.26), channel_id=1, source_target_pairs={{0,192},{64,128},{128,64},{192,0},{1,193},{65,129},{129,65},{193,1... | collective-permute-start | bytes 786440 | tf_op jit(solution)/shard_map/rel_terms/ppermute | solution.py:19
  99.2 3.7 %collective-permute-done.9 = bf16[8,4,8,512]{3,2,0,1:T(8,128)(2,1)} collective-permute-done((bf16[8,4,8,512]{3,2,0,1:T(8,128)(2,1)}, bf16[8,4,8,512]{3,2,0,1:T(8,128)(2,1)}, u32[]{:S(2)}, u32[]{:S(2)}) %collective-permute-start.9) | collective-permute-done | bytes 262176 | tf_op jit(solution)/shard_map/rel_terms/ppermute | solution.py:19
  103.0 1.4 fusion.25
  105.2 1.5 collective-permute-start.10
  106.7 9.0 %all-to-all-start.3 = ((bf16[64,16,128]{2,1,0:T(8,128)(2,1)}), bf16[64,16,128]{2,1,0:T(8,128)(2,1)}, u32[]{:S(2)}, u32[]{:S(2)}) async-start(bf16[64,16,128]{2,1,0:T(8,128)(2,1)} %pad_maximum_fusion.7), calls=%async_computation.3 | async-start | bytes 524288 | tf_op jit(solution)/shard_map/small/all_to_all | solution.py:170
  115.8 4.5 %fusion.12 = bf16[1024,512]{1,0:T(8,128)(2,1)} fusion(s32[512]{0:T(512)S(1)} %copy-done.26, bf16[512,4,512]{0,2,1:T(8,128)(2,1)} %bitcast.97, bf16[4,512,512]{2,1,0:T(8,128)(2,1)S(1)} %copy-done), kind=kOutput, calls=%fused_computation.22 | convolution fusion | flops 1611923456 | bytes 5244928 | tf_op jit(solution)/shard_map/pack_heads/dot_general | solution.py:135
  120.2 1.1 select_add_fusion
  122.0 1.5 collective-permute-start.11
  123.5 4.5 %all-to-all-done.3 = bf16[64,16,128]{2,1,0:T(8,128)(2,1)} async-done(((bf16[64,16,128]{2,1,0:T(8,128)(2,1)}), bf16[64,16,128]{2,1,0:T(8,128)(2,1)}, u32[]{:S(2)}, u32[]{:S(2)}) %all-to-all-start.3) | async-done | bytes 262176 | tf_op jit(solution)/shard_map/small/all_to_all | solution.py:170
  128.0 6.2 %all-to-all-start.2 = ((bf16[64,16,512]{2,1,0:T(8,128)(2,1)}), bf16[64,16,512]{2,1,0:T(8,128)(2,1)}, u32[]{:S(2)}, u32[]{:S(2)}) async-start(bf16[64,16,512]{2,1,0:T(8,128)(2,1)} %bitcast.102), calls=%async_computation.2 | async-start | bytes 2097152 | tf_op jit(solution)/shard_map/pack_heads/all_to_all | solution.py:136
  134.2 0.9 slice_convert_fusion.1
  135.2 5.7 %collective-permute-start.12 = (f32[4,8,512]{2,1,0:T(8,128)S(1)}, f32[4,8,512]{2,1,0:T(8,128)S(1)}, u32[]{:S(2)}, u32[]{:S(2)}) collective-permute-start(f32[4,8,512]{2,1,0:T(8,128)S(1)} %slice_select_fusion.2), channel_id=1, source_target_pairs={{0,32},{8,40},{16,48},{24,56},{32,0},{40,8},{48,16},{56,24},{1,33}... | collective-permute-start | bytes 196616 | tf_op jit(solution)/shard_map/rel_terms/ppermute | solution.py:19
  141.6 24.1 %collective-permute-done.12 = f32[4,8,512]{2,1,0:T(8,128)S(1)} collective-permute-done((f32[4,8,512]{2,1,0:T(8,128)S(1)}, f32[4,8,512]{2,1,0:T(8,128)S(1)}, u32[]{:S(2)}, u32[]{:S(2)}) %collective-permute-start.12) | collective-permute-done | bytes 65568 | tf_op jit(solution)/shard_map/rel_terms/ppermute | solution.py:19
  166.4 4.6 %collective-permute-done.13 = f32[2,8,512]{2,1,0:T(8,128)S(1)} collective-permute-done((f32[2,8,512]{2,1,0:T(8,128)S(1)}, f32[2,8,512]{2,1,0:T(8,128)S(1)}, u32[]{:S(2)}, u32[]{:S(2)}) %collective-permute-start.13) | collective-permute-done | bytes 32800 | tf_op jit(solution)/shard_map/rel_terms/ppermute | solution.py:19
  171.6 0.9 slice.197
  172.6 0.8 sub.51.tl_ref
  173.7 8.3 %combine.1 = f32[2048,512]{1,0:T(8,128)} custom-call(bf16[1024,512]{1,0:T(8,128)(2,1)S(1)} %bitcast.91, bf16[1024,512]{1,0:T(8,128)(2,1)} %bitcast.10.head_ref, bf16[128,512]{1,0:T(8,128)(2,1)S(1)} %reshape.346.neg_ref, s32[1,1024]{1,0:T(1,128)S(1)} %sub.51.tl_ref, s32[1,1024]{1,0:T(1,128)S(1)} %sub.53.hl_ref, s32[1,128]{1,0:T(1,128)S(1)} %sub.55.nl_ref, ...), custom_call_target="tpu_custom_call" | custom-call | tf_op jit(solution)/shard_map/combine/combine/pallas_call | solution.py:81
  182.0 1.3 add_bitcast_fusion
  (145 shorter events, 15.4 us)
Async XLA Ops:
  0.6 19.1 %copy-start = (bf16[4,512,512]{2,1,0:T(8,128)(2,1)S(1)}, bf16[4,512,512]{2,1,0:T(8,128)(2,1)}, u32[]{:S(2)}) copy-start(bf16[4,512,512]{2,1,0:T(8,128)(2,1)} %param.23) | copy-start | bytes 6291460
  0.6 15.5 %copy-start.31 = (s32[16,1]{0,1:T(1,128)S(1)}, s32[16,1]{0,1:T(1,128)}, u32[]{:S(2)}) copy-start(s32[16,1]{0,1:T(1,128)} %param.20) | copy-start | bytes 196
  0.7 15.6 %copy-start.23 = (s32[512,1]{0,1:T(1,128)S(1)}, s32[512,1]{0,1:T(1,128)}, u32[]{:S(2)}) copy-start(s32[512,1]{0,1:T(1,128)} %param.17) | copy-start | bytes 6148
  0.7 15.8 %copy-start.27 = (s32[512]{0:T(512)S(1)}, s32[512]{0:T(512)}, u32[]{:S(2)}) copy-start(s32[512]{0:T(512)} %param.18) | copy-start | bytes 6148
  0.7 16.1 %copy-start.24 = (s32[512,1]{0,1:T(1,128)S(1)}, s32[512,1]{0,1:T(1,128)}, u32[]{:S(2)}) copy-start(s32[512,1]{0,1:T(1,128)} %param.15) | copy-start | bytes 6148
  0.7 16.3 %copy-start.28 = (s32[512]{0:T(512)S(1)}, s32[512]{0:T(512)}, u32[]{:S(2)}) copy-start(s32[512]{0:T(512)} %param.16) | copy-start | bytes 6148
  2.4 28.6 %all-to-all-start.1 = ((bf16[32,16,512]{2,1,0:T(8,128)(2,1)}), bf16[32,16,512]{2,1,0:T(8,128)(2,1)}, u32[]{:S(2)}, u32[]{:S(2)}) async-start(bf16[32,16,512]{2,1,0:T(8,128)(2,1)} %broadcast_in_dim.137), calls=%async_computation.1 | async-start | bytes 1048576 | tf_op jit(solution)/shard_map/gather_negatives/all_to_all | solution.py:103
  14.1 4.6 %copy-start.12 = (bf16[512,512]{1,0:T(8,128)(2,1)S(1)}, bf16[512,512]{1,0:T(8,128)(2,1)}, u32[]{:S(2)}) copy-start(bf16[512,512]{1,0:T(8,128)(2,1)} %param.13) | copy-start | bytes 1572868
  16.2 22.0 %copy-start.29 = (s32[16]{0:T(128)}, s32[16]{0:T(128)S(1)}, u32[]{:S(2)}) copy-start(s32[16]{0:T(128)S(1)} %multiply_add_fusion.2) | copy-start | bytes 196
  17.0 5.7 %copy-start.25 = (s32[512]{0:T(512)}, s32[512]{0:T(512)S(1)}, u32[]{:S(2)}) copy-start(s32[512]{0:T(512)S(1)} %get-tuple-element.42) | copy-start | bytes 6148
  22.7 8.3 %copy-start.10 = (bf16[512,512]{0,1:T(8,128)(2,1)}, bf16[512,512]{0,1:T(8,128)(2,1)S(1)}, u32[]{:S(2)}) copy-start(bf16[512,512]{0,1:T(8,128)(2,1)S(1)} %get-tuple-element.37) | copy-start | bytes 1572868
  22.7 14.5 %copy-start.32 = (s32[16]{0:T(128)S(1)}, s32[16]{0:T(128)}, u32[]{:S(2)}) copy-start(s32[16]{0:T(128)} %param.21) | copy-start | bytes 196
  31.0 75.7 %all-to-all-start = ((bf16[64,16,512]{2,1,0:T(8,128)(2,1)}), bf16[64,16,512]{2,1,0:T(8,128)(2,1)S(1)}, u32[]{:S(2)}, u32[]{:S(2)}) async-start(bf16[64,16,512]{2,1,0:T(8,128)(2,1)} %bitcast.101), calls=%async_computation | async-start | bytes 2097152 | tf_op jit(solution)/shard_map/pack_tails/all_to_all | solution.py:113
  37.0 2.3 %collective-permute-start = (bf16[512,512]{1,0:T(8,128)(2,1)}, bf16[512,512]{1,0:T(8,128)(2,1)}, u32[]{:S(2)}, u32[]{:S(2)}) collective-permute-start(bf16[512,512]{1,0:T(8,128)(2,1)} %bitcast.6), channel_id=1, source_target_pairs={{0,1},{1,0},{2,3},{3,2},{4,5},{5,4},{6,7},{7,6},{8,9},{9,8},{10,11... | collective-permute-start | bytes 1572872 | tf_op jit(solution)/shard_map/gather_negatives/ppermute | solution.py:19
  42.0 1.0 copy-start.11
  43.1 1.0 copy-start.14
  44.1 2.1 %copy-start.13 = (bf16[512,512]{1,0:T(8,128)(2,1)S(1)}, bf16[512,512]{1,0:T(8,128)(2,1)}, u32[]{:S(2)}) copy-start(bf16[512,512]{1,0:T(8,128)(2,1)} %param.12) | copy-start | bytes 1572868
  46.2 1.4 copy-start.15
  46.2 1.4 copy-start.17
  46.2 1.4 copy-start.19
  46.2 1.4 copy-start.21
  48.1 2.1 %copy-start.1 = (f32[8,4,1,8,2048]{4,3,2,1,0:T(8,128)}, f32[8,4,1,8,2048]{4,3,2,1,0:T(8,128)S(1)}, u32[]{:S(2)}) copy-start(f32[8,4,1,8,2048]{4,3,2,1,0:T(8,128)S(1)} %get-tuple-element.4) | copy-start | bytes 6291460
  48.1 2.3 %copy-start.3 = (f32[8,4,1,8,2048]{4,3,2,1,0:T(8,128)}, f32[8,4,1,8,2048]{4,3,2,1,0:T(8,128)S(1)}, u32[]{:S(2)}) copy-start(f32[8,4,1,8,2048]{4,3,2,1,0:T(8,128)S(1)} %get-tuple-element.5) | copy-start | bytes 6291460
  48.2 2.2 %collective-permute-start.1 = (bf16[512,512]{1,0:T(8,128)(2,1)S(1)}, bf16[512,512]{1,0:T(8,128)(2,1)S(1)}, u32[]{:S(2)}, u32[]{:S(2)}) collective-permute-start(bf16[512,512]{1,0:T(8,128)(2,1)S(1)} %slice.304), channel_id=1, source_target_pairs={{0,1},{1,0},{2,3},{3,2},{4,5},{5,4},{6,7},{7,6},{8,9},{9,8},{10,11... | collective-permute-start | bytes 1572872 | tf_op jit(solution)/shard_map/neg_terms/ppermute | solution.py:19
  50.6 1.7 copy-start.8
  52.3 11.5 %collective-permute-start.2 = (bf16[2,8,16,512]{3,2,0,1:T(8,128)(2,1)}, bf16[2,8,16,512]{3,2,0,1:T(8,128)(2,1)}, u32[]{:S(2)}, u32[]{:S(2)}) collective-permute-start(bf16[2,8,16,512]{3,2,0,1:T(8,128)(2,1)} %select_convert_fusion.4), channel_id=1, source_target_pairs={{0,2},{2,0},{4,6},{6,4},{1,3},{3,1},{5,7},{7,5},{8,10},{10,8},{12,... | collective-permute-start | bytes 786440 | tf_op jit(solution)/shard_map/neg_terms/ppermute | solution.py:19
  53.0 25.5 %collective-permute-start.7 = (bf16[8,4,8,2048]{3,2,0,1:T(8,128)(2,1)}, bf16[8,4,8,2048]{3,2,0,1:T(8,128)(2,1)}, u32[]{:S(2)}, u32[]{:S(2)}) collective-permute-start(bf16[8,4,8,2048]{3,2,0,1:T(8,128)(2,1)} %fusion.19), channel_id=1, source_target_pairs={{0,1},{1,0},{2,3},{3,2},{4,5},{5,4},{6,7},{7,6},{8,9},{9,8},{10,11... | collective-permute-start | bytes 3145736 | tf_op jit(solution)/shard_map/rel_terms/ppermute | solution.py:19
  54.7 12.9 %copy-start.16 = (bf16[512,512]{0,1:T(8,128)(2,1)S(1)}, bf16[512,512]{0,1:T(8,128)(2,1)}, u32[]{:S(2)}) copy-start(bf16[512,512]{0,1:T(8,128)(2,1)} %copy-done.15) | copy-start | bytes 1572868
  54.7 12.9 %copy-start.18 = (bf16[512,512]{0,1:T(8,128)(2,1)S(1)}, bf16[512,512]{0,1:T(8,128)(2,1)}, u32[]{:S(2)}) copy-start(bf16[512,512]{0,1:T(8,128)(2,1)} %copy-done.17) | copy-start | bytes 1572868
  54.7 12.9 %copy-start.20 = (bf16[512,512]{0,1:T(8,128)(2,1)S(1)}, bf16[512,512]{0,1:T(8,128)(2,1)}, u32[]{:S(2)}) copy-start(bf16[512,512]{0,1:T(8,128)(2,1)} %copy-done.19) | copy-start | bytes 1572868
  54.7 12.9 %copy-start.22 = (bf16[512,512]{0,1:T(8,128)(2,1)S(1)}, bf16[512,512]{0,1:T(8,128)(2,1)}, u32[]{:S(2)}) copy-start(bf16[512,512]{0,1:T(8,128)(2,1)} %copy-done.21) | copy-start | bytes 1572868
  65.2 13.3 %copy-start.2 = (f32[8,4,1,8,2048]{4,3,2,1,0:T(8,128)S(1)}, f32[8,4,1,8,2048]{4,3,2,1,0:T(8,128)}, u32[]{:S(2)}) copy-start(f32[8,4,1,8,2048]{4,3,2,1,0:T(8,128)} %copy-done.1) | copy-start | bytes 6291460
  65.2 13.3 %copy-start.4 = (f32[8,4,1,8,2048]{4,3,2,1,0:T(8,128)S(1)}, f32[8,4,1,8,2048]{4,3,2,1,0:T(8,128)}, u32[]{:S(2)}) copy-start(f32[8,4,1,8,2048]{4,3,2,1,0:T(8,128)} %copy-done.3) | copy-start | bytes 6291460
  65.2 8.4 %collective-permute-start.3 = (f32[8,16,512]{2,1,0:T(8,128)S(1)}, f32[8,16,512]{2,1,0:T(8,128)S(1)}, u32[]{:S(2)}, u32[]{:S(2)}) collective-permute-start(f32[8,16,512]{2,1,0:T(8,128)S(1)} %select_bitcast_fusion), channel_id=1, source_target_pairs={{0,6},{2,4},{4,2},{6,0},{1,7},{3,5},{5,3},{7,1},{8,14},{10,12},{12... | collective-permute-start | bytes 786440 | tf_op jit(solution)/shard_map/neg_terms/ppermute | solution.py:19
  73.7 9.1 %collective-permute-start.4 = (f32[4,16,512]{2,1,0:T(8,128)S(1)}, f32[4,16,512]{2,1,0:T(8,128)S(1)}, u32[]{:S(2)}, u32[]{:S(2)}) collective-permute-start(f32[4,16,512]{2,1,0:T(8,128)S(1)} %slice_select_fusion.1), channel_id=1, source_target_pairs={{0,32},{8,40},{16,48},{24,56},{32,0},{40,8},{48,16},{56,24},{1,33}... | collective-permute-start | bytes 393224 | tf_op jit(solution)/shard_map/neg_terms/ppermute | solution.py:19
  80.6 12.4 %collective-permute-start.8 = (bf16[2,8,4,8,512]{4,3,1,2,0:T(8,128)(2,1)S(1)}, bf16[2,8,4,8,512]{4,3,1,2,0:T(8,128)(2,1)S(1)}, u32[]{:S(2)}, u32[]{:S(2)}) collective-permute-start(bf16[2,8,4,8,512]{4,3,1,2,0:T(8,128)(2,1)S(1)} %select_convert_fusion.2), channel_id=1, source_target_pairs={{0,64},{64,0},{128,192},{192,128},{1,65},{65,1},{129,193},{193,129... | collective-permute-start | bytes 1572872 | tf_op jit(solution)/shard_map/rel_terms/ppermute | solution.py:19
  82.8 5.9 %collective-permute-start.5 = (f32[2,16,512]{2,1,0:T(8,128)S(1)}, f32[2,16,512]{2,1,0:T(8,128)S(1)}, u32[]{:S(2)}, u32[]{:S(2)}) collective-permute-start(f32[2,16,512]{2,1,0:T(8,128)S(1)} %slice_select_fusion.3), channel_id=1, source_target_pairs={{0,16},{8,24},{16,0},{24,8},{32,48},{40,56},{48,32},{56,40},{1,17}... | collective-permute-start | bytes 196616 | tf_op jit(solution)/shard_map/neg_terms/ppermute | solution.py:19
  88.7 9.4 %copy-start.30 = (s32[16]{0:T(128)S(1)}, s32[16]{0:T(128)}, u32[]{:S(2)}) copy-start(s32[16]{0:T(128)} %copy-done.29) | copy-start | bytes 196
  88.7 9.4 %collective-permute-start.6 = (f32[1,16,512]{2,1,0:T(8,128)S(1)}, f32[1,16,512]{2,1,0:T(8,128)S(1)}, u32[]{:S(2)}, u32[]{:S(2)}) collective-permute-start(f32[1,16,512]{2,1,0:T(8,128)S(1)} %slice_select_fusion.5), channel_id=1, source_target_pairs={{0,8},{8,0},{16,24},{24,16},{32,40},{40,32},{48,56},{56,48},{1,9},... | collective-permute-start | bytes 98312 | tf_op jit(solution)/shard_map/neg_terms/ppermute | solution.py:19
  95.1 7.9 %collective-permute-start.9 = (bf16[8,4,8,512]{3,2,0,1:T(8,128)(2,1)}, bf16[8,4,8,512]{3,2,0,1:T(8,128)(2,1)}, u32[]{:S(2)}, u32[]{:S(2)}) collective-permute-start(bf16[8,4,8,512]{3,2,0,1:T(8,128)(2,1)} %fusion.26), channel_id=1, source_target_pairs={{0,192},{64,128},{128,64},{192,0},{1,193},{65,129},{129,65},{193,1... | collective-permute-start | bytes 786440 | tf_op jit(solution)/shard_map/rel_terms/ppermute | solution.py:19
  98.5 17.3 %copy-start.26 = (s32[512]{0:T(512)S(1)}, s32[512]{0:T(512)}, u32[]{:S(2)}) copy-start(s32[512]{0:T(512)} %copy-done.25) | copy-start | bytes 6148
  105.2 15.0 %collective-permute-start.10 = (f32[2,8,8,512]{3,2,1,0:T(8,128)S(1)}, f32[2,8,8,512]{3,2,1,0:T(8,128)}, u32[]{:S(2)}, u32[]{:S(2)}) collective-permute-start(f32[2,8,8,512]{3,2,1,0:T(8,128)S(1)} %slice_select_fusion), channel_id=1, source_target_pairs={{0,2},{2,0},{4,6},{6,4},{1,3},{3,1},{5,7},{7,5},{8,10},{10,8},{12,... | collective-permute-start | bytes 786440 | tf_op jit(solution)/shard_map/rel_terms/ppermute | solution.py:19
  106.7 21.2 %all-to-all-start.3 = ((bf16[64,16,128]{2,1,0:T(8,128)(2,1)}), bf16[64,16,128]{2,1,0:T(8,128)(2,1)}, u32[]{:S(2)}, u32[]{:S(2)}) async-start(bf16[64,16,128]{2,1,0:T(8,128)(2,1)} %pad_maximum_fusion.7), calls=%async_computation.3 | async-start | bytes 524288 | tf_op jit(solution)/shard_map/small/all_to_all | solution.py:170
  122.0 13.1 %collective-permute-start.11 = (f32[8,8,512]{2,1,0:T(8,128)}, f32[8,8,512]{2,1,0:T(8,128)S(1)}, u32[]{:S(2)}, u32[]{:S(2)}) collective-permute-start(f32[8,8,512]{2,1,0:T(8,128)} %select_bitcast_fusion.1), channel_id=1, source_target_pairs={{0,6},{2,4},{4,2},{6,0},{1,7},{3,5},{5,3},{7,1},{8,14},{10,12},{12... | collective-permute-start | bytes 393224 | tf_op jit(solution)/shard_map/rel_terms/ppermute | solution.py:19
  128.0 45.7 %all-to-all-start.2 = ((bf16[64,16,512]{2,1,0:T(8,128)(2,1)}), bf16[64,16,512]{2,1,0:T(8,128)(2,1)}, u32[]{:S(2)}, u32[]{:S(2)}) async-start(bf16[64,16,512]{2,1,0:T(8,128)(2,1)} %bitcast.102), calls=%async_computation.2 | async-start | bytes 2097152 | tf_op jit(solution)/shard_map/pack_heads/all_to_all | solution.py:136
  135.2 30.5 %collective-permute-start.12 = (f32[4,8,512]{2,1,0:T(8,128)S(1)}, f32[4,8,512]{2,1,0:T(8,128)S(1)}, u32[]{:S(2)}, u32[]{:S(2)}) collective-permute-start(f32[4,8,512]{2,1,0:T(8,128)S(1)} %slice_select_fusion.2), channel_id=1, source_target_pairs={{0,32},{8,40},{16,48},{24,56},{32,0},{40,8},{48,16},{56,24},{1,33}... | collective-permute-start | bytes 196616 | tf_op jit(solution)/shard_map/rel_terms/ppermute | solution.py:19
  165.7 5.3 %collective-permute-start.13 = (f32[2,8,512]{2,1,0:T(8,128)S(1)}, f32[2,8,512]{2,1,0:T(8,128)S(1)}, u32[]{:S(2)}, u32[]{:S(2)}) collective-permute-start(f32[2,8,512]{2,1,0:T(8,128)S(1)} %slice_select_fusion.4), channel_id=1, source_target_pairs={{0,16},{8,24},{16,0},{24,8},{32,48},{40,56},{48,32},{56,40},{1,17}... | collective-permute-start | bytes 98312 | tf_op jit(solution)/shard_map/rel_terms/ppermute | solution.py:19
  171.0 11.0 %collective-permute-start.14 = (f32[1,8,512]{2,1,0:T(8,128)S(1)}, f32[1,8,512]{2,1,0:T(8,128)}, u32[]{:S(2)}, u32[]{:S(2)}) collective-permute-start(f32[1,8,512]{2,1,0:T(8,128)S(1)} %slice_select_fusion.6), channel_id=1, source_target_pairs={{0,8},{8,0},{16,24},{24,16},{32,40},{40,32},{48,56},{56,48},{1,9},... | collective-permute-start | bytes 49160 | tf_op jit(solution)/shard_map/rel_terms/ppermute | solution.py:19
  (4 other events, 3.6 us)

commit v2 on v1

v2 whole, which is shorter than its diff:
```python
import jax
import jax.numpy as jnp
from jax import lax
from jax.experimental import pallas as pl
from jax.experimental.pallas import tpu as pltpu
from jax.sharding import Mesh, PartitionSpec as P

CLS_DEV = 2048
CAP = 16
CAP_N = 2
SIZES = {"y": 4, "z": 8, "x": 4, "c": 2}
SHARD = ("z", "x", "c")
ALL = ("y",) + SHARD
BF = jnp.bfloat16
F32 = jnp.float32


def swap(a, axis, flip):
    return lax.ppermute(a, axis, [(i, i ^ flip) for i in range(SIZES[axis])])


def pair_send(blocks):
    me = lax.axis_index("y")
    inner = (me == 1) | (me == 2)
    outer_set = jnp.stack([blocks[0], blocks[3]])
    inner_set = jnp.stack([blocks[1], blocks[2]])
    return jnp.where(inner, outer_set, inner_set).astype(BF), jnp.where(inner, inner_set, outer_set)


def pair_keep(arrived, keep):
    keep = keep + arrived.astype(F32)
    low = lax.axis_index("y") < 2
    send = jnp.where(low, keep[1], keep[0]).astype(BF)
    return jnp.where(low, keep[0], keep[1]) + swap(send, "y", 3).astype(F32)


def column_sum(own, dtype):
    me = lax.axis_index("x")
    block = lambda flip: lax.dynamic_index_in_dim(own, me ^ flip, 1, keepdims=False)
    moved = [swap(block(flip).astype(dtype), "x", flip).astype(F32) for flip in (1, 3, 2)]
    return block(0) + moved[0] + moved[1] + moved[2]


def slots_of(owners, cap):
    n = owners.shape[0]
    column = owners
    row = owners.reshape(1, n)
    before = lax.broadcasted_iota(jnp.int32, (n, n), 0) < lax.broadcasted_iota(jnp.int32, (n, n), 1)
    rank = jnp.sum(jnp.where((column == row) & before, 1, 0), axis=0, keepdims=True)
    return row * cap + rank


def onehot_of(slots, count):
    return lax.broadcasted_iota(jnp.int32, (count, slots.shape[1]), 0) == slots


def pick(hot, values):
    return jnp.sum(jnp.where(hot, values.reshape(1, -1), 0), axis=1)


def heads_kernel(dquery_ref, rel_ref, relations_ref, slots_ref, out_ref):
    owners = out_ref.shape[0]
    dquery = dquery_ref[...]
    dhead = jnp.zeros(dquery.shape, F32)
    for r in range(relations_ref.shape[0]):
        masked = jnp.where(rel_ref[...] == r, dquery.astype(F32), 0.0).astype(BF)
        dhead += lax.dot_general(masked, relations_ref[r], (((1,), (1,)), ((), ())), preferred_element_type=F32)
    hot = onehot_of(slots_ref[...], owners * CAP)
    rows = jnp.dot(jnp.where(hot, 1.0, 0.0).astype(BF), dhead.astype(BF), preferred_element_type=F32).astype(BF)
    for block in range(4):
        out_ref[:, block * CAP:(block + 1) * CAP, :] = rows[:, block * 128:(block + 1) * 128].reshape(owners, CAP, 128)


def pack_heads(dquery, rel_id, relations, slots, owners):
    return pl.pallas_call(
        heads_kernel,
        out_shape=jax.ShapeDtypeStruct((owners, 4 * CAP, 128), BF),
        compiler_params=pltpu.CompilerParams(vmem_limit_bytes=32 * 2**20),
        name="pack_heads",
    )(dquery, rel_id, relations, slots)


def finish_kernel(terms_ref, slots_ref, heads_ref, line_ref, out_ref):
    owners = out_ref.shape[0]
    grad = jnp.sum(terms_ref[...].astype(F32), axis=0).astype(BF)
    count = grad.shape[0]
    entry = lax.broadcasted_iota(jnp.int32, (owners * 8, count), 0)
    filled = (entry // 8) * CAP_N + entry % CAP_N == slots_ref[...]
    column = (entry % 8) // CAP_N
    rows = jnp.zeros((owners * 8, 128), F32)
    for block in range(4):
        hot = jnp.where(filled & (column == block), 1.0, 0.0).astype(BF)
        rows += jnp.dot(hot, grad[:, block * 128:(block + 1) * 128], preferred_element_type=F32)
    out_ref[:, :64, :] = heads_ref[...]
    small = jnp.concatenate([rows.reshape(owners, 8, 128), line_ref[...].astype(F32)], axis=1)
    out_ref[:, 64:, :] = small.astype(BF)


def finish(terms, slots, heads, line):
    args = (terms, slots, heads, line)
    return pl.pallas_call(
        finish_kernel,
        out_shape=jax.ShapeDtypeStruct((heads.shape[0], 80, 128), BF),
        compiler_params=pltpu.CompilerParams(vmem_limit_bytes=32 * 2**20),
        name="finish",
    )(*args)


FIELDS = dict(tail_hi=0, head_hi=16, neg_hi=32, tail_lo=34, head_lo=50, neg_lo=66, gpos_hi=68, gpos_lo=84)


def combine_kernel(tail_ref, got_ref, out_ref, head_rows, tail_ids, head_ids, neg_ids, gpos):
    owners = got_ref.shape[0]
    rows = out_ref.shape[0]

    @pl.when(pl.program_id(0) == 0)
    def _():
        for block in range(4):
            head_rows[:, block * 128:(block + 1) * 128] = got_ref[:, block * CAP:(block + 1) * CAP, :].reshape(-1, 128)
        line = got_ref[:, 72:80, :].astype(F32)[:, 0, :].astype(BF)

        def spread(high, low, scale, per, cap):
            total = owners * per
            field = lax.broadcasted_iota(jnp.int32, (128, total), 0)
            place = lax.broadcasted_iota(jnp.int32, (128, total), 1) % cap
            take = jnp.where(field == FIELDS[high] + place, scale, 0.0) + jnp.where(field == FIELDS[low] + place, 1.0, 0.0)
            every = jnp.dot(line, take.astype(BF), preferred_element_type=F32)
            mine = lax.broadcasted_iota(jnp.int32, (owners, total), 1) // per
            mine = mine == lax.broadcasted_iota(jnp.int32, (owners, total), 0)
            return jnp.sum(jnp.where(mine, every, 0.0), axis=0, keepdims=True)

        tail_ids[...] = spread("tail_hi", "tail_lo", 128.0, CAP, CAP).astype(jnp.int32) - 1
        head_ids[...] = spread("head_hi", "head_lo", 128.0, CAP, CAP).astype(jnp.int32) - 1
        gpos[...] = spread("gpos_hi", "gpos_lo", 1.0, CAP, CAP)
        ids = spread("neg_hi", "neg_lo", 128.0, 8, CAP_N).astype(jnp.int32) - 1
        column = (lax.broadcasted_iota(jnp.int32, (4, owners * 8), 1) % 8) // CAP_N
        neg_ids[...] = jnp.where(column == lax.broadcasted_iota(jnp.int32, (4, owners * 8), 0), ids, -1)

    first = pl.program_id(0) * rows

    def hot(labels, weights):
        ids = lax.broadcasted_iota(jnp.int32, (rows, labels.shape[1]), 0) + first
        return jnp.where(ids == labels, weights, 0.0).astype(BF)

    negs = got_ref[:, 64:72, :].reshape(owners * 8, 128)
    total = jnp.dot(hot(tail_ids[...], gpos[...]), tail_ref[...], preferred_element_type=F32)
    total += jnp.dot(hot(head_ids[...], 1.0), head_rows[...], preferred_element_type=F32)
    parts = [jnp.dot(hot(neg_ids[block:block + 1, :], 1.0), negs, preferred_element_type=F32) for block in range(4)]
    out_ref[...] = total + jnp.concatenate(parts, axis=1)


def combine(tails, got):
    tile = 256
    width = tails.shape[1]
    return pl.pallas_call(
        combine_kernel,
        grid=(CLS_DEV // tile,),
        in_specs=[pl.BlockSpec(tails.shape, lambda i: (0, 0)), pl.BlockSpec(got.shape, lambda i: (0, 0, 0))],
        out_specs=pl.BlockSpec((tile, width), lambda i: (i, 0)),
        out_shape=jax.ShapeDtypeStruct((CLS_DEV, width), F32),
        scratch_shapes=[
            pltpu.VMEM(tails.shape, BF),
            pltpu.VMEM((1, tails.shape[0]), jnp.int32),
            pltpu.VMEM((1, tails.shape[0]), jnp.int32),
            pltpu.VMEM((4, got.shape[0] * 8), jnp.int32),
            pltpu.VMEM((1, tails.shape[0]), F32),
        ],
        compiler_params=pltpu.CompilerParams(vmem_limit_bytes=40 * 2**20),
        name="combine",
    )(tails, got)


def on_device(
    head_vecs, tail_vecs, rel_id, head_owner, head_row, tail_owner, tail_row,
    neg_vecs, neg_owner, neg_row, counts, relations,
):
    n, width = head_vecs.shape
    rels = relations.shape[0]
    owners = SIZES["z"] * SIZES["x"] * SIZES["c"]
    core = lax.axis_index("c")

    with jax.named_scope("gather_negatives"):
        wide = jnp.broadcast_to(neg_vecs[None], (SIZES["z"],) + neg_vecs.shape)
        column = lax.all_to_all(wide, "z", 0, 0, tiled=True).reshape(-1, width)
        near = jnp.concatenate([column] + [swap(column, "x", flip) for flip in (1, 3, 2)], axis=0)

    with jax.named_scope("query"):
        of_rel = [(rel_id == r)[:, None] for r in range(rels)]
        spread = lambda v: jnp.concatenate([jnp.where(m, v, jnp.zeros_like(v)) for m in of_rel], axis=1)
        query = jnp.dot(spread(head_vecs), relations.reshape(rels * width, width), preferred_element_type=F32).astype(BF)
    with jax.named_scope("pack_tails"):
        tail_hot = onehot_of(slots_of(tail_owner, CAP), owners * CAP)
        tail_rows = jnp.dot(tail_hot.astype(BF), query, preferred_element_type=F32).astype(BF)
        near, tail_rows = lax.optimization_barrier((near, tail_rows))
        got_tails = lax.all_to_all(tail_rows.reshape(owners, CAP, width), SHARD, 0, 0, tiled=True)
        negatives = jnp.concatenate([near, swap(near, "c", 1)], axis=0)
    with jax.named_scope("rel_heads"):
        feature = lax.broadcasted_iota(jnp.int32, (width, width // 2), 0)
        place = lax.broadcasted_iota(jnp.int32, (width, width // 2), 1)
        wanted = (feature == place // 8 * 16 + core * 8 + place % 8).astype(BF)
        both = jnp.concatenate([head_vecs, swap(head_vecs, "c", 1)], axis=0)
        both = jnp.dot(both, wanted, preferred_element_type=F32).astype(BF)
        both_rel = jnp.concatenate([rel_id, swap(rel_id, "c", 1)])
        both = jnp.concatenate(
            [jnp.where((both_rel == r)[:, None], both, jnp.zeros_like(both)) for r in range(rels)], axis=1
        )

    with jax.named_scope("weights"):
        live = jnp.arange(n, dtype=jnp.int32) < counts[0, 0]
        positive = jnp.sum(query.astype(F32) * tail_vecs.astype(F32), axis=1)
        scores = lax.dot_general(query, negatives, (((1,), (1,)), ((), ())), preferred_element_type=F32)
        top = jnp.maximum(positive, jnp.max(scores, axis=1))
        pos_exp = jnp.exp(positive - top)
        neg_exp = jnp.exp(scores - top[:, None])
        total = pos_exp + jnp.sum(neg_exp, axis=1)
        gpos = jnp.where(live, pos_exp / total - 1.0, 0.0)
        gneg = jnp.where(live[:, None], neg_exp / total[:, None], 0.0).astype(BF)
    with jax.named_scope("dquery"):
        dquery = (
            gpos[:, None] * tail_vecs.astype(F32) + jnp.dot(gneg, negatives, preferred_element_type=F32)
        ).astype(BF)
    with jax.named_scope("neg_terms"):
        neg_terms = lax.dot_general(gneg, query, (((0,), (0,)), ((), ())), preferred_element_type=F32)
        half = neg_terms.shape[0] // 2
        own = neg_terms[:half] + swap(neg_terms[half:].astype(BF), "c", 1).astype(F32)
        dquery, own = lax.optimization_barrier((dquery, own))
        own = own.reshape(4, 8, -1, width)
        moved = [swap(own[at].astype(BF), "x", flip).astype(F32) for at, flip in ((1, 1), (2, 3), (3, 2))]
        own = (own[0] + moved[0] + moved[1] + moved[2]).astype(BF)
    with jax.named_scope("pack_heads"):
        head_slots = slots_of(head_owner, CAP)
        head_hot = onehot_of(head_slots, owners * CAP)
        head_rows = pack_heads(dquery, rel_id.reshape(n, 1), relations, head_slots, owners)
    with jax.named_scope("rel_terms"):
        both_dquery = jnp.concatenate([dquery, swap(dquery, "c", 1)], axis=0)
        mine = lax.dot_general(both, both_dquery, (((0,), (0,)), ((), ())), preferred_element_type=F32)
        mine, keep = pair_send(mine.reshape(rels, -1, width))
        mine = swap(mine, "y", 1)
    with jax.named_scope("line"):
        neg_slots = slots_of(neg_owner, CAP_N)
        neg_hot = onehot_of(neg_slots, owners * CAP_N)
        ids = [
            pick(hot, rows + 1).reshape(owners, -1)
            for hot, rows in ((tail_hot, tail_row), (head_hot, head_row), (neg_hot, neg_row))
        ]
        gp = pick(tail_hot, gpos).reshape(owners, CAP)
        gp_top = gp.astype(BF)
        fields = [(i >> 7).astype(BF) for i in ids] + [(i & 127).astype(BF) for i in ids]
        fields += [gp_top, (gp - gp_top.astype(F32)).astype(BF)]
        line = jnp.concatenate(fields, axis=1)
        line = jnp.pad(line, ((0, 0), (0, 1024 - line.shape[1]))).reshape(owners, 8, 128)
    own, got_tails, mine = lax.optimization_barrier((own, got_tails, mine))
    with jax.named_scope("neg_exchange"):
        got_negs = lax.all_to_all(own, "z", 0, 0, tiled=True)
    with jax.named_scope("send_heads"):
        got = lax.all_to_all(finish(got_negs, neg_slots, head_rows, line), SHARD, 0, 0, tiled=True)
    with jax.named_scope("rel_sum"):
        mine = pair_keep(mine, keep)
        mine = column_sum(mine.reshape(8, 4, 8, width), F32)
        mine, got = lax.optimization_barrier((mine, got))
        relation_grad = jnp.sum(lax.all_to_all(mine, "z", 0, 0, tiled=True), axis=0)
    with jax.named_scope("combine"):
        owned = combine(got_tails.reshape(-1, width), got)
    return owned[None], relation_grad


def solution(mesh):
    fine = Mesh(mesh.devices.reshape(*SIZES.values()), tuple(SIZES))
    whole = P(ALL)
    wide = P(ALL, None)
    return jax.shard_map(
        on_device,
        mesh=fine,
        in_specs=(
            wide, wide, whole, wide, whole, wide, whole, wide, wide, whole, P("y", SHARD), P(),
        ),
        out_specs=(P("y", SHARD, None), wide),
        check_vma=False,
    )
```

time: 184 us -> 148 us (0.80)
  waiting for transfers between devices: 61.6 us -> 42.9 us
  starting transfers between devices: 62.4 us -> 51.2 us
  matrix products: 15.8 us -> 9.61 us
  Pallas kernels: 8.29 us -> 12.6 us
  local copies, waits for them, and re-layouts: 12.3 us -> 9.64 us
  other arithmetic: 21 us -> 18.5 us
    ppermute x15 -> x16, waiting for transfers between devices: 50.6 us -> 31.5 us  [swap(): return lax.ppermute(a, axis, [(i, i ^ flip) for i in range(SIZES[axis])])]
    ppermute x15 -> x16, starting transfers between devices: 29.5 us -> 19.8 us  [swap(): return lax.ppermute(a, axis, [(i, i ^ flip) for i in range(SIZES[axis])])]
    all_to_all x3 -> x4, starting transfers between devices: 26.9 us -> 21.1 us  [the longest x1 8.47 us: on_device(): column = lax.all_to_all(wide, 'z', 0, 0, tiled=True).reshape(-1, width)]
    all_to_all x1, starting transfers between devices: 5.97 us -> 10.3 us  [on_device(): lax.all_to_all(tail_rows.reshape(owners, CAP, width), SHARD, 0, 0, tiled=...]
    pallas_call x1 -> x3, Pallas kernels: 8.29 us -> 12.6 us  [the longest x1 9.26 us: combine(): pl.pallas_call(combine_kernel, grid=(CLS_DEV // tile,), in_specs=[pl.Bloc...]
    dot_general x3 -> x2, matrix products: 6.09 us -> 2.81 us  [the longest x1 1.56 us: on_device(): both = jnp.dot(both, wanted, preferred_element_type=F32).astype(BF)]
    reduce_sum x3, other arithmetic: 0.49 us -> 2.73 us  [slots_of(): jnp.sum(jnp.where((column == row) & before, 1, 0), axis=0, keepdims=True)]
    concatenate x2 -> x1, other arithmetic: 2.2 us -> 0.03 us  [on_device(): jnp.concatenate([column] + [swap(column, 'x', flip) for flip in (1, 3, 2)...]
  transfers between devices with their start and end apart: 19 -> 21, of which waited for: 11 -> 12; matrix products, arithmetic and copies ran while one was open for 23% -> 21% of each run, Pallas kernels for 5% -> 8%
where the time goes in v2:
time: 148 us; the launch traced here: 146 us
  starting transfers between devices  51.2 us (35%)
  waiting for transfers between devices  42.9 us (29%)
  other arithmetic  18.5 us (12%)
  Pallas kernels  12.6 us (9%)
  local copies, waits for them, and re-layouts  9.64 us (7%)
  matrix products  9.61 us (6%)
  between operations  1.85 us (1%)
    ppermute x16, waiting for transfers between devices, swap(): return lax.ppermute(a, axis, [(i, i ^ flip) for i in range(SIZES[axis])])  31.5 us
    ppermute x16, starting transfers between devices, swap(): return lax.ppermute(a, axis, [(i, i ^ flip) for i in range(SIZES[axis])])  19.8 us
    all_to_all x1, starting transfers between devices, on_device(): lax.all_to_all(tail_rows.reshape(owners, CAP, width), SHARD, 0, 0, tiled=...  10.3 us
    pallas_call x1, Pallas kernels, combine(): pl.pallas_call(combine_kernel, grid=(CLS_DEV // tile,), in_specs=[pl.Bloc...  9.26 us
    all_to_all x1, starting transfers between devices, on_device(): column = lax.all_to_all(wide, 'z', 0, 0, tiled=True).reshape(-1, width)  8.47 us
    all_to_all x1, waiting for transfers between devices, on_device(): got_negs = lax.all_to_all(own, 'z', 0, 0, tiled=True)  5.63 us
    unnamed x52, local copies, waits for them, and re-layouts  5.17 us
    all_to_all x1, starting transfers between devices, on_device(): got_negs = lax.all_to_all(own, 'z', 0, 0, tiled=True)  4.67 us
  transfers between devices with their start and end apart: 21, of which 12 were waited for; matrix products, arithmetic and copies ran while one was open for 21% of the time, Pallas kernels for 8%

profile of v2, /device:TPU:2, one launch (start us, length us, event | category | flops | bytes accessed | tf_op | source)
XLA Modules:
  0.0 146.3 jit_solution(5780278641021936218)
XLA Ops:
  0.6 1.5 %broadcast_in_dim.150 = bf16[8,16,512]{2,1,0:T(8,128)(2,1)} broadcast(bf16[16,512]{1,0:T(8,128)(2,1)} %param.19), dimensions={1,2} | broadcast | bytes 147456 | tf_op jit(solution)/shard_map/gather_negatives/broadcast_in_dim | solution.py:183
  2.2 8.5 %all-to-all-start = ((bf16[8,16,512]{2,1,0:T(8,128)(2,1)}), bf16[8,16,512]{2,1,0:T(8,128)(2,1)S(1)}, u32[]{:S(2)}, u32[]{:S(2)}) async-start(bf16[8,16,512]{2,1,0:T(8,128)(2,1)} %broadcast_in_dim.150), calls=%async_computation | async-start | bytes 262144 | tf_op jit(solution)/shard_map/gather_negatives/all_to_all | solution.py:184
  11.9 1.0 select_reduce_fusion.4
  13.6 0.8 select_reduce_fusion.6
  14.4 1.0 select_reduce_fusion.3
  16.0 1.5 %broadcast_select_fusion.3 = (bf16[512,512]{1,0:T(8,128)(2,1)S(1)}, bf16[512,512]{1,0:T(8,128)(2,1)S(1)}, bf16[512,512]{1,0:T(8,128)(2,1)S(1)}, bf16[512,512]{1,0:T(8,128)(2,1)S(1)}) fusion(bf16[512,512]{1,0:T(8,128)(2,1)} %param.12, pred[512]{0:T(512)(128)(4,1)S(1)} %get-tuple-element.50, pred[512]{0:T(512)(128)(4,1)S(1)} %get-tuple-element.51, ...), kind=kLoop, calls=%fused_computation.62 | loop fusion | flops 1048576 | bytes 2623488 | tf_op jit(solution)/shard_map/query/jit(_where)/select_n | solution.py:189
  17.5 1.3 fusion.23
  18.9 1.7 %fusion.18 = bf16[1024,512]{1,0:T(8,128)(2,1)} fusion(bf16[512,512]{1,0:T(8,128)(2,1)S(1)} %get-tuple-element.57, s32[512]{0:T(512)S(1)} %multiply_add_fusion.1), kind=kOutput, calls=%fused_computation.25 | convolution fusion | flops 537919488 | bytes 1574912 | tf_op jit(solution)/shard_map/pack_tails/dot_general | solution.py:193
  22.0 2.2 %collective-permute-start.2 = (bf16[128,512]{1,0:T(8,128)(2,1)S(1)}, bf16[128,512]{1,0:T(8,128)(2,1)S(1)}, u32[]{:S(2)}, u32[]{:S(2)}) collective-permute-start(bf16[128,512]{1,0:T(8,128)(2,1)S(1)} %bitcast.68), channel_id=1, source_target_pairs={{0,4},{2,6},{4,0},{6,2},{1,5},{3,7},{5,1},{7,3},{8,12},{10,14},{12... | collective-permute-start | bytes 393224 | tf_op jit(solution)/shard_map/gather_negatives/ppermute | solution.py:19
  24.2 2.6 %collective-permute-start = (bf16[128,512]{1,0:T(8,128)(2,1)S(1)}, bf16[128,512]{1,0:T(8,128)(2,1)S(1)}, u32[]{:S(2)}, u32[]{:S(2)}) collective-permute-start(bf16[128,512]{1,0:T(8,128)(2,1)S(1)} %bitcast.70), channel_id=1, source_target_pairs={{0,2},{2,0},{4,6},{6,4},{1,3},{3,1},{5,7},{7,5},{8,10},{10,8},{12,... | collective-permute-start | bytes 393224 | tf_op jit(solution)/shard_map/gather_negatives/ppermute | solution.py:19
  28.8 1.1 collective-permute-done.2
  29.9 1.9 %collective-permute-done.1 = bf16[128,512]{1,0:T(8,128)(2,1)S(1)} collective-permute-done((bf16[128,512]{1,0:T(8,128)(2,1)S(1)}, bf16[128,512]{1,0:T(8,128)(2,1)S(1)}, u32[]{:S(2)}, u32[]{:S(2)}) %collective-permute-start.1) | collective-permute-done | bytes 131104 | tf_op jit(solution)/shard_map/gather_negatives/ppermute | solution.py:19
  32.2 1.8 %collective-permute-done.3 = bf16[512,512]{1,0:T(8,128)(2,1)S(1)} collective-permute-done((bf16[512,512]{1,0:T(8,128)(2,1)S(1)}, bf16[512,512]{1,0:T(8,128)(2,1)S(1)}, u32[]{:S(2)}, u32[]{:S(2)}) %collective-permute-start.3) | collective-permute-done | bytes 524320 | tf_op jit(solution)/shard_map/pack_tails/ppermute | solution.py:19
  34.0 0.9 copy-done.8
  35.0 0.8 fusion.53
  37.7 0.9 slice.99
  39.3 10.3 %all-to-all-start.1 = ((bf16[64,16,512]{2,1,0:T(8,128)(2,1)}), bf16[64,16,512]{2,1,0:T(8,128)(2,1)S(1)}, u32[]{:S(2)}, u32[]{:S(2)}) async-start(bf16[64,16,512]{2,1,0:T(8,128)(2,1)} %bitcast.67), calls=%async_computation.1 | async-start | bytes 2097152 | tf_op jit(solution)/shard_map/pack_tails/all_to_all | solution.py:195
  49.7 2.2 %fusion.19.dquery_ref = bf16[512,512]{1,0:T(8,128)(2,1)S(1)} fusion(bf16[512,1024]{1,0:T(8,128)(2,1)S(1)} %select_convert_fusion, bf16[1024,512]{1,0:T(8,128)(2,1)} %copy-done.8, bf16[512,512]{1,0:T(8,128)(2,1)} %param.13, f32[512]{0:T(512)S(1)} %get-tuple-element.40), kind=kOutput, calls=%fused_computation.29 | convolution fusion | flops 537919488 | bytes 3147776 | tf_op jit(solution)/shard_map/dquery/dot_general | solution.py:220
  53.0 1.6 %broadcast_select_fusion.7 = (bf16[1024,256]{0,1:T(8,128)(2,1)S(1)}, bf16[1024,256]{0,1:T(8,128)(2,1)S(1)}, bf16[1024,256]{0,1:T(8,128)(2,1)S(1)}, bf16[1024,256]{0,1:T(8,128)(2,1)S(1)}) fusion(pred[1024]{0:T(1024)(128)(4,1)S(1)} %get-tuple-element.46, pred[1024]{0:T(1024)(128)(4,1)S(1)} %get-tuple-element.47, pred[1024]{0:T(1024)(128)(4,1)S(1)} %get-tuple-element.48, ...), kind=kOutput, calls=%fused_computation.66 | convolution fusion | flops 272629760 | bytes 3154436 | tf_op jit(solution)/shard_map/rel_heads/dot_general | solution.py:202
  54.6 1.2 fusion.8
  56.9 0.9 select_convert_fusion.1
  57.8 1.6 %collective-permute-start.11 = (bf16[2,256,512]{2,1,0:T(8,128)(2,1)}, bf16[2,256,512]{2,1,0:T(8,128)(2,1)S(1)}, u32[]{:S(2)}, u32[]{:S(2)}) collective-permute-start(bf16[2,256,512]{2,1,0:T(8,128)(2,1)} %select_convert_fusion.1), channel_id=1, source_target_pairs={{0,64},{64,0},{128,192},{192,128},{1,65},{65,1},{129,193},{193,129... | collective-permute-start | bytes 1572872 | tf_op jit(solution)/shard_map/rel_terms/ppermute | solution.py:19
  59.4 0.8 fusion.52
  60.2 2.1 %collective-permute-start.7 = (bf16[8,16,512]{2,1,0:T(8,128)(2,1)}, bf16[8,16,512]{2,1,0:T(8,128)(2,1)}, u32[]{:S(2)}, u32[]{:S(2)}) collective-permute-start(bf16[8,16,512]{2,1,0:T(8,128)(2,1)} %bitcast.7), channel_id=1, source_target_pairs={{0,4},{2,6},{4,0},{6,2},{1,5},{3,7},{5,1},{7,3},{8,12},{10,14},{12... | collective-permute-start | bytes 393224 | tf_op jit(solution)/shard_map/neg_terms/ppermute | solution.py:19
  62.2 2.6 %collective-permute-start.5 = (bf16[8,16,512]{2,1,0:T(8,128)(2,1)}, bf16[8,16,512]{2,1,0:T(8,128)(2,1)}, u32[]{:S(2)}, u32[]{:S(2)}) collective-permute-start(bf16[8,16,512]{2,1,0:T(8,128)(2,1)} %bitcast.5), channel_id=1, source_target_pairs={{0,2},{2,0},{4,6},{6,4},{1,3},{3,1},{5,7},{7,5},{8,10},{10,8},{12,... | collective-permute-start | bytes 393224 | tf_op jit(solution)/shard_map/neg_terms/ppermute | solution.py:19
  65.3 6.2 %collective-permute-done.7 = bf16[8,16,512]{2,1,0:T(8,128)(2,1)} collective-permute-done((bf16[8,16,512]{2,1,0:T(8,128)(2,1)}, bf16[8,16,512]{2,1,0:T(8,128)(2,1)}, u32[]{:S(2)}, u32[]{:S(2)}) %collective-permute-start.7) | collective-permute-done | bytes 131104 | tf_op jit(solution)/shard_map/neg_terms/ppermute | solution.py:19
  71.4 3.6 %collective-permute-done.6 = bf16[8,16,512]{2,1,0:T(8,128)(2,1)} collective-permute-done((bf16[8,16,512]{2,1,0:T(8,128)(2,1)}, bf16[8,16,512]{2,1,0:T(8,128)(2,1)}, u32[]{:S(2)}, u32[]{:S(2)}) %collective-permute-start.6) | collective-permute-done | bytes 131104 | tf_op jit(solution)/shard_map/neg_terms/ppermute | solution.py:19
  75.1 1.8 %add_convert_fusion = bf16[8,16,512]{2,1,0:T(8,128)(2,1)} fusion(bf16[8,16,512]{2,1,0:T(8,128)(2,1)} %collective-permute-done.7, bf16[8,16,512]{2,1,0:T(8,128)(2,1)} %collective-permute-done.6, f32[8,16,512]{2,1,0:T(8,128)S(1)} %bitcast.66, bf16[8,16,512]{2,1,0:T(8,128)(2,1)} %collective-permute-done.5), kind=kLoop, calls=%fused_computation.74 | loop fusion | flops 458752 | bytes 786432 | tf_op jit(solution)/shard_map/neg_terms/convert_element_type | solution.py:229
  76.8 1.7 %all-to-all-done.1 = bf16[64,16,512]{2,1,0:T(8,128)(2,1)S(1)} async-done(((bf16[64,16,512]{2,1,0:T(8,128)(2,1)}), bf16[64,16,512]{2,1,0:T(8,128)(2,1)S(1)}, u32[]{:S(2)}, u32[]{:S(2)}) %all-to-all-start.1) | async-done | bytes 1048608 | tf_op jit(solution)/shard_map/pack_tails/all_to_all | solution.py:195
  78.5 4.7 %all-to-all-start.2 = ((bf16[8,16,512]{2,1,0:T(8,128)(2,1)}), bf16[8,16,512]{2,1,0:T(8,128)(2,1)S(1)}, u32[]{:S(2)}, u32[]{:S(2)}) async-start(bf16[8,16,512]{2,1,0:T(8,128)(2,1)} %add_convert_fusion), calls=%async_computation.2 | async-start | bytes 262144 | tf_op jit(solution)/shard_map/neg_exchange/all_to_all | solution.py:254
  83.4 1.6 %copy-done.1 = bf16[4,512,512]{2,1,0:T(8,128)(2,1)S(1)} copy-done((bf16[4,512,512]{2,1,0:T(8,128)(2,1)S(1)}, bf16[4,512,512]{2,1,0:T(8,128)(2,1)}, u32[]{:S(2)}) %copy-start.1) | copy-done | bytes 2097176
  85.0 1.9 %pack_heads.1.heads_ref = bf16[64,64,128]{2,1,0:T(8,128)(2,1)S(1)} custom-call(bf16[512,512]{1,0:T(8,128)(2,1)S(1)} %fusion.19.dquery_ref, s32[512,1]{1,0:T(8,128)S(1)} %copy.18.rel_ref, bf16[4,512,512]{2,1,0:T(8,128)(2,1)S(1)} %copy-done.1, s32[1,512]{1,0:T(1,128)S(1)} %bitcast_add_fusion.2.slots_ref), custom_call_target="tpu_custom_call" | custom-call | tf_op jit(solution)/shard_map/pack_heads/pack_heads/pallas_call | solution.py:75
  86.9 5.6 %all-to-all-done.2.terms_ref = bf16[8,16,512]{2,1,0:T(8,128)(2,1)S(1)} async-done(((bf16[8,16,512]{2,1,0:T(8,128)(2,1)}), bf16[8,16,512]{2,1,0:T(8,128)(2,1)S(1)}, u32[]{:S(2)}, u32[]{:S(2)}) %all-to-all-start.2) | async-done | bytes 131104 | tf_op jit(solution)/shard_map/neg_exchange/all_to_all | solution.py:254
  92.5 1.5 finish.1
  94.0 4.6 %all-to-all-start.3 = ((bf16[64,80,128]{2,1,0:T(8,128)(2,1)}), bf16[64,80,128]{2,1,0:T(8,128)(2,1)S(1)}, u32[]{:S(2)}, u32[]{:S(2)}) async-start(bf16[64,80,128]{2,1,0:T(8,128)(2,1)} %finish.1), calls=%async_computation.3 | async-start | bytes 2621440 | tf_op jit(solution)/shard_map/send_heads/all_to_all | solution.py:256
  98.5 1.9 %convert_add_fusion = f32[2,256,512]{2,1,0:T(8,128)S(1)} fusion(bf16[2,256,512]{2,1,0:T(8,128)(2,1)} %copy-done.11, f32[1,256,512]{2,1,0:T(8,128)} %copy-done.5, f32[1,256,512]{2,1,0:T(8,128)} %copy-done.6, f32[1,256,512]{2,1,0:T(8,128)} %copy-done.7, f32[1,256,512]{2,1,0:T(8,128)} %copy-done.4, pred[]{:T(512)S(6)} %or.3), kind=kLoop, calls=%fused_computation.44 | loop fusion | flops 1310720 | bytes 3670017 | tf_op jit(solution)/shard_map/rel_sum/add | solution.py:31
  101.2 2.7 %collective-permute-start.12 = (bf16[256,512]{1,0:T(8,128)(2,1)}, bf16[256,512]{1,0:T(8,128)(2,1)}, u32[]{:S(2)}, u32[]{:S(2)}) collective-permute-start(bf16[256,512]{1,0:T(8,128)(2,1)} %fusion.33), channel_id=1, source_target_pairs={{0,192},{64,128},{128,64},{192,0},{1,193},{65,129},{129,65},{193,1... | collective-permute-start | bytes 786440 | tf_op jit(solution)/shard_map/rel_sum/ppermute | solution.py:19
  104.0 7.2 %collective-permute-done.12 = bf16[256,512]{1,0:T(8,128)(2,1)} collective-permute-done((bf16[256,512]{1,0:T(8,128)(2,1)}, bf16[256,512]{1,0:T(8,128)(2,1)}, u32[]{:S(2)}, u32[]{:S(2)}) %collective-permute-start.12) | collective-permute-done | bytes 262176 | tf_op jit(solution)/shard_map/rel_sum/ppermute | solution.py:19
  111.1 1.1 bitcast_add_fusion
  112.2 0.8 copy-done.9
  113.0 2.2 %collective-permute-start.15 = (f32[8,8,512]{2,1,0:T(8,128)S(1)}, f32[8,8,512]{2,1,0:T(8,128)S(1)}, u32[]{:S(2)}, u32[]{:S(2)}) collective-permute-start(f32[8,8,512]{2,1,0:T(8,128)S(1)} %get-tuple-element.27), channel_id=1, source_target_pairs={{0,4},{2,6},{4,0},{6,2},{1,5},{3,7},{5,1},{7,3},{8,12},{10,14},{12... | collective-permute-start | bytes 393224 | tf_op jit(solution)/shard_map/rel_sum/ppermute | solution.py:19
  115.2 2.6 %collective-permute-start.13 = (f32[8,8,512]{2,1,0:T(8,128)S(1)}, f32[8,8,512]{2,1,0:T(8,128)S(1)}, u32[]{:S(2)}, u32[]{:S(2)}) collective-permute-start(f32[8,8,512]{2,1,0:T(8,128)S(1)} %get-tuple-element.26), channel_id=1, source_target_pairs={{0,2},{2,0},{4,6},{6,4},{1,3},{3,1},{5,7},{7,5},{8,10},{10,8},{12,... | collective-permute-start | bytes 393224 | tf_op jit(solution)/shard_map/rel_sum/ppermute | solution.py:19
  117.8 5.6 %collective-permute-done.15 = f32[8,8,512]{2,1,0:T(8,128)S(1)} collective-permute-done((f32[8,8,512]{2,1,0:T(8,128)S(1)}, f32[8,8,512]{2,1,0:T(8,128)S(1)}, u32[]{:S(2)}, u32[]{:S(2)}) %collective-permute-start.15) | collective-permute-done | bytes 131104 | tf_op jit(solution)/shard_map/rel_sum/ppermute | solution.py:19
  123.4 4.0 %collective-permute-done.14 = f32[8,8,512]{2,1,0:T(8,128)S(1)} collective-permute-done((f32[8,8,512]{2,1,0:T(8,128)S(1)}, f32[8,8,512]{2,1,0:T(8,128)S(1)}, u32[]{:S(2)}, u32[]{:S(2)}) %collective-permute-start.14) | collective-permute-done | bytes 131104 | tf_op jit(solution)/shard_map/rel_sum/ppermute | solution.py:19
  127.4 1.6 %fusion.43 = f32[8,8,512]{2,1,0:T(8,128)} fusion(f32[8,8,512]{2,1,0:T(8,128)S(1)} %collective-permute-done.15, f32[8,8,512]{2,1,0:T(8,128)S(1)} %collective-permute-done.14, f32[8,8,512]{2,1,0:T(8,128)S(1)} %collective-permute-done.13, f32[8,4,8,512]{3,2,1,0:T(8,128)} %bitcast.65, s32[]{:T(128)S(6)} %select_n.141), kind=kLoop, calls=%fused_computation.79 | loop fusion | flops 98304 | bytes 655364 | tf_op jit(solution)/shard_map/rel_sum/add | solution.py:41
  129.0 4.1 %all-to-all-done.3.got_ref = bf16[64,80,128]{2,1,0:T(8,128)(2,1)S(1)} async-done(((bf16[64,80,128]{2,1,0:T(8,128)(2,1)}), bf16[64,80,128]{2,1,0:T(8,128)(2,1)S(1)}, u32[]{:S(2)}, u32[]{:S(2)}) %all-to-all-start.3) | async-done | bytes 1310752 | tf_op jit(solution)/shard_map/send_heads/all_to_all | solution.py:256
  133.1 3.4 %all-to-all-start.4 = ((f32[8,8,512]{2,1,0:T(8,128)}), f32[8,8,512]{2,1,0:T(8,128)S(1)}, u32[]{:S(2)}, u32[]{:S(2)}) async-start(f32[8,8,512]{2,1,0:T(8,128)} %fusion.43), calls=%async_computation.4 | async-start | bytes 262144 | tf_op jit(solution)/shard_map/rel_sum/all_to_all | solution.py:261
  136.4 9.3 %combine.1 = f32[2048,512]{1,0:T(8,128)} custom-call(bf16[1024,512]{1,0:T(8,128)(2,1)S(1)} %bitcast.60, bf16[64,80,128]{2,1,0:T(8,128)(2,1)S(1)} %all-to-all-done.3.got_ref), custom_call_target="tpu_custom_call" | custom-call | tf_op jit(solution)/shard_map/combine/combine/pallas_call | solution.py:155
  (112 shorter events, 12.2 us)
Async XLA Ops:
  0.6 16.9 %copy-start = (bf16[4,512,512]{2,1,0:T(8,128)(2,1)S(1)}, bf16[4,512,512]{2,1,0:T(8,128)(2,1)}, u32[]{:S(2)}) copy-start(bf16[4,512,512]{2,1,0:T(8,128)(2,1)} %relations_ref.1) | copy-start | bytes 6291460
  2.2 19.8 %all-to-all-start = ((bf16[8,16,512]{2,1,0:T(8,128)(2,1)}), bf16[8,16,512]{2,1,0:T(8,128)(2,1)S(1)}, u32[]{:S(2)}, u32[]{:S(2)}) async-start(bf16[8,16,512]{2,1,0:T(8,128)(2,1)} %broadcast_in_dim.150), calls=%async_computation | async-start | bytes 262144 | tf_op jit(solution)/shard_map/gather_negatives/all_to_all | solution.py:184
  10.6 6.9 %copy-start.21 = (bf16[512,512]{1,0:T(8,128)(2,1)S(1)}, bf16[512,512]{1,0:T(8,128)(2,1)}, u32[]{:S(2)}) copy-start(bf16[512,512]{1,0:T(8,128)(2,1)} %param.13) | copy-start | bytes 1572868
  10.6 41.9 %collective-permute-start.8 = (s32[512]{0:T(512)}, s32[512]{0:T(512)S(1)}, u32[]{:S(2)}, u32[]{:S(2)}) collective-permute-start(s32[512]{0:T(512)} %param.14), channel_id=1, source_target_pairs={{0,1},{1,0},{2,3},{3,2},{4,5},{5,4},{6,7},{7,6},{8,9},{9,8},{10,11... | collective-permute-start | bytes 6152 | tf_op jit(solution)/shard_map/rel_heads/ppermute | solution.py:19
  10.7 41.9 %collective-permute-start.9 = (bf16[512,512]{1,0:T(8,128)(2,1)}, bf16[512,512]{1,0:T(8,128)(2,1)}, u32[]{:S(2)}, u32[]{:S(2)}) collective-permute-start(bf16[512,512]{1,0:T(8,128)(2,1)} %param.12), channel_id=1, source_target_pairs={{0,1},{1,0},{2,3},{3,2},{4,5},{5,4},{6,7},{7,6},{8,9},{9,8},{10,11... | collective-permute-start | bytes 1572872 | tf_op jit(solution)/shard_map/rel_heads/ppermute | solution.py:19
  14.4 6.5 %copy-start.19 = (s32[16]{0:T(128)}, s32[16]{0:T(128)S(1)}, u32[]{:S(2)}) copy-start(s32[16]{0:T(128)S(1)} %select_reduce_fusion.6) | copy-start | bytes 196
  18.9 2.1 %copy-start.17 = (s32[16]{0:T(128)S(1)}, s32[16]{0:T(128)}, u32[]{:S(2)}) copy-start(s32[16]{0:T(128)} %param.21) | copy-start | bytes 196
  18.9 2.1 %copy-start.18 = (s32[16,1]{0,1:T(1,128)S(1)}, s32[16,1]{0,1:T(1,128)}, u32[]{:S(2)}) copy-start(s32[16,1]{0,1:T(1,128)} %param.20) | copy-start | bytes 196
  18.9 2.2 %copy-start.12 = (s32[512,1]{0,1:T(1,128)S(1)}, s32[512,1]{0,1:T(1,128)}, u32[]{:S(2)}) copy-start(s32[512,1]{0,1:T(1,128)} %param.15) | copy-start | bytes 6148
  18.9 2.2 %copy-start.14 = (s32[512]{0:T(512)S(1)}, s32[512]{0:T(512)}, u32[]{:S(2)}) copy-start(s32[512]{0:T(512)} %param.16) | copy-start | bytes 6148
  18.9 9.0 %copy-start.13 = (s32[512]{0:T(512)S(1)}, s32[512]{0:T(512)}, u32[]{:S(2)}) copy-start(s32[512]{0:T(512)} %param.14) | copy-start | bytes 6148
  22.0 8.0 %collective-permute-start.2 = (bf16[128,512]{1,0:T(8,128)(2,1)S(1)}, bf16[128,512]{1,0:T(8,128)(2,1)S(1)}, u32[]{:S(2)}, u32[]{:S(2)}) collective-permute-start(bf16[128,512]{1,0:T(8,128)(2,1)S(1)} %bitcast.68), channel_id=1, source_target_pairs={{0,4},{2,6},{4,0},{6,2},{1,5},{3,7},{5,1},{7,3},{8,12},{10,14},{12... | collective-permute-start | bytes 393224 | tf_op jit(solution)/shard_map/gather_negatives/ppermute | solution.py:19
  24.2 7.7 %collective-permute-start.1 = (bf16[128,512]{1,0:T(8,128)(2,1)S(1)}, bf16[128,512]{1,0:T(8,128)(2,1)S(1)}, u32[]{:S(2)}, u32[]{:S(2)}) collective-permute-start(bf16[128,512]{1,0:T(8,128)(2,1)S(1)} %bitcast.69), channel_id=1, source_target_pairs={{0,6},{2,4},{4,2},{6,0},{1,7},{3,5},{5,3},{7,1},{8,14},{10,12},{12... | collective-permute-start | bytes 393224 | tf_op jit(solution)/shard_map/gather_negatives/ppermute | solution.py:19
  24.2 7.8 %collective-permute-start = (bf16[128,512]{1,0:T(8,128)(2,1)S(1)}, bf16[128,512]{1,0:T(8,128)(2,1)S(1)}, u32[]{:S(2)}, u32[]{:S(2)}) collective-permute-start(bf16[128,512]{1,0:T(8,128)(2,1)S(1)} %bitcast.70), channel_id=1, source_target_pairs={{0,2},{2,0},{4,6},{6,4},{1,3},{3,1},{5,7},{7,5},{8,10},{10,8},{12,... | collective-permute-start | bytes 393224 | tf_op jit(solution)/shard_map/gather_negatives/ppermute | solution.py:19
  32.0 2.0 %collective-permute-start.3 = (bf16[512,512]{1,0:T(8,128)(2,1)S(1)}, bf16[512,512]{1,0:T(8,128)(2,1)S(1)}, u32[]{:S(2)}, u32[]{:S(2)}) collective-permute-start(bf16[512,512]{1,0:T(8,128)(2,1)S(1)} %pad_maximum_fusion.2), channel_id=1, source_target_pairs={{0,1},{1,0},{2,3},{3,2},{4,5},{5,4},{6,7},{7,6},{8,9},{9,8},{10,11... | collective-permute-start | bytes 1572872 | tf_op jit(solution)/shard_map/pack_tails/ppermute | solution.py:19
  34.0 1.0 copy-start.8
  37.0 2.4 %copy-start.20 = (s32[16]{0:T(128)S(1)}, s32[16]{0:T(128)}, u32[]{:S(2)}) copy-start(s32[16]{0:T(128)} %copy-done.19) | copy-start | bytes 196
  37.7 1.5 %copy-start.2 = (f32[1024,512]{1,0:T(8,128)}, f32[1024,512]{1,0:T(8,128)S(1)}, u32[]{:S(2)}) copy-start(f32[1024,512]{1,0:T(8,128)S(1)} %fusion.54) | copy-start | bytes 6291460
  39.2 12.8 %collective-permute-start.4 = (bf16[512,512]{1,0:T(8,128)(2,1)}, bf16[512,512]{1,0:T(8,128)(2,1)S(1)}, u32[]{:S(2)}, u32[]{:S(2)}) collective-permute-start(bf16[512,512]{1,0:T(8,128)(2,1)} %slice.99), channel_id=1, source_target_pairs={{0,1},{1,0},{2,3},{3,2},{4,5},{5,4},{6,7},{7,6},{8,9},{9,8},{10,11... | collective-permute-start | bytes 1572872 | tf_op jit(solution)/shard_map/neg_terms/ppermute | solution.py:19
  39.3 39.1 %all-to-all-start.1 = ((bf16[64,16,512]{2,1,0:T(8,128)(2,1)}), bf16[64,16,512]{2,1,0:T(8,128)(2,1)S(1)}, u32[]{:S(2)}, u32[]{:S(2)}) async-start(bf16[64,16,512]{2,1,0:T(8,128)(2,1)} %bitcast.67), calls=%async_computation.1 | async-start | bytes 2097152 | tf_op jit(solution)/shard_map/pack_tails/all_to_all | solution.py:195
  49.7 2.3 %copy-start.3 = (f32[1024,512]{1,0:T(8,128)S(1)}, f32[1024,512]{1,0:T(8,128)}, u32[]{:S(2)}) copy-start(f32[1024,512]{1,0:T(8,128)} %copy-done.2) | copy-start | bytes 6291460
  51.9 1.0 copy-start.10
  51.9 1.0 copy-start.15
  51.9 1.0 copy-start.16
  52.0 1.0 copy-start.22
  52.0 1.0 copy-start.23
  52.2 2.5 %collective-permute-start.10 = (bf16[512,512]{1,0:T(8,128)(2,1)S(1)}, bf16[512,512]{1,0:T(8,128)(2,1)S(1)}, u32[]{:S(2)}, u32[]{:S(2)}) collective-permute-start(bf16[512,512]{1,0:T(8,128)(2,1)S(1)} %fusion.19.dquery_ref), channel_id=1, source_target_pairs={{0,1},{1,0},{2,3},{3,2},{4,5},{5,4},{6,7},{7,6},{8,9},{9,8},{10,11... | collective-permute-start | bytes 1572872 | tf_op jit(solution)/shard_map/rel_terms/ppermute | solution.py:19
  56.1 0.8 copy-start.4
  56.1 1.7 %copy-start.5 = (f32[1,256,512]{2,1,0:T(8,128)}, f32[1,256,512]{2,1,0:T(8,128)S(1)}, u32[]{:S(2)}) copy-start(f32[1,256,512]{2,1,0:T(8,128)S(1)} %get-tuple-element.23) | copy-start | bytes 1572868
  56.1 3.3 %copy-start.6 = (f32[1,256,512]{2,1,0:T(8,128)}, f32[1,256,512]{2,1,0:T(8,128)S(1)}, u32[]{:S(2)}) copy-start(f32[1,256,512]{2,1,0:T(8,128)S(1)} %get-tuple-element.24) | copy-start | bytes 1572868
  56.1 4.0 %copy-start.7 = (f32[1,256,512]{2,1,0:T(8,128)}, f32[1,256,512]{2,1,0:T(8,128)S(1)}, u32[]{:S(2)}) copy-start(f32[1,256,512]{2,1,0:T(8,128)S(1)} %get-tuple-element.25) | copy-start | bytes 1572868
  57.8 20.7 %collective-permute-start.11 = (bf16[2,256,512]{2,1,0:T(8,128)(2,1)}, bf16[2,256,512]{2,1,0:T(8,128)(2,1)S(1)}, u32[]{:S(2)}, u32[]{:S(2)}) collective-permute-start(bf16[2,256,512]{2,1,0:T(8,128)(2,1)} %select_convert_fusion.1), channel_id=1, source_target_pairs={{0,64},{64,0},{128,192},{192,128},{1,65},{65,1},{129,193},{193,129... | collective-permute-start | bytes 1572872 | tf_op jit(solution)/shard_map/rel_terms/ppermute | solution.py:19
  60.2 11.3 %collective-permute-start.7 = (bf16[8,16,512]{2,1,0:T(8,128)(2,1)}, bf16[8,16,512]{2,1,0:T(8,128)(2,1)}, u32[]{:S(2)}, u32[]{:S(2)}) collective-permute-start(bf16[8,16,512]{2,1,0:T(8,128)(2,1)} %bitcast.7), channel_id=1, source_target_pairs={{0,4},{2,6},{4,0},{6,2},{1,5},{3,7},{5,1},{7,3},{8,12},{10,14},{12... | collective-permute-start | bytes 393224 | tf_op jit(solution)/shard_map/neg_terms/ppermute | solution.py:19
  62.2 12.8 %collective-permute-start.6 = (bf16[8,16,512]{2,1,0:T(8,128)(2,1)}, bf16[8,16,512]{2,1,0:T(8,128)(2,1)}, u32[]{:S(2)}, u32[]{:S(2)}) collective-permute-start(bf16[8,16,512]{2,1,0:T(8,128)(2,1)} %bitcast.6), channel_id=1, source_target_pairs={{0,6},{2,4},{4,2},{6,0},{1,7},{3,5},{5,3},{7,1},{8,14},{10,12},{12... | collective-permute-start | bytes 393224 | tf_op jit(solution)/shard_map/neg_terms/ppermute | solution.py:19
  62.2 12.8 %collective-permute-start.5 = (bf16[8,16,512]{2,1,0:T(8,128)(2,1)}, bf16[8,16,512]{2,1,0:T(8,128)(2,1)}, u32[]{:S(2)}, u32[]{:S(2)}) collective-permute-start(bf16[8,16,512]{2,1,0:T(8,128)(2,1)} %bitcast.5), channel_id=1, source_target_pairs={{0,2},{2,0},{4,6},{6,4},{1,3},{3,1},{5,7},{7,5},{8,10},{10,8},{12,... | collective-permute-start | bytes 393224 | tf_op jit(solution)/shard_map/neg_terms/ppermute | solution.py:19
  78.5 4.8 %copy-start.11 = (bf16[2,256,512]{2,1,0:T(8,128)(2,1)}, bf16[2,256,512]{2,1,0:T(8,128)(2,1)S(1)}, u32[]{:S(2)}) copy-start(bf16[2,256,512]{2,1,0:T(8,128)(2,1)S(1)} %collective-permute-done.11) | copy-start | bytes 1572868
  78.5 14.0 %all-to-all-start.2 = ((bf16[8,16,512]{2,1,0:T(8,128)(2,1)}), bf16[8,16,512]{2,1,0:T(8,128)(2,1)S(1)}, u32[]{:S(2)}, u32[]{:S(2)}) async-start(bf16[8,16,512]{2,1,0:T(8,128)(2,1)} %add_convert_fusion), calls=%async_computation.2 | async-start | bytes 262144 | tf_op jit(solution)/shard_map/neg_exchange/all_to_all | solution.py:254
  83.4 1.6 %copy-start.1 = (bf16[4,512,512]{2,1,0:T(8,128)(2,1)S(1)}, bf16[4,512,512]{2,1,0:T(8,128)(2,1)}, u32[]{:S(2)}) copy-start(bf16[4,512,512]{2,1,0:T(8,128)(2,1)} %relations_ref.1) | copy-start | bytes 6291460
  94.0 39.1 %all-to-all-start.3 = ((bf16[64,80,128]{2,1,0:T(8,128)(2,1)}), bf16[64,80,128]{2,1,0:T(8,128)(2,1)S(1)}, u32[]{:S(2)}, u32[]{:S(2)}) async-start(bf16[64,80,128]{2,1,0:T(8,128)(2,1)} %finish.1), calls=%async_computation.3 | async-start | bytes 2621440 | tf_op jit(solution)/shard_map/send_heads/all_to_all | solution.py:256
  101.2 9.9 %collective-permute-start.12 = (bf16[256,512]{1,0:T(8,128)(2,1)}, bf16[256,512]{1,0:T(8,128)(2,1)}, u32[]{:S(2)}, u32[]{:S(2)}) collective-permute-start(bf16[256,512]{1,0:T(8,128)(2,1)} %fusion.33), channel_id=1, source_target_pairs={{0,192},{64,128},{128,64},{192,0},{1,193},{65,129},{129,65},{193,1... | collective-permute-start | bytes 786440 | tf_op jit(solution)/shard_map/rel_sum/ppermute | solution.py:19
  112.2 0.8 copy-start.9
  113.0 10.4 %collective-permute-start.15 = (f32[8,8,512]{2,1,0:T(8,128)S(1)}, f32[8,8,512]{2,1,0:T(8,128)S(1)}, u32[]{:S(2)}, u32[]{:S(2)}) collective-permute-start(f32[8,8,512]{2,1,0:T(8,128)S(1)} %get-tuple-element.27), channel_id=1, source_target_pairs={{0,4},{2,6},{4,0},{6,2},{1,5},{3,7},{5,1},{7,3},{8,12},{10,14},{12... | collective-permute-start | bytes 393224 | tf_op jit(solution)/shard_map/rel_sum/ppermute | solution.py:19
  115.2 12.2 %collective-permute-start.14 = (f32[8,8,512]{2,1,0:T(8,128)S(1)}, f32[8,8,512]{2,1,0:T(8,128)S(1)}, u32[]{:S(2)}, u32[]{:S(2)}) collective-permute-start(f32[8,8,512]{2,1,0:T(8,128)S(1)} %get-tuple-element.28), channel_id=1, source_target_pairs={{0,6},{2,4},{4,2},{6,0},{1,7},{3,5},{5,3},{7,1},{8,14},{10,12},{12... | collective-permute-start | bytes 393224 | tf_op jit(solution)/shard_map/rel_sum/ppermute | solution.py:19
  115.2 12.2 %collective-permute-start.13 = (f32[8,8,512]{2,1,0:T(8,128)S(1)}, f32[8,8,512]{2,1,0:T(8,128)S(1)}, u32[]{:S(2)}, u32[]{:S(2)}) collective-permute-start(f32[8,8,512]{2,1,0:T(8,128)S(1)} %get-tuple-element.26), channel_id=1, source_target_pairs={{0,2},{2,0},{4,6},{6,4},{1,3},{3,1},{5,7},{7,5},{8,10},{10,8},{12,... | collective-permute-start | bytes 393224 | tf_op jit(solution)/shard_map/rel_sum/ppermute | solution.py:19
  133.1 12.6 %all-to-all-start.4 = ((f32[8,8,512]{2,1,0:T(8,128)}), f32[8,8,512]{2,1,0:T(8,128)S(1)}, u32[]{:S(2)}, u32[]{:S(2)}) async-start(f32[8,8,512]{2,1,0:T(8,128)} %fusion.43), calls=%async_computation.4 | async-start | bytes 262144 | tf_op jit(solution)/shard_map/rel_sum/all_to_all | solution.py:261

commit v3 on v2

v3 whole, which is shorter than its diff:
```python
import jax
import jax.numpy as jnp
from jax import lax
from jax.experimental import pallas as pl
from jax.experimental.pallas import tpu as pltpu
from jax.sharding import Mesh, PartitionSpec as P

CLS_DEV = 2048
CAP = 16
CAP_N = 2
SIZES = {"y": 4, "z": 8, "x": 4, "c": 2}
SHARD = ("z", "x", "c")
ALL = ("y",) + SHARD
BF = jnp.bfloat16
F32 = jnp.float32


def swap(a, axis, flip):
    return lax.ppermute(a, axis, [(i, i ^ flip) for i in range(SIZES[axis])])


def pair_keep(arrived, keep):
    keep = keep + arrived.astype(F32)
    low = lax.axis_index("y") < 2
    send = jnp.where(low, keep[1], keep[0]).astype(BF)
    return jnp.where(low, keep[0], keep[1]) + swap(send, "y", 3).astype(F32)


def column_sum(own, dtype):
    me = lax.axis_index("x")
    block = lambda flip: lax.dynamic_index_in_dim(own, me ^ flip, 1, keepdims=False)
    moved = [swap(block(flip).astype(dtype), "x", flip).astype(F32) for flip in (1, 3, 2)]
    return block(0) + moved[0] + moved[1] + moved[2]


def onehot_of(slots, count):
    return lax.broadcasted_iota(jnp.int32, (count, slots.shape[1]), 0) == slots


def eye(n):
    return lax.broadcasted_iota(jnp.int32, (n, n), 0) == lax.broadcasted_iota(jnp.int32, (n, n), 1)


def to_column(row):
    return jnp.sum(jnp.where(eye(row.shape[1]), row.astype(F32), 0.0), axis=1, keepdims=True)


def query_kernel(heads_ref, rel_ref, relations_ref, query_ref, column_ref):
    heads = heads_ref[...].astype(F32)
    rel = to_column(rel_ref[...])
    column_ref[...] = rel.astype(jnp.int32)
    total = jnp.zeros(heads.shape, F32)
    for r in range(relations_ref.shape[0]):
        masked = jnp.where(rel == r, heads, 0.0).astype(BF)
        total += jnp.dot(masked, relations_ref[r], preferred_element_type=F32)
    query_ref[...] = total.astype(BF)


def make_query(heads, rel_id, relations):
    n = heads.shape[0]
    return pl.pallas_call(
        query_kernel,
        out_shape=(jax.ShapeDtypeStruct(heads.shape, BF), jax.ShapeDtypeStruct((n, 1), jnp.int32)),
        compiler_params=pltpu.CompilerParams(vmem_limit_bytes=32 * 2**20),
        cost_estimate=pl.CostEstimate(flops=4 * 10**9, bytes_accessed=4 * 2**20, transcendentals=0),
        name="query",
    )(heads, rel_id.reshape(1, n), relations)


FIELDS = dict(head_hi=0, tail_hi=16, neg_hi=32, head_lo=34, tail_lo=50, neg_lo=66, gpos_hi=68, gpos_lo=84)


def slots_kernel(ho_ref, to_ref, no_ref, hr_ref, tr_ref, nr_ref, hs_ref, ts_ref, ns_ref, line_ref, rank_ref):
    owners = line_ref.shape[0]
    line = jnp.zeros((owners, 128), F32)
    kinds = (("head", CAP, ho_ref, hr_ref, hs_ref), ("tail", CAP, to_ref, tr_ref, ts_ref), ("neg", CAP_N, no_ref, nr_ref, ns_ref))
    for kind, cap, owner_ref, row_ref, slots_ref in kinds:
        column = owner_ref[...].astype(F32)
        n = column.shape[0]
        row = jnp.sum(jnp.where(eye(n), column, 0.0), axis=0, keepdims=True)
        down = lax.broadcasted_iota(jnp.int32, (n, n), 0)
        across = lax.broadcasted_iota(jnp.int32, (n, n), 1)
        same = column == row
        rank_row = jnp.sum(jnp.where(same & (down < across), 1.0, 0.0), axis=0, keepdims=True)
        rank = jnp.sum(jnp.where(same & (across < down), 1.0, 0.0), axis=1, keepdims=True).astype(jnp.int32)
        slots_ref[...] = (row * cap + rank_row).astype(jnp.int32)
        if kind == "tail":
            rank_ref[...] = rank
        value = to_column(row_ref[...]).astype(jnp.int32) + 1
        field = lax.broadcasted_iota(jnp.int32, (n, 128), 1)
        put = jnp.where(field == FIELDS[kind + "_hi"] + rank, (value >> 7).astype(F32), 0.0)
        put += jnp.where(field == FIELDS[kind + "_lo"] + rank, (value & 127).astype(F32), 0.0)
        hot = lax.broadcasted_iota(jnp.int32, (owners, n), 0) == row.astype(jnp.int32)
        line += jnp.dot(jnp.where(hot, 1.0, 0.0).astype(BF), put.astype(BF), preferred_element_type=F32)
    wide = jnp.broadcast_to(line[:, None, :], (owners, 8, 128))
    line_ref[...] = jnp.where(lax.broadcasted_iota(jnp.int32, wide.shape, 1) == 0, wide, 0.0).astype(BF)


def make_slots(columns, rows, owners):
    return pl.pallas_call(
        slots_kernel,
        out_shape=tuple(jax.ShapeDtypeStruct((1, c.shape[0]), jnp.int32) for c in columns)
        + (jax.ShapeDtypeStruct((owners, 8, 128), BF), jax.ShapeDtypeStruct(columns[1].shape, jnp.int32)),
        compiler_params=pltpu.CompilerParams(vmem_limit_bytes=32 * 2**20),
        cost_estimate=pl.CostEstimate(flops=4 * 10**9, bytes_accessed=2**20, transcendentals=0),
        name="slots",
    )(*columns, *[r.reshape(1, -1) for r in rows])


def weights_kernel(count_ref, query_ref, tail_ref, near_ref, far_ref, dquery_ref, gpos_ref, own_ref, other_ref):
    query, near, far = query_ref[...], near_ref[...], far_ref[...]
    tails = tail_ref[...].astype(F32)
    n = query.shape[0]
    scores = lambda negatives: lax.dot_general(query, negatives, (((1,), (1,)), ((), ())), preferred_element_type=F32)
    near_scores, far_scores = scores(near), scores(far)
    positive = jnp.sum(query.astype(F32) * tails, axis=1, keepdims=True)
    top = jnp.maximum(jnp.max(near_scores, axis=1, keepdims=True), jnp.max(far_scores, axis=1, keepdims=True))
    top = jnp.maximum(positive, top)
    pos_exp = jnp.exp(positive - top)
    near_exp, far_exp = jnp.exp(near_scores - top), jnp.exp(far_scores - top)
    total = pos_exp + jnp.sum(near_exp, axis=1, keepdims=True) + jnp.sum(far_exp, axis=1, keepdims=True)
    live = lax.broadcasted_iota(jnp.int32, (n, 1), 0) < count_ref[0, 0]
    gpos = jnp.where(live, pos_exp / total - 1.0, 0.0)
    share = jnp.where(live, 1.0 / total, 0.0)
    near_w, far_w = (near_exp * share).astype(BF), (far_exp * share).astype(BF)
    terms = lambda w: lax.dot_general(w, query, (((0,), (0,)), ((), ())), preferred_element_type=F32)
    other_ref[...] = terms(far_w).astype(BF)
    own_ref[...] = terms(near_w)
    dquery = gpos * tails + jnp.dot(near_w, near, preferred_element_type=F32)
    dquery_ref[...] = (dquery + jnp.dot(far_w, far, preferred_element_type=F32)).astype(BF)
    gpos_ref[...] = gpos


def weights(counts, query, tails, near, far):
    n, width = query.shape
    shape = lambda rows, dtype: jax.ShapeDtypeStruct((rows, width), dtype)
    m = near.shape[0]
    return pl.pallas_call(
        weights_kernel,
        in_specs=[pl.BlockSpec(memory_space=pltpu.SMEM)] + [pl.BlockSpec(memory_space=pltpu.VMEM)] * 4,
        out_shape=(shape(n, BF), jax.ShapeDtypeStruct((n, 1), F32), shape(m, F32), shape(m, BF)),
        compiler_params=pltpu.CompilerParams(vmem_limit_bytes=40 * 2**20),
        name="weights",
    )(counts, query, tails, near, far)


NEGS, LINE, SUB = 4 * CAP, 4 * CAP + 8, 4 * CAP + 16


def tails_kernel(query_ref, slots_ref, out_ref):
    hot = jnp.where(onehot_of(slots_ref[...], out_ref.shape[0]), 1.0, 0.0).astype(BF)
    out_ref[...] = jnp.dot(hot, query_ref[...], preferred_element_type=F32).astype(BF)


def pack_tails(query, slots, owners):
    return pl.pallas_call(
        tails_kernel,
        out_shape=jax.ShapeDtypeStruct((owners * CAP, query.shape[1]), BF),
        compiler_params=pltpu.CompilerParams(vmem_limit_bytes=32 * 2**20),
        cost_estimate=pl.CostEstimate(flops=10**9, bytes_accessed=2**20, transcendentals=0),
        name="pack_tails",
    )(query, slots)


def heads_kernel(dquery_ref, rel_ref, relations_ref, slots_ref, line_ref, gpos_ref, rank_ref, tail_slots_ref, out_ref):
    owners = out_ref.shape[0]
    dquery = dquery_ref[...].astype(F32)
    n = dquery.shape[0]
    dhead = jnp.zeros(dquery.shape, F32)
    for r in range(relations_ref.shape[0]):
        masked = jnp.where(rel_ref[...] == r, dquery, 0.0).astype(BF)
        dhead += lax.dot_general(masked, relations_ref[r], (((1,), (1,)), ((), ())), preferred_element_type=F32)
    hot = jnp.where(onehot_of(slots_ref[...], owners * CAP), 1.0, 0.0).astype(BF)
    rows = jnp.dot(hot, dhead.astype(BF), preferred_element_type=F32).astype(BF)
    for block in range(4):
        at = block * CAP
        out_ref[:, at:at + CAP, :] = rows[:, block * 128:(block + 1) * 128].reshape(owners, CAP, 128)
    gpos = gpos_ref[...]
    high = gpos.astype(BF).astype(F32)
    field = lax.broadcasted_iota(jnp.int32, (n, 128), 1)
    put = jnp.where(field == FIELDS["gpos_hi"] + rank_ref[...], high, 0.0)
    put += jnp.where(field == FIELDS["gpos_lo"] + rank_ref[...], gpos - high, 0.0)
    of_owner = lax.broadcasted_iota(jnp.int32, (owners, n), 0) == tail_slots_ref[...] // CAP
    extra = jnp.dot(jnp.where(of_owner, 1.0, 0.0).astype(BF), put.astype(BF), preferred_element_type=F32)
    wide = jnp.broadcast_to(extra[:, None, :], (owners, 8, 128))
    wide = jnp.where(lax.broadcasted_iota(jnp.int32, wide.shape, 1) == 0, wide, 0.0)
    line = (line_ref[...].astype(F32) + wide).astype(BF)
    out_ref[:, NEGS:, :] = jnp.concatenate([jnp.zeros((owners, 8, 128), F32), line.astype(F32)], axis=1).astype(BF)


def pack_heads(dquery, rel_id, relations, slots, line, gpos, rank, tail_slots):
    return pl.pallas_call(
        heads_kernel,
        out_shape=jax.ShapeDtypeStruct((line.shape[0], SUB, 128), BF),
        compiler_params=pltpu.CompilerParams(vmem_limit_bytes=40 * 2**20),
        name="pack_heads",
    )(dquery, rel_id, relations, slots, line, gpos, rank, tail_slots)


def negs_kernel(terms_ref, slots_ref, have_ref, out_ref):
    owners = out_ref.shape[0]
    grad = jnp.sum(terms_ref[...].astype(F32), axis=0).astype(BF)
    entry = lax.broadcasted_iota(jnp.int32, (owners * 8, grad.shape[0]), 0)
    filled = (entry // 8) * CAP_N + entry % CAP_N == slots_ref[...]
    column = (entry % 8) // CAP_N
    rows = jnp.zeros((owners * 8, 128), F32)
    for block in range(4):
        hot = jnp.where(filled & (column == block), 1.0, 0.0).astype(BF)
        rows += jnp.dot(hot, grad[:, block * 128:(block + 1) * 128], preferred_element_type=F32)
    out_ref[...] = rows.reshape(owners, 8, 128).astype(BF)


def pack_negs(terms, slots, have):
    return pl.pallas_call(
        negs_kernel,
        grid=(1,),
        in_specs=[
            pl.BlockSpec(terms.shape, lambda i: (0, 0, 0)),
            pl.BlockSpec(slots.shape, lambda i: (0, 0)),
            pl.BlockSpec(memory_space=pl.ANY),
        ],
        out_specs=pl.BlockSpec((have.shape[0], 8, 128), lambda i: (0, NEGS // 8, 0)),
        out_shape=jax.ShapeDtypeStruct(have.shape, BF),
        input_output_aliases={2: 0},
        name="pack_negs",
    )(terms, slots, have)


def relation_kernel(inner_ref, both_ref, rel_ref, far_rel_ref, dquery_ref, far_ref, send_ref, keep_ref):
    n = dquery_ref.shape[0]
    near_rel, far_rel = rel_ref[...], to_column(far_rel_ref[...]).astype(jnp.int32)
    near_dquery, far_dquery = dquery_ref[...], far_ref[...]
    inner = inner_ref[0, 0] == 1

    def terms(relation):
        def part(rel, heads, dquery):
            masked = jnp.where(rel == relation, heads.astype(F32), 0.0).astype(BF)
            return lax.dot_general(masked, dquery, (((0,), (0,)), ((), ())), preferred_element_type=F32)

        return part(near_rel, both_ref[:n, :], near_dquery) + part(far_rel, both_ref[n:, :], far_dquery)

    for at, (outer_one, inner_one) in enumerate(((0, 1), (3, 2))):
        outer_terms, inner_terms = terms(outer_one), terms(inner_one)
        send_ref[at] = jnp.where(inner, outer_terms, inner_terms).astype(BF)
        keep_ref[at] = jnp.where(inner, inner_terms, outer_terms)


def relation_terms(inner, both, rel, far_rel, dquery, far_dquery):
    shape = (2, both.shape[1], dquery.shape[1])
    return pl.pallas_call(
        relation_kernel,
        in_specs=[pl.BlockSpec(memory_space=pltpu.SMEM)] + [pl.BlockSpec(memory_space=pltpu.VMEM)] * 5,
        out_shape=(jax.ShapeDtypeStruct(shape, BF), jax.ShapeDtypeStruct(shape, F32)),
        compiler_params=pltpu.CompilerParams(vmem_limit_bytes=40 * 2**20),
        name="relation_terms",
    )(inner, both, rel, far_rel, dquery, far_dquery)


def spread_line(block, high, low, scale, cap):
    owners = block.shape[0]
    line = block.astype(F32)[:, 0, :].astype(BF)
    total = owners * cap
    field = lax.broadcasted_iota(jnp.int32, (128, total), 0)
    place = lax.broadcasted_iota(jnp.int32, (128, total), 1) % cap
    take = jnp.where(field == FIELDS[high] + place, scale, 0.0)
    take += jnp.where(field == FIELDS[low] + place, 1.0, 0.0)
    every = jnp.dot(line, take.astype(BF), preferred_element_type=F32)
    mine = lax.broadcasted_iota(jnp.int32, (owners, total), 1) // cap
    mine = mine == lax.broadcasted_iota(jnp.int32, (owners, total), 0)
    return jnp.sum(jnp.where(mine, every, 0.0), axis=0, keepdims=True)


def combine_kernel(tails_ref, got_ref, out_ref, rows_of, ids, weights_of):
    owners = got_ref.shape[0]
    slots, negs = owners * CAP, owners * CAP_N
    rows = out_ref.shape[0]

    @pl.when(pl.program_id(0) == 0)
    def _():
        for block in range(4):
            at = block * CAP
            rows_of[:slots, block * 128:(block + 1) * 128] = got_ref[:, at:at + CAP, :].reshape(slots, 128)
        packed = got_ref[:, NEGS:LINE, :].reshape(owners * 8, 128)
        entry = lax.broadcasted_iota(jnp.int32, (negs, owners * 8), 0)
        source = lax.broadcasted_iota(jnp.int32, (negs, owners * 8), 1)
        for block in range(4):
            take = jnp.where(source == entry // CAP_N * 8 + block * CAP_N + entry % CAP_N, 1.0, 0.0).astype(BF)
            rows_of[slots:, block * 128:(block + 1) * 128] = jnp.dot(take, packed, preferred_element_type=F32).astype(BF)
        line = got_ref[:, LINE:, :]
        for first, kind, cap in ((0, "head", CAP), (slots, "neg", CAP_N), (slots + negs, "tail", CAP)):
            row = spread_line(line, kind + "_hi", kind + "_lo", 128.0, cap)
            ids[:, first:first + owners * cap] = row.astype(jnp.int32) - 1
        weights_of[...] = spread_line(line, "gpos_hi", "gpos_lo", 1.0, CAP)

    first = pl.program_id(0) * rows
    labels = ids[...]
    here = (labels >= first) & (labels < first + rows)
    here = jnp.where(here, labels - first, -1).astype(F32).astype(BF)
    cut = slots + negs

    def hot(labels, weights):
        place = lax.broadcasted_iota(jnp.int32, (rows, labels.shape[1]), 0).astype(F32).astype(BF)
        return jnp.where(place == labels, weights, jnp.zeros((1, 1), BF))

    total = jnp.dot(hot(here[:, :cut], jnp.ones((1, 1), BF)), rows_of[...], preferred_element_type=F32)
    total += jnp.dot(hot(here[:, cut:], weights_of[...].astype(BF)), tails_ref[...], preferred_element_type=F32)
    out_ref[...] = total


def combine(tails, got):
    tile, width = 256, tails.shape[1]
    slots, negs = got.shape[0] * CAP, got.shape[0] * CAP_N
    return pl.pallas_call(
        combine_kernel,
        grid=(CLS_DEV // tile,),
        in_specs=[pl.BlockSpec(tails.shape, lambda i: (0, 0)), pl.BlockSpec(got.shape, lambda i: (0, 0, 0))],
        out_specs=pl.BlockSpec((tile, width), lambda i: (i, 0)),
        out_shape=jax.ShapeDtypeStruct((CLS_DEV, width), F32),
        scratch_shapes=[
            pltpu.VMEM((slots + negs, width), BF),
            pltpu.VMEM((1, 2 * slots + negs), jnp.int32),
            pltpu.VMEM((1, slots), F32),
        ],
        compiler_params=pltpu.CompilerParams(vmem_limit_bytes=40 * 2**20),
        cost_estimate=pl.CostEstimate(flops=8 * 10**9, bytes_accessed=8 * 2**20, transcendentals=0),
        name="combine",
    )(tails, got)


def on_device(
    head_vecs, tail_vecs, rel_id, head_owner, head_row, tail_owner, tail_row,
    neg_vecs, neg_owner, neg_row, counts, relations,
):
    n, width = head_vecs.shape
    rels = relations.shape[0]
    owners = SIZES["z"] * SIZES["x"] * SIZES["c"]
    core = lax.axis_index("c")

    with jax.named_scope("query"):
        query, rel_column = make_query(head_vecs, rel_id, relations)
    with jax.named_scope("slots"):
        *slots, line, tail_rank = make_slots(
            (head_owner, tail_owner, neg_owner), (head_row, tail_row, neg_row), owners
        )
    with jax.named_scope("gather_negatives"):
        wide = jnp.broadcast_to(neg_vecs[None], (SIZES["z"],) + neg_vecs.shape)
        column = lax.all_to_all(wide, "z", 0, 0, tiled=True).reshape(-1, width)
        tail_rows = pack_tails(query, slots[1], owners)
        column, tail_rows = lax.optimization_barrier((column, tail_rows))
        near = jnp.concatenate([column] + [swap(column, "x", flip) for flip in (1, 3, 2)], axis=0)
        near, tail_rows = lax.optimization_barrier((near, tail_rows))
        far = swap(near, "c", 1)
    with jax.named_scope("send_tails"):
        got_tails = lax.all_to_all(tail_rows.reshape(owners, CAP, width), SHARD, 0, 0, tiled=True)
    with jax.named_scope("rel_heads"):
        feature = lax.broadcasted_iota(jnp.int32, (width, width // 2), 0)
        place = lax.broadcasted_iota(jnp.int32, (width, width // 2), 1)
        wanted = (feature == place // 8 * 16 + core * 8 + place % 8).astype(BF)
        both = jnp.concatenate([head_vecs, swap(head_vecs, "c", 1)], axis=0)
        both = jnp.dot(both, wanted, preferred_element_type=F32).astype(BF)
        far_rel = swap(rel_id, "c", 1).reshape(1, n)
        row = lax.axis_index("y")
        inner = ((row == 1) | (row == 2)).astype(jnp.int32).reshape(1, 1)

    with jax.named_scope("weights"):
        dquery, gpos, own, other = weights(counts, query, tail_vecs, near, far)
    with jax.named_scope("neg_sum"):
        own = own + swap(other, "c", 1).astype(F32)
        own = own.reshape(4, 8, -1, width)
        moved = [swap(own[at].astype(BF), "x", flip).astype(F32) for at, flip in ((1, 1), (2, 3), (3, 2))]
        own = (own[0] + moved[0] + moved[1] + moved[2]).astype(BF)
    with jax.named_scope("pack_heads"):
        heads = pack_heads(dquery, rel_column, relations, slots[0], line, gpos, tail_rank, slots[1])
    with jax.named_scope("rel_sum"):
        mine, keep = relation_terms(inner, both, rel_column, far_rel, dquery, swap(dquery, "c", 1))
    own, got_tails, heads, mine, keep = lax.optimization_barrier((own, got_tails, heads, mine, keep))
    with jax.named_scope("neg_exchange"):
        terms = lax.all_to_all(own, "z", 0, 0, tiled=True)
    with jax.named_scope("rel_halves"):
        mine = swap(mine, "y", 1)
        terms, mine = lax.optimization_barrier((terms, mine))
    with jax.named_scope("send_heads"):
        got = lax.all_to_all(pack_negs(terms, slots[2], heads), SHARD, 0, 0, tiled=True)
    with jax.named_scope("rel_column"):
        mine = column_sum(pair_keep(mine, keep).reshape(8, 4, 8, width), F32)
        mine, got = lax.optimization_barrier((mine, got))
    with jax.named_scope("rel_end"):
        relation_grad = jnp.sum(lax.all_to_all(mine, "z", 0, 0, tiled=True), axis=0)
    with jax.named_scope("combine"):
        owned = combine(got_tails.reshape(-1, width), got)
    return owned[None], relation_grad


def solution(mesh):
    fine = Mesh(mesh.devices.reshape(*SIZES.values()), tuple(SIZES))
    whole = P(ALL)
    wide = P(ALL, None)
    return jax.shard_map(
        on_device,
        mesh=fine,
        in_specs=(
            wide, wide, whole, wide, whole, wide, whole, wide, wide, whole, P("y", SHARD), P(),
        ),
        out_specs=(P("y", SHARD, None), wide),
        check_vma=False,
    )
```

time: 148 us -> 142 us (0.959)
  blocking collectives: 0 us -> 12.5 us
  other arithmetic: 18.5 us -> 6.15 us
  matrix products: 9.61 us -> 1.53 us
  waiting for transfers between devices: 42.9 us -> 35.6 us
  Pallas kernels: 12.6 us -> 19.8 us
  local copies, waits for them, and re-layouts: 9.64 us -> 15.9 us
  starting transfers between devices: 51.2 us -> 46.9 us
    all_to_all x0 -> x1, blocking collectives: none -> 12.5 us  [on_device(): terms = lax.all_to_all(own, 'z', 0, 0, tiled=True)]
    unnamed x52 -> x47, local copies, waits for them, and re-layouts: 5.17 us -> 14.4 us
    pallas_call x2 -> x7, Pallas kernels: 3.36 us -> 12.1 us  [the longest x1 2.36 us: weights(): pl.pallas_call(weights_kernel, in_specs=[pl.BlockSpec(memory_space=pltpu....]
    dot_general x6 -> x0, matrix products: 8.04 us -> none  [the longest x1 2.21 us: on_device(): jnp.dot(gneg, negatives, preferred_element_type=F32)]
    all_to_all x2 -> x1, waiting for transfers between devices: 9.72 us -> 4.05 us  [on_device(): lax.all_to_all(pack_negs(terms, slots[2], heads), SHARD, 0, 0, tiled=True)]
    reduce_sum x8 -> x0, other arithmetic: 4.2 us -> none  [the longest x3 2.73 us: slots_of(): jnp.sum(jnp.where((column == row) & before, 1, 0), axis=0, keepdims=True)]
    ppermute x16, waiting for transfers between devices: 31.5 us -> 27.9 us  [swap(): return lax.ppermute(a, axis, [(i, i ^ flip) for i in range(SIZES[axis])])]
    all_to_all x2 -> x1, starting transfers between devices: 9.24 us -> 6.36 us  [on_device(): lax.all_to_all(pack_negs(terms, slots[2], heads), SHARD, 0, 0, tiled=True)]
  transfers between devices with their start and end apart: 21 -> 20, of which waited for: 12 -> 13; matrix products, arithmetic and copies ran while one was open for 21% -> 7% of each run, Pallas kernels for 8% -> 13%
where the time goes in v3:
time: 142 us; the launch traced here: 140 us
  starting transfers between devices  46.9 us (33%)
  waiting for transfers between devices  35.6 us (25%)
  Pallas kernels  19.8 us (14%)
  local copies, waits for them, and re-layouts  15.9 us (11%)
  blocking collectives  12.5 us (9%)
  other arithmetic  6.15 us (4%)
  between operations  1.63 us (1%)
  matrix products  1.53 us (1%)
    ppermute x16, waiting for transfers between devices, swap(): return lax.ppermute(a, axis, [(i, i ^ flip) for i in range(SIZES[axis])])  27.9 us
    ppermute x16, starting transfers between devices, swap(): return lax.ppermute(a, axis, [(i, i ^ flip) for i in range(SIZES[axis])])  18.3 us
    unnamed x47, local copies, waits for them, and re-layouts  14.4 us
    all_to_all x1, blocking collectives, on_device(): terms = lax.all_to_all(own, 'z', 0, 0, tiled=True)  12.5 us
    all_to_all x1, starting transfers between devices, on_device(): lax.all_to_all(tail_rows.reshape(owners, CAP, width), SHARD, 0, 0, tiled=...  10.4 us
    all_to_all x1, starting transfers between devices, on_device(): column = lax.all_to_all(wide, 'z', 0, 0, tiled=True).reshape(-1, width)  8.47 us
    pallas_call x1, Pallas kernels, combine(): pl.pallas_call(combine_kernel, grid=(CLS_DEV // tile,), in_specs=[pl.Bloc...  7.75 us
    all_to_all x1, starting transfers between devices, on_device(): lax.all_to_all(pack_negs(terms, slots[2], heads), SHARD, 0, 0, tiled=True)  6.36 us
  transfers between devices with their start and end apart: 20, of which 13 were waited for; matrix products, arithmetic and copies ran while one was open for 7% of the time, Pallas kernels for 13%

profile of v3, /device:TPU:2, one launch (start us, length us, event | category | flops | bytes accessed | tf_op | source)
XLA Modules:
  0.0 140.0 jit_solution(1145938093150556550)
XLA Ops:
  0.6 1.4 broadcast_in_dim.4
  2.0 8.5 %all-to-all-start = ((bf16[8,16,512]{2,1,0:T(8,128)(2,1)}), bf16[8,16,512]{2,1,0:T(8,128)(2,1)S(1)}, u32[]{:S(2)}, u32[]{:S(2)}) async-start(bf16[8,16,512]{2,1,0:T(8,128)(2,1)} %broadcast_in_dim.4), calls=%async_computation | async-start | bytes 262144 | tf_op jit(solution)/shard_map/gather_negatives/all_to_all | solution.py:347
  11.2 0.8 copy.15.ho_ref
  12.0 0.8 copy.16.to_ref
  12.9 1.6 %copy-done.1 = bf16[4,512,512]{2,1,0:T(8,128)(2,1)S(1)} copy-done((bf16[4,512,512]{2,1,0:T(8,128)(2,1)S(1)}, bf16[4,512,512]{2,1,0:T(8,128)(2,1)}, u32[]{:S(2)}) %copy-start.1) | copy-done | bytes 2097176
  14.5 1.0 copy-done.13
  16.2 1.3 query.1
  17.6 1.0 slots.1
  19.8 1.7 %pack_tails.1 = bf16[1024,512]{1,0:T(8,128)(2,1)} custom-call(bf16[512,512]{1,0:T(8,128)(2,1)S(1)} %get-tuple-element.28.query_ref, s32[1,512]{1,0:T(1,128)S(1)} %get-tuple-element.29.slots_ref.tail_slots_ref), custom_call_target="tpu_custom_call" | custom-call | flops 1000000000 | bytes 1048576 | tf_op jit(solution)/shard_map/gather_negatives/pack_tails/pallas_call | solution.py:156
  21.5 2.1 %collective-permute-start.2 = (bf16[128,512]{1,0:T(8,128)(2,1)S(1)}, bf16[128,512]{1,0:T(8,128)(2,1)S(1)}, u32[]{:S(2)}, u32[]{:S(2)}) collective-permute-start(bf16[128,512]{1,0:T(8,128)(2,1)S(1)} %bitcast.40), channel_id=1, source_target_pairs={{0,4},{2,6},{4,0},{6,2},{1,5},{3,7},{5,1},{7,3},{8,12},{10,14},{12... | collective-permute-start | bytes 393224 | tf_op jit(solution)/shard_map/gather_negatives/ppermute | solution.py:19
  23.7 2.6 %collective-permute-start = (bf16[128,512]{1,0:T(8,128)(2,1)S(1)}, bf16[128,512]{1,0:T(8,128)(2,1)S(1)}, u32[]{:S(2)}, u32[]{:S(2)}) collective-permute-start(bf16[128,512]{1,0:T(8,128)(2,1)S(1)} %bitcast.42), channel_id=1, source_target_pairs={{0,2},{2,0},{4,6},{6,4},{1,3},{3,1},{5,7},{7,5},{8,10},{10,8},{12,... | collective-permute-start | bytes 393224 | tf_op jit(solution)/shard_map/gather_negatives/ppermute | solution.py:19
  26.2 2.9 %collective-permute-done.2 = bf16[128,512]{1,0:T(8,128)(2,1)S(1)} collective-permute-done((bf16[128,512]{1,0:T(8,128)(2,1)S(1)}, bf16[128,512]{1,0:T(8,128)(2,1)S(1)}, u32[]{:S(2)}, u32[]{:S(2)}) %collective-permute-start.2) | collective-permute-done | bytes 131104 | tf_op jit(solution)/shard_map/gather_negatives/ppermute | solution.py:19
  29.1 1.7 %collective-permute-done.1 = bf16[128,512]{1,0:T(8,128)(2,1)S(1)} collective-permute-done((bf16[128,512]{1,0:T(8,128)(2,1)S(1)}, bf16[128,512]{1,0:T(8,128)(2,1)S(1)}, u32[]{:S(2)}, u32[]{:S(2)}) %collective-permute-start.1) | collective-permute-done | bytes 131104 | tf_op jit(solution)/shard_map/gather_negatives/ppermute | solution.py:19
  31.0 10.4 %all-to-all-start.1 = ((bf16[64,16,512]{2,1,0:T(8,128)(2,1)}), bf16[64,16,512]{2,1,0:T(8,128)(2,1)S(1)}, u32[]{:S(2)}, u32[]{:S(2)}) async-start(bf16[64,16,512]{2,1,0:T(8,128)(2,1)} %bitcast.9), calls=%async_computation.1 | async-start | bytes 2097152 | tf_op jit(solution)/shard_map/send_tails/all_to_all | solution.py:354
  42.1 0.8 copy-done.6
  42.9 1.0 copy-done.3
  43.9 1.0 copy-done.5
  45.0 1.0 copy-done.7
  46.0 2.4 %weights.1 = (bf16[512,512]{1,0:T(8,128)(2,1)S(1)}, f32[512,1]{1,0:T(8,128)S(1)}, f32[512,512]{1,0:T(8,128)S(1)}, bf16[512,512]{1,0:T(8,128)(2,1)}) custom-call(s32[1,1]{1,0:T(1,128)S(6)} %copy.19.count_ref, bf16[512,512]{1,0:T(8,128)(2,1)S(1)} %copy-done.5, bf16[512,512]{1,0:T(8,128)(2,1)S(1)} %copy-done.3, bf16[512,512]{1,0:T(8,128)(2,1)S(1)} %pad_maximum_fusion.near_ref, ...), custom_call_target="tpu_custom_call" | custom-call | tf_op jit(solution)/shard_map/weights/weights/pallas_call | solution.py:138
  50.2 1.1 collective-permute-done.4
  51.3 1.2 fusion.18
  52.6 2.2 %collective-permute-start.7 = (bf16[8,16,512]{2,1,0:T(8,128)(2,1)S(1)}, bf16[8,16,512]{2,1,0:T(8,128)(2,1)S(1)}, u32[]{:S(2)}, u32[]{:S(2)}) collective-permute-start(bf16[8,16,512]{2,1,0:T(8,128)(2,1)S(1)} %bitcast.46), channel_id=1, source_target_pairs={{0,4},{2,6},{4,0},{6,2},{1,5},{3,7},{5,1},{7,3},{8,12},{10,14},{12... | collective-permute-start | bytes 393224 | tf_op jit(solution)/shard_map/neg_sum/ppermute | solution.py:19
  54.8 1.5 %collective-permute-start.5 = (bf16[8,16,512]{2,1,0:T(8,128)(2,1)S(1)}, bf16[8,16,512]{2,1,0:T(8,128)(2,1)S(1)}, u32[]{:S(2)}, u32[]{:S(2)}) collective-permute-start(bf16[8,16,512]{2,1,0:T(8,128)(2,1)S(1)} %bitcast.45), channel_id=1, source_target_pairs={{0,2},{2,0},{4,6},{6,4},{1,3},{3,1},{5,7},{7,5},{8,10},{10,8},{12,... | collective-permute-start | bytes 393224 | tf_op jit(solution)/shard_map/neg_sum/ppermute | solution.py:19
  56.8 1.5 %convolution_convert_fusion.both_ref = bf16[1024,256]{1,0:T(8,128)(2,1)S(1)} fusion(bf16[512,512]{1,0:T(8,128)(2,1)} %collective-permute-done.8, bf16[512,512]{1,0:T(8,128)(2,1)S(1)} %copy-done.14, s32[256]{0:T(256)S(1)} %get-tuple-element.65, s32[256]{0:T(256)S(1)} %get-tuple-element.66, s32[]{:T(128)S(6)} %mul.11, s32[256]{0:T(256)S(1)} %get-tuple-element.64, ...), kind=kOutput, calls=%fused_computation | convolution fusion | flops 271581184 | bytes 1577476 | tf_op jit(solution)/shard_map/rel_heads/dot_general | solution.py:360
  58.4 2.0 %pack_heads.1.have_ref = bf16[64,80,128]{2,1,0:T(8,128)(2,1)S(1)} custom-call(bf16[512,512]{1,0:T(8,128)(2,1)S(1)} %get-tuple-element.36.dquery_ref, s32[512,1]{1,0:T(8,128)S(1)} %get-tuple-element.37.rel_ref, bf16[4,512,512]{2,1,0:T(8,128)(2,1)S(1)} %copy-done.2, s32[1,512]{1,0:T(1,128)S(1)} %get-tuple-element.38.slots_ref, ...), custom_call_target="tpu_custom_call" | custom-call | tf_op jit(solution)/shard_map/pack_heads/pack_heads/pallas_call | solution.py:192
  60.4 1.0 copy-done
  61.5 1.7 %relation_terms.1 = (bf16[2,256,512]{2,1,0:T(8,128)(2,1)S(1)}, f32[2,256,512]{2,1,0:T(8,128)S(1)}) custom-call(s32[1,1]{1,0:T(1,128)} %bitcast.10.inner_ref, bf16[1024,256]{1,0:T(8,128)(2,1)S(1)} %convolution_convert_fusion.both_ref, s32[512,1]{1,0:T(8,128)S(1)} %get-tuple-element.37.rel_ref, s32[1,512]{1,0:T(1,128)S(1)} %bitcast.32, ...), custom_call_target="tpu_custom_call" | custom-call | tf_op jit(solution)/shard_map/rel_sum/relation_terms/pallas_call | solution.py:250
  64.0 1.9 %collective-permute-done.5 = bf16[8,16,512]{2,1,0:T(8,128)(2,1)S(1)} collective-permute-done((bf16[8,16,512]{2,1,0:T(8,128)(2,1)S(1)}, bf16[8,16,512]{2,1,0:T(8,128)(2,1)S(1)}, u32[]{:S(2)}, u32[]{:S(2)}) %collective-permute-start.5) | collective-permute-done | bytes 131104 | tf_op jit(solution)/shard_map/neg_sum/ppermute | solution.py:19
  65.9 1.8 %collective-permute-done.6 = bf16[8,16,512]{2,1,0:T(8,128)(2,1)S(1)} collective-permute-done((bf16[8,16,512]{2,1,0:T(8,128)(2,1)S(1)}, bf16[8,16,512]{2,1,0:T(8,128)(2,1)S(1)}, u32[]{:S(2)}, u32[]{:S(2)}) %collective-permute-start.6) | collective-permute-done | bytes 131104 | tf_op jit(solution)/shard_map/neg_sum/ppermute | solution.py:19
  67.8 2.4 %all-to-all-done.1 = bf16[64,16,512]{2,1,0:T(8,128)(2,1)S(1)} async-done(((bf16[64,16,512]{2,1,0:T(8,128)(2,1)}), bf16[64,16,512]{2,1,0:T(8,128)(2,1)S(1)}, u32[]{:S(2)}, u32[]{:S(2)}) %all-to-all-start.1) | async-done | bytes 1048608 | tf_op jit(solution)/shard_map/send_tails/all_to_all | solution.py:354
  70.2 1.6 %collective-permute-start.11 = (bf16[2,256,512]{2,1,0:T(8,128)(2,1)}, bf16[2,256,512]{2,1,0:T(8,128)(2,1)}, u32[]{:S(2)}, u32[]{:S(2)}) collective-permute-start(bf16[2,256,512]{2,1,0:T(8,128)(2,1)} %copy-done.15), channel_id=1, source_target_pairs={{0,64},{64,0},{128,192},{192,128},{1,65},{65,1},{129,193},{193,129... | collective-permute-start | bytes 1572872 | tf_op jit(solution)/shard_map/rel_halves/ppermute | solution.py:19
  71.8 12.5 %all_to_all.25.terms_ref = bf16[8,16,512]{2,1,0:T(8,128)(2,1)} all-to-all(bf16[8,16,512]{2,1,0:T(8,128)(2,1)S(1)} %add_convert_fusion), channel_id=1, replica_groups=mesh['y'=4,'z'=8,'x'=4,'c'=2] {'z'}, dimensions={0} | all-to-all | bytes 262144 | tf_op jit(solution)/shard_map/neg_exchange/all_to_all | solution.py:378
  84.3 2.0 %pack_negs.1 = bf16[64,80,128]{2,1,0:T(8,128)(2,1)} custom-call(bf16[8,16,512]{2,1,0:T(8,128)(2,1)} %all_to_all.25.terms_ref, s32[1,16]{1,0:T(1,128)} %copy-done.12, bf16[64,80,128]{2,1,0:T(8,128)(2,1)} %copy-done), custom_call_target="tpu_custom_call", output_to_operand_aliasing={{}: (2, {})} | custom-call | tf_op jit(solution)/shard_map/send_heads/pack_negs/pallas_call | solution.py:214
  86.3 6.4 %all-to-all-start.3 = ((bf16[64,80,128]{2,1,0:T(8,128)(2,1)}), bf16[64,80,128]{2,1,0:T(8,128)(2,1)S(1)}, u32[]{:S(2)}, u32[]{:S(2)}) async-start(bf16[64,80,128]{2,1,0:T(8,128)(2,1)} %pack_negs.1), calls=%async_computation.3 | async-start | bytes 2621440 | tf_op jit(solution)/shard_map/send_heads/all_to_all | solution.py:383
  92.6 1.2 convert_add_fusion
  93.9 1.0 copy-done.21
  94.9 3.1 %collective-permute-start.12 = (bf16[256,512]{1,0:T(8,128)(2,1)S(1)}, bf16[256,512]{1,0:T(8,128)(2,1)S(1)}, u32[]{:S(2)}, u32[]{:S(2)}) collective-permute-start(bf16[256,512]{1,0:T(8,128)(2,1)S(1)} %fusion.3), channel_id=1, source_target_pairs={{0,192},{64,128},{128,64},{192,0},{1,193},{65,129},{129,65},{193,1... | collective-permute-start | bytes 786440 | tf_op jit(solution)/shard_map/rel_column/ppermute | solution.py:19
  98.0 6.6 %collective-permute-done.12 = bf16[256,512]{1,0:T(8,128)(2,1)S(1)} collective-permute-done((bf16[256,512]{1,0:T(8,128)(2,1)S(1)}, bf16[256,512]{1,0:T(8,128)(2,1)S(1)}, u32[]{:S(2)}, u32[]{:S(2)}) %collective-permute-start.12) | collective-permute-done | bytes 262176 | tf_op jit(solution)/shard_map/rel_column/ppermute | solution.py:19
  104.6 1.3 bitcast_add_fusion
  106.4 2.6 %collective-permute-start.15 = (f32[8,8,512]{2,1,0:T(8,128)S(1)}, f32[8,8,512]{2,1,0:T(8,128)S(1)}, u32[]{:S(2)}, u32[]{:S(2)}) collective-permute-start(f32[8,8,512]{2,1,0:T(8,128)S(1)} %get-tuple-element.57), channel_id=1, source_target_pairs={{0,4},{2,6},{4,0},{6,2},{1,5},{3,7},{5,1},{7,3},{8,12},{10,14},{12... | collective-permute-start | bytes 393224 | tf_op jit(solution)/shard_map/rel_column/ppermute | solution.py:19
  109.6 4.4 %collective-permute-done.13 = f32[8,8,512]{2,1,0:T(8,128)S(1)} collective-permute-done((f32[8,8,512]{2,1,0:T(8,128)S(1)}, f32[8,8,512]{2,1,0:T(8,128)S(1)}, u32[]{:S(2)}, u32[]{:S(2)}) %collective-permute-start.13) | collective-permute-done | bytes 131104 | tf_op jit(solution)/shard_map/rel_column/ppermute | solution.py:19
  114.0 5.6 %collective-permute-done.15 = f32[8,8,512]{2,1,0:T(8,128)S(1)} collective-permute-done((f32[8,8,512]{2,1,0:T(8,128)S(1)}, f32[8,8,512]{2,1,0:T(8,128)S(1)}, u32[]{:S(2)}, u32[]{:S(2)}) %collective-permute-start.15) | collective-permute-done | bytes 131104 | tf_op jit(solution)/shard_map/rel_column/ppermute | solution.py:19
  119.6 1.8 %collective-permute-done.14 = f32[8,8,512]{2,1,0:T(8,128)} collective-permute-done((f32[8,8,512]{2,1,0:T(8,128)S(1)}, f32[8,8,512]{2,1,0:T(8,128)}, u32[]{:S(2)}, u32[]{:S(2)}) %collective-permute-start.14) | collective-permute-done | bytes 131104 | tf_op jit(solution)/shard_map/rel_column/ppermute | solution.py:19
  121.4 1.6 %fusion.13 = f32[8,8,512]{2,1,0:T(8,128)} fusion(f32[8,8,512]{2,1,0:T(8,128)S(1)} %collective-permute-done.15, f32[8,8,512]{2,1,0:T(8,128)} %collective-permute-done.14, f32[8,8,512]{2,1,0:T(8,128)S(1)} %collective-permute-done.13, f32[8,4,8,512]{3,2,1,0:T(8,128)S(1)} %bitcast.38, s32[]{:T(128)S(6)} %select_n.47), kind=kLoop, calls=%fused_computation.22 | loop fusion | flops 98304 | bytes 655364 | tf_op jit(solution)/shard_map/rel_column/add | solution.py:33
  123.0 4.0 %all-to-all-done.3.got_ref = bf16[64,80,128]{2,1,0:T(8,128)(2,1)S(1)} async-done(((bf16[64,80,128]{2,1,0:T(8,128)(2,1)}), bf16[64,80,128]{2,1,0:T(8,128)(2,1)S(1)}, u32[]{:S(2)}, u32[]{:S(2)}) %all-to-all-start.3) | async-done | bytes 1310752 | tf_op jit(solution)/shard_map/send_heads/all_to_all | solution.py:383
  127.0 3.4 %all-to-all-start.4 = ((f32[8,8,512]{2,1,0:T(8,128)}), f32[8,8,512]{2,1,0:T(8,128)S(1)}, u32[]{:S(2)}, u32[]{:S(2)}) async-start(f32[8,8,512]{2,1,0:T(8,128)} %fusion.13), calls=%async_computation.4 | async-start | bytes 262144 | tf_op jit(solution)/shard_map/rel_end/all_to_all | solution.py:388
  130.4 7.7 %combine.1 = f32[2048,512]{1,0:T(8,128)} custom-call(bf16[1024,512]{1,0:T(8,128)(2,1)S(1)} %bitcast.31, bf16[64,80,128]{2,1,0:T(8,128)(2,1)S(1)} %all-to-all-done.3.got_ref), custom_call_target="tpu_custom_call" | custom-call | flops 8000000000 | bytes 8388608 | tf_op jit(solution)/shard_map/combine/combine/pallas_call | solution.py:313
  138.2 1.3 all-to-all-done.4
  (64 shorter events, 7.9 us)
Async XLA Ops:
  2.0 19.5 %all-to-all-start = ((bf16[8,16,512]{2,1,0:T(8,128)(2,1)}), bf16[8,16,512]{2,1,0:T(8,128)(2,1)S(1)}, u32[]{:S(2)}, u32[]{:S(2)}) async-start(bf16[8,16,512]{2,1,0:T(8,128)(2,1)} %broadcast_in_dim.4), calls=%async_computation | async-start | bytes 262144 | tf_op jit(solution)/shard_map/gather_negatives/all_to_all | solution.py:347
  12.9 1.6 %copy-start.1 = (bf16[4,512,512]{2,1,0:T(8,128)(2,1)S(1)}, bf16[4,512,512]{2,1,0:T(8,128)(2,1)}, u32[]{:S(2)}) copy-start(bf16[4,512,512]{2,1,0:T(8,128)(2,1)} %relations_ref.3) | copy-start | bytes 6291460
  14.5 1.0 copy-start.13
  15.5 0.7 copy-start.18
  16.2 1.3 copy-start.16
  16.2 1.4 copy-start.17
  16.2 1.4 copy-start.20
  17.5 2.3 %copy-start.4 = (bf16[512,512]{1,0:T(8,128)(2,1)}, bf16[512,512]{1,0:T(8,128)(2,1)S(1)}, u32[]{:S(2)}) copy-start(bf16[512,512]{1,0:T(8,128)(2,1)S(1)} %get-tuple-element.28.query_ref) | copy-start | bytes 1572868
  18.6 0.7 copy-start.8
  19.3 0.5 copy-start.12
  21.5 7.6 %collective-permute-start.2 = (bf16[128,512]{1,0:T(8,128)(2,1)S(1)}, bf16[128,512]{1,0:T(8,128)(2,1)S(1)}, u32[]{:S(2)}, u32[]{:S(2)}) collective-permute-start(bf16[128,512]{1,0:T(8,128)(2,1)S(1)} %bitcast.40), channel_id=1, source_target_pairs={{0,4},{2,6},{4,0},{6,2},{1,5},{3,7},{5,1},{7,3},{8,12},{10,14},{12... | collective-permute-start | bytes 393224 | tf_op jit(solution)/shard_map/gather_negatives/ppermute | solution.py:19
  23.7 7.1 %collective-permute-start.1 = (bf16[128,512]{1,0:T(8,128)(2,1)S(1)}, bf16[128,512]{1,0:T(8,128)(2,1)S(1)}, u32[]{:S(2)}, u32[]{:S(2)}) collective-permute-start(bf16[128,512]{1,0:T(8,128)(2,1)S(1)} %bitcast.41), channel_id=1, source_target_pairs={{0,6},{2,4},{4,2},{6,0},{1,7},{3,5},{5,3},{7,1},{8,14},{10,12},{12... | collective-permute-start | bytes 393224 | tf_op jit(solution)/shard_map/gather_negatives/ppermute | solution.py:19
  23.7 7.2 %collective-permute-start = (bf16[128,512]{1,0:T(8,128)(2,1)S(1)}, bf16[128,512]{1,0:T(8,128)(2,1)S(1)}, u32[]{:S(2)}, u32[]{:S(2)}) collective-permute-start(bf16[128,512]{1,0:T(8,128)(2,1)S(1)} %bitcast.42), channel_id=1, source_target_pairs={{0,2},{2,0},{4,6},{6,4},{1,3},{3,1},{5,7},{7,5},{8,10},{10,8},{12,... | collective-permute-start | bytes 393224 | tf_op jit(solution)/shard_map/gather_negatives/ppermute | solution.py:19
  30.9 11.1 %collective-permute-start.3 = (bf16[512,512]{1,0:T(8,128)(2,1)S(1)}, bf16[512,512]{1,0:T(8,128)(2,1)S(1)}, u32[]{:S(2)}, u32[]{:S(2)}) collective-permute-start(bf16[512,512]{1,0:T(8,128)(2,1)S(1)} %pad_maximum_fusion.near_ref), channel_id=1, source_target_pairs={{0,1},{1,0},{2,3},{3,2},{4,5},{5,4},{6,7},{7,6},{8,9},{9,8},{10,11... | collective-permute-start | bytes 1572872 | tf_op jit(solution)/shard_map/gather_negatives/ppermute | solution.py:19
  31.0 18.2 %copy-start.19 = (s32[512]{0:T(512)S(1)}, s32[512]{0:T(512)}, u32[]{:S(2)}) copy-start(s32[512]{0:T(512)} %param.14) | copy-start | bytes 6148
  31.0 39.2 %all-to-all-start.1 = ((bf16[64,16,512]{2,1,0:T(8,128)(2,1)}), bf16[64,16,512]{2,1,0:T(8,128)(2,1)S(1)}, u32[]{:S(2)}, u32[]{:S(2)}) async-start(bf16[64,16,512]{2,1,0:T(8,128)(2,1)} %bitcast.9), calls=%async_computation.1 | async-start | bytes 2097152 | tf_op jit(solution)/shard_map/send_tails/all_to_all | solution.py:354
  42.0 0.8 copy-start.6
  42.9 1.0 copy-start.3
  43.9 1.0 copy-start.5
  44.9 1.0 copy-start.7
  48.4 0.7 copy-start.10
  49.0 7.8 %copy-start.14 = (bf16[512,512]{1,0:T(8,128)(2,1)S(1)}, bf16[512,512]{1,0:T(8,128)(2,1)}, u32[]{:S(2)}) copy-start(bf16[512,512]{1,0:T(8,128)(2,1)} %heads_ref.1) | copy-start | bytes 1572868
  49.1 2.3 %collective-permute-start.4 = (bf16[512,512]{1,0:T(8,128)(2,1)}, bf16[512,512]{1,0:T(8,128)(2,1)}, u32[]{:S(2)}, u32[]{:S(2)}) collective-permute-start(bf16[512,512]{1,0:T(8,128)(2,1)} %get-tuple-element.34), channel_id=1, source_target_pairs={{0,1},{1,0},{2,3},{3,2},{4,5},{5,4},{6,7},{7,6},{8,9},{9,8},{10,11... | collective-permute-start | bytes 1572872 | tf_op jit(solution)/shard_map/neg_sum/ppermute | solution.py:19
  49.2 12.3 %collective-permute-start.9 = (s32[512]{0:T(512)S(1)}, s32[512]{0:T(512)S(1)}, u32[]{:S(2)}, u32[]{:S(2)}) collective-permute-start(s32[512]{0:T(512)S(1)} %copy-done.19), channel_id=1, source_target_pairs={{0,1},{1,0},{2,3},{3,2},{4,5},{5,4},{6,7},{7,6},{8,9},{9,8},{10,11... | collective-permute-start | bytes 6152 | tf_op jit(solution)/shard_map/rel_heads/ppermute | solution.py:19
  49.6 6.7 %collective-permute-start.8 = (bf16[512,512]{1,0:T(8,128)(2,1)}, bf16[512,512]{1,0:T(8,128)(2,1)}, u32[]{:S(2)}, u32[]{:S(2)}) collective-permute-start(bf16[512,512]{1,0:T(8,128)(2,1)} %heads_ref.1), channel_id=1, source_target_pairs={{0,1},{1,0},{2,3},{3,2},{4,5},{5,4},{6,7},{7,6},{8,9},{9,8},{10,11... | collective-permute-start | bytes 1572872 | tf_op jit(solution)/shard_map/rel_heads/ppermute | solution.py:19
  49.7 11.7 %collective-permute-start.10 = (bf16[512,512]{1,0:T(8,128)(2,1)S(1)}, bf16[512,512]{1,0:T(8,128)(2,1)S(1)}, u32[]{:S(2)}, u32[]{:S(2)}) collective-permute-start(bf16[512,512]{1,0:T(8,128)(2,1)S(1)} %get-tuple-element.36.dquery_ref), channel_id=1, source_target_pairs={{0,1},{1,0},{2,3},{3,2},{4,5},{5,4},{6,7},{7,6},{8,9},{9,8},{10,11... | collective-permute-start | bytes 1572872 | tf_op jit(solution)/shard_map/rel_sum/ppermute | solution.py:19
  52.5 5.8 %copy-start.2 = (bf16[4,512,512]{2,1,0:T(8,128)(2,1)S(1)}, bf16[4,512,512]{2,1,0:T(8,128)(2,1)}, u32[]{:S(2)}) copy-start(bf16[4,512,512]{2,1,0:T(8,128)(2,1)} %relations_ref.3) | copy-start | bytes 6291460
  52.6 5.8 %copy-start.9 = (s32[512,1]{1,0:T(8,128)S(1)}, s32[512,1]{1,0:T(8,128)}, u32[]{:S(2)}) copy-start(s32[512,1]{1,0:T(8,128)} %copy-done.8) | copy-start | bytes 6148
  52.6 5.8 %copy-start.11 = (f32[512,1]{1,0:T(8,128)S(1)}, f32[512,1]{1,0:T(8,128)}, u32[]{:S(2)}) copy-start(f32[512,1]{1,0:T(8,128)} %copy-done.10) | copy-start | bytes 6148
  52.6 11.4 %collective-permute-start.7 = (bf16[8,16,512]{2,1,0:T(8,128)(2,1)S(1)}, bf16[8,16,512]{2,1,0:T(8,128)(2,1)S(1)}, u32[]{:S(2)}, u32[]{:S(2)}) collective-permute-start(bf16[8,16,512]{2,1,0:T(8,128)(2,1)S(1)} %bitcast.46), channel_id=1, source_target_pairs={{0,4},{2,6},{4,0},{6,2},{1,5},{3,7},{5,1},{7,3},{8,12},{10,14},{12... | collective-permute-start | bytes 393224 | tf_op jit(solution)/shard_map/neg_sum/ppermute | solution.py:19
  54.8 11.1 %collective-permute-start.5 = (bf16[8,16,512]{2,1,0:T(8,128)(2,1)S(1)}, bf16[8,16,512]{2,1,0:T(8,128)(2,1)S(1)}, u32[]{:S(2)}, u32[]{:S(2)}) collective-permute-start(bf16[8,16,512]{2,1,0:T(8,128)(2,1)S(1)} %bitcast.45), channel_id=1, source_target_pairs={{0,2},{2,0},{4,6},{6,4},{1,3},{3,1},{5,7},{7,5},{8,10},{10,8},{12,... | collective-permute-start | bytes 393224 | tf_op jit(solution)/shard_map/neg_sum/ppermute | solution.py:19
  56.2 11.5 %collective-permute-start.6 = (bf16[8,16,512]{2,1,0:T(8,128)(2,1)S(1)}, bf16[8,16,512]{2,1,0:T(8,128)(2,1)S(1)}, u32[]{:S(2)}, u32[]{:S(2)}) collective-permute-start(bf16[8,16,512]{2,1,0:T(8,128)(2,1)S(1)} %bitcast.44), channel_id=1, source_target_pairs={{0,6},{2,4},{4,2},{6,0},{1,7},{3,5},{5,3},{7,1},{8,14},{10,12},{12... | collective-permute-start | bytes 393224 | tf_op jit(solution)/shard_map/neg_sum/ppermute | solution.py:19
  60.4 1.1 copy-start
  63.2 0.8 copy-start.15
  70.2 14.1 %collective-permute-start.11 = (bf16[2,256,512]{2,1,0:T(8,128)(2,1)}, bf16[2,256,512]{2,1,0:T(8,128)(2,1)}, u32[]{:S(2)}, u32[]{:S(2)}) collective-permute-start(bf16[2,256,512]{2,1,0:T(8,128)(2,1)} %copy-done.15), channel_id=1, source_target_pairs={{0,64},{64,0},{128,192},{192,128},{1,65},{65,1},{129,193},{193,129... | collective-permute-start | bytes 1572872 | tf_op jit(solution)/shard_map/rel_halves/ppermute | solution.py:19
  86.3 40.8 %all-to-all-start.3 = ((bf16[64,80,128]{2,1,0:T(8,128)(2,1)}), bf16[64,80,128]{2,1,0:T(8,128)(2,1)S(1)}, u32[]{:S(2)}, u32[]{:S(2)}) async-start(bf16[64,80,128]{2,1,0:T(8,128)(2,1)} %pack_negs.1), calls=%async_computation.3 | async-start | bytes 2621440 | tf_op jit(solution)/shard_map/send_heads/all_to_all | solution.py:383
  93.9 1.0 copy-start.21
  94.9 9.7 %collective-permute-start.12 = (bf16[256,512]{1,0:T(8,128)(2,1)S(1)}, bf16[256,512]{1,0:T(8,128)(2,1)S(1)}, u32[]{:S(2)}, u32[]{:S(2)}) collective-permute-start(bf16[256,512]{1,0:T(8,128)(2,1)S(1)} %fusion.3), channel_id=1, source_target_pairs={{0,192},{64,128},{128,64},{192,0},{1,193},{65,129},{129,65},{193,1... | collective-permute-start | bytes 786440 | tf_op jit(solution)/shard_map/rel_column/ppermute | solution.py:19
  106.0 8.0 %collective-permute-start.13 = (f32[8,8,512]{2,1,0:T(8,128)S(1)}, f32[8,8,512]{2,1,0:T(8,128)S(1)}, u32[]{:S(2)}, u32[]{:S(2)}) collective-permute-start(f32[8,8,512]{2,1,0:T(8,128)S(1)} %get-tuple-element.56), channel_id=1, source_target_pairs={{0,2},{2,0},{4,6},{6,4},{1,3},{3,1},{5,7},{7,5},{8,10},{10,8},{12,... | collective-permute-start | bytes 393224 | tf_op jit(solution)/shard_map/rel_column/ppermute | solution.py:19
  106.4 13.2 %collective-permute-start.15 = (f32[8,8,512]{2,1,0:T(8,128)S(1)}, f32[8,8,512]{2,1,0:T(8,128)S(1)}, u32[]{:S(2)}, u32[]{:S(2)}) collective-permute-start(f32[8,8,512]{2,1,0:T(8,128)S(1)} %get-tuple-element.57), channel_id=1, source_target_pairs={{0,4},{2,6},{4,0},{6,2},{1,5},{3,7},{5,1},{7,3},{8,12},{10,14},{12... | collective-permute-start | bytes 393224 | tf_op jit(solution)/shard_map/rel_column/ppermute | solution.py:19
  109.0 12.4 %collective-permute-start.14 = (f32[8,8,512]{2,1,0:T(8,128)S(1)}, f32[8,8,512]{2,1,0:T(8,128)}, u32[]{:S(2)}, u32[]{:S(2)}) collective-permute-start(f32[8,8,512]{2,1,0:T(8,128)S(1)} %get-tuple-element.58), channel_id=1, source_target_pairs={{0,6},{2,4},{4,2},{6,0},{1,7},{3,5},{5,3},{7,1},{8,14},{10,12},{12... | collective-permute-start | bytes 393224 | tf_op jit(solution)/shard_map/rel_column/ppermute | solution.py:19
  127.0 12.4 %all-to-all-start.4 = ((f32[8,8,512]{2,1,0:T(8,128)}), f32[8,8,512]{2,1,0:T(8,128)S(1)}, u32[]{:S(2)}, u32[]{:S(2)}) async-start(f32[8,8,512]{2,1,0:T(8,128)} %fusion.13), calls=%async_computation.4 | async-start | bytes 262144 | tf_op jit(solution)/shard_map/rel_end/all_to_all | solution.py:388

commit v4 on v3

--- a/solution.py
+++ b/solution.py
@@ -346,7 +346,6 @@
         wide = jnp.broadcast_to(neg_vecs[None], (SIZES["z"],) + neg_vecs.shape)
         column = lax.all_to_all(wide, "z", 0, 0, tiled=True).reshape(-1, width)
         tail_rows = pack_tails(query, slots[1], owners)
-        column, tail_rows = lax.optimization_barrier((column, tail_rows))
         near = jnp.concatenate([column] + [swap(column, "x", flip) for flip in (1, 3, 2)], axis=0)
         near, tail_rows = lax.optimization_barrier((near, tail_rows))
         far = swap(near, "c", 1)

time: 142 us -> 138 us (0.972)
  waiting for transfers between devices: 35.6 us -> 33.1 us
    ppermute x16, waiting for transfers between devices: 27.9 us -> 23.3 us  [swap(): return lax.ppermute(a, axis, [(i, i ^ flip) for i in range(SIZES[axis])])]
    all_to_all x1, waiting for transfers between devices: 0.01 us -> 2.04 us  [on_device(): column = lax.all_to_all(wide, 'z', 0, 0, tiled=True).reshape(-1, width)]
  transfers between devices with their start and end apart: 20 -> 20, of which waited for: 13 -> 11; matrix products, arithmetic and copies ran while one was open for 7% -> 7% of each run, Pallas kernels for 13% -> 13%
where the time goes in v4:
time: 138 us; the launch traced here: 136 us
  starting transfers between devices  45.6 us (33%)
  waiting for transfers between devices  33.1 us (24%)
  Pallas kernels  19.8 us (14%)
  local copies, waits for them, and re-layouts  15.9 us (12%)
  blocking collectives  12.5 us (9%)
  other arithmetic  6.15 us (4%)
  between operations  1.61 us (1%)
  matrix products  1.53 us (1%)
    ppermute x16, waiting for transfers between devices, swap(): return lax.ppermute(a, axis, [(i, i ^ flip) for i in range(SIZES[axis])])  23.3 us
    ppermute x16, starting transfers between devices, swap(): return lax.ppermute(a, axis, [(i, i ^ flip) for i in range(SIZES[axis])])  18.3 us
    unnamed x47, local copies, waits for them, and re-layouts  14.4 us
    all_to_all x1, blocking collectives, on_device(): terms = lax.all_to_all(own, 'z', 0, 0, tiled=True)  12.5 us
    all_to_all x1, starting transfers between devices, on_device(): lax.all_to_all(tail_rows.reshape(owners, CAP, width), SHARD, 0, 0, tiled=...  9.09 us
    all_to_all x1, starting transfers between devices, on_device(): column = lax.all_to_all(wide, 'z', 0, 0, tiled=True).reshape(-1, width)  8.47 us
    pallas_call x1, Pallas kernels, combine(): pl.pallas_call(combine_kernel, grid=(CLS_DEV // tile,), in_specs=[pl.Bloc...  7.73 us
    all_to_all x1, starting transfers between devices, on_device(): lax.all_to_all(pack_negs(terms, slots[2], heads), SHARD, 0, 0, tiled=True)  6.37 us
  transfers between devices with their start and end apart: 20, of which 11 were waited for; matrix products, arithmetic and copies ran while one was open for 7% of the time, Pallas kernels for 13%

profile of v4, /device:TPU:2, one launch (start us, length us, event | category | flops | bytes accessed | tf_op | source)
XLA Modules:
  0.0 136.2 jit_solution(12790817855641279086)
XLA Ops:
  0.6 1.4 %broadcast_in_dim.4 = bf16[8,16,512]{2,1,0:T(8,128)(2,1)} broadcast(bf16[16,512]{1,0:T(8,128)(2,1)} %param.19), dimensions={1,2} | broadcast | bytes 147456 | tf_op jit(solution)/shard_map/gather_negatives/broadcast_in_dim | solution.py:346
  2.0 8.5 %all-to-all-start = ((bf16[8,16,512]{2,1,0:T(8,128)(2,1)}), bf16[8,16,512]{2,1,0:T(8,128)(2,1)S(1)}, u32[]{:S(2)}, u32[]{:S(2)}) async-start(bf16[8,16,512]{2,1,0:T(8,128)(2,1)} %broadcast_in_dim.4), calls=%async_computation | async-start | bytes 262144 | tf_op jit(solution)/shard_map/gather_negatives/all_to_all | solution.py:347
  11.2 0.8 copy.15.ho_ref
  12.0 0.8 copy.16.to_ref
  12.9 1.6 %copy-done.1 = bf16[4,512,512]{2,1,0:T(8,128)(2,1)S(1)} copy-done((bf16[4,512,512]{2,1,0:T(8,128)(2,1)S(1)}, bf16[4,512,512]{2,1,0:T(8,128)(2,1)}, u32[]{:S(2)}) %copy-start.1) | copy-done | bytes 2097176
  14.5 1.0 copy-done.13
  16.2 1.3 query.1
  17.5 2.0 %all-to-all-done = bf16[8,16,512]{2,1,0:T(8,128)(2,1)S(1)} async-done(((bf16[8,16,512]{2,1,0:T(8,128)(2,1)}), bf16[8,16,512]{2,1,0:T(8,128)(2,1)S(1)}, u32[]{:S(2)}, u32[]{:S(2)}) %all-to-all-start) | async-done | bytes 131104 | tf_op jit(solution)/shard_map/gather_negatives/all_to_all | solution.py:347
  19.6 2.1 %collective-permute-start.2 = (bf16[128,512]{1,0:T(8,128)(2,1)S(1)}, bf16[128,512]{1,0:T(8,128)(2,1)S(1)}, u32[]{:S(2)}, u32[]{:S(2)}) collective-permute-start(bf16[128,512]{1,0:T(8,128)(2,1)S(1)} %bitcast.40), channel_id=1, source_target_pairs={{0,4},{2,6},{4,0},{6,2},{1,5},{3,7},{5,1},{7,3},{8,12},{10,14},{12... | collective-permute-start | bytes 393224 | tf_op jit(solution)/shard_map/gather_negatives/ppermute | solution.py:19
  21.7 2.6 %collective-permute-start = (bf16[128,512]{1,0:T(8,128)(2,1)S(1)}, bf16[128,512]{1,0:T(8,128)(2,1)S(1)}, u32[]{:S(2)}, u32[]{:S(2)}) collective-permute-start(bf16[128,512]{1,0:T(8,128)(2,1)S(1)} %bitcast.42), channel_id=1, source_target_pairs={{0,2},{2,0},{4,6},{6,4},{1,3},{3,1},{5,7},{7,5},{8,10},{10,8},{12,... | collective-permute-start | bytes 393224 | tf_op jit(solution)/shard_map/gather_negatives/ppermute | solution.py:19
  24.3 1.0 slots.1
  26.5 1.7 %pack_tails.1 = bf16[1024,512]{1,0:T(8,128)(2,1)} custom-call(bf16[512,512]{1,0:T(8,128)(2,1)S(1)} %get-tuple-element.26.query_ref, s32[1,512]{1,0:T(1,128)S(1)} %get-tuple-element.27.slots_ref.tail_slots_ref), custom_call_target="tpu_custom_call" | custom-call | flops 1000000000 | bytes 1048576 | tf_op jit(solution)/shard_map/gather_negatives/pack_tails/pallas_call | solution.py:156
  28.4 9.1 %all-to-all-start.1 = ((bf16[64,16,512]{2,1,0:T(8,128)(2,1)}), bf16[64,16,512]{2,1,0:T(8,128)(2,1)S(1)}, u32[]{:S(2)}, u32[]{:S(2)}) async-start(bf16[64,16,512]{2,1,0:T(8,128)(2,1)} %bitcast.9), calls=%async_computation.1 | async-start | bytes 2097152 | tf_op jit(solution)/shard_map/send_tails/all_to_all | solution.py:353
  38.2 0.8 copy-done.6
  39.0 1.0 copy-done.3
  40.0 1.0 copy-done.5
  41.1 1.0 copy-done.7
  42.1 2.4 %weights.1 = (bf16[512,512]{1,0:T(8,128)(2,1)S(1)}, f32[512,1]{1,0:T(8,128)S(1)}, f32[512,512]{1,0:T(8,128)S(1)}, bf16[512,512]{1,0:T(8,128)(2,1)}) custom-call(s32[1,1]{1,0:T(1,128)S(6)} %copy.19.count_ref, bf16[512,512]{1,0:T(8,128)(2,1)S(1)} %copy-done.5, bf16[512,512]{1,0:T(8,128)(2,1)S(1)} %copy-done.3, bf16[512,512]{1,0:T(8,128)(2,1)S(1)} %pad_maximum_fusion.near_ref, ...), custom_call_target="tpu_custom_call" | custom-call | tf_op jit(solution)/shard_map/weights/weights/pallas_call | solution.py:138
  46.3 1.1 collective-permute-done.4
  47.4 1.2 fusion.18
  48.7 2.2 %collective-permute-start.7 = (bf16[8,16,512]{2,1,0:T(8,128)(2,1)S(1)}, bf16[8,16,512]{2,1,0:T(8,128)(2,1)S(1)}, u32[]{:S(2)}, u32[]{:S(2)}) collective-permute-start(bf16[8,16,512]{2,1,0:T(8,128)(2,1)S(1)} %bitcast.46), channel_id=1, source_target_pairs={{0,4},{2,6},{4,0},{6,2},{1,5},{3,7},{5,1},{7,3},{8,12},{10,14},{12... | collective-permute-start | bytes 393224 | tf_op jit(solution)/shard_map/neg_sum/ppermute | solution.py:19
  50.9 1.5 %collective-permute-start.5 = (bf16[8,16,512]{2,1,0:T(8,128)(2,1)S(1)}, bf16[8,16,512]{2,1,0:T(8,128)(2,1)S(1)}, u32[]{:S(2)}, u32[]{:S(2)}) collective-permute-start(bf16[8,16,512]{2,1,0:T(8,128)(2,1)S(1)} %bitcast.45), channel_id=1, source_target_pairs={{0,2},{2,0},{4,6},{6,4},{1,3},{3,1},{5,7},{7,5},{8,10},{10,8},{12,... | collective-permute-start | bytes 393224 | tf_op jit(solution)/shard_map/neg_sum/ppermute | solution.py:19
  52.9 1.5 %convolution_convert_fusion.both_ref = bf16[1024,256]{1,0:T(8,128)(2,1)S(1)} fusion(bf16[512,512]{1,0:T(8,128)(2,1)} %collective-permute-done.8, bf16[512,512]{1,0:T(8,128)(2,1)S(1)} %copy-done.14, s32[256]{0:T(256)S(1)} %get-tuple-element.61, s32[256]{0:T(256)S(1)} %get-tuple-element.62, s32[]{:T(128)S(6)} %mul.11, s32[256]{0:T(256)S(1)} %get-tuple-element.60, ...), kind=kOutput, calls=%fused_computation | convolution fusion | flops 271581184 | bytes 1577476 | tf_op jit(solution)/shard_map/rel_heads/dot_general | solution.py:359
  54.5 2.0 %pack_heads.1.have_ref = bf16[64,80,128]{2,1,0:T(8,128)(2,1)S(1)} custom-call(bf16[512,512]{1,0:T(8,128)(2,1)S(1)} %get-tuple-element.32.dquery_ref, s32[512,1]{1,0:T(8,128)S(1)} %get-tuple-element.33.rel_ref, bf16[4,512,512]{2,1,0:T(8,128)(2,1)S(1)} %copy-done.2, s32[1,512]{1,0:T(1,128)S(1)} %get-tuple-element.34.slots_ref, ...), custom_call_target="tpu_custom_call" | custom-call | tf_op jit(solution)/shard_map/pack_heads/pack_heads/pallas_call | solution.py:192
  56.5 1.0 copy-done
  57.6 1.7 %relation_terms.1 = (bf16[2,256,512]{2,1,0:T(8,128)(2,1)S(1)}, f32[2,256,512]{2,1,0:T(8,128)S(1)}) custom-call(s32[1,1]{1,0:T(1,128)} %bitcast.10.inner_ref, bf16[1024,256]{1,0:T(8,128)(2,1)S(1)} %convolution_convert_fusion.both_ref, s32[512,1]{1,0:T(8,128)S(1)} %get-tuple-element.33.rel_ref, s32[1,512]{1,0:T(1,128)S(1)} %bitcast.32, ...), custom_call_target="tpu_custom_call" | custom-call | tf_op jit(solution)/shard_map/rel_sum/relation_terms/pallas_call | solution.py:250
  59.3 0.8 copy-done.15
  60.1 1.9 %collective-permute-done.5 = bf16[8,16,512]{2,1,0:T(8,128)(2,1)S(1)} collective-permute-done((bf16[8,16,512]{2,1,0:T(8,128)(2,1)S(1)}, bf16[8,16,512]{2,1,0:T(8,128)(2,1)S(1)}, u32[]{:S(2)}, u32[]{:S(2)}) %collective-permute-start.5) | collective-permute-done | bytes 131104 | tf_op jit(solution)/shard_map/neg_sum/ppermute | solution.py:19
  62.0 1.8 %collective-permute-done.6 = bf16[8,16,512]{2,1,0:T(8,128)(2,1)S(1)} collective-permute-done((bf16[8,16,512]{2,1,0:T(8,128)(2,1)S(1)}, bf16[8,16,512]{2,1,0:T(8,128)(2,1)S(1)}, u32[]{:S(2)}, u32[]{:S(2)}) %collective-permute-start.6) | collective-permute-done | bytes 131104 | tf_op jit(solution)/shard_map/neg_sum/ppermute | solution.py:19
  63.9 2.4 %all-to-all-done.1 = bf16[64,16,512]{2,1,0:T(8,128)(2,1)S(1)} async-done(((bf16[64,16,512]{2,1,0:T(8,128)(2,1)}), bf16[64,16,512]{2,1,0:T(8,128)(2,1)S(1)}, u32[]{:S(2)}, u32[]{:S(2)}) %all-to-all-start.1) | async-done | bytes 1048608 | tf_op jit(solution)/shard_map/send_tails/all_to_all | solution.py:353
  66.3 1.6 %collective-permute-start.11 = (bf16[2,256,512]{2,1,0:T(8,128)(2,1)}, bf16[2,256,512]{2,1,0:T(8,128)(2,1)}, u32[]{:S(2)}, u32[]{:S(2)}) collective-permute-start(bf16[2,256,512]{2,1,0:T(8,128)(2,1)} %copy-done.15), channel_id=1, source_target_pairs={{0,64},{64,0},{128,192},{192,128},{1,65},{65,1},{129,193},{193,129... | collective-permute-start | bytes 1572872 | tf_op jit(solution)/shard_map/rel_halves/ppermute | solution.py:19
  67.9 12.5 %all_to_all.25.terms_ref = bf16[8,16,512]{2,1,0:T(8,128)(2,1)} all-to-all(bf16[8,16,512]{2,1,0:T(8,128)(2,1)S(1)} %add_convert_fusion), channel_id=1, replica_groups=mesh['y'=4,'z'=8,'x'=4,'c'=2] {'z'}, dimensions={0} | all-to-all | bytes 262144 | tf_op jit(solution)/shard_map/neg_exchange/all_to_all | solution.py:377
  80.4 2.0 %pack_negs.1 = bf16[64,80,128]{2,1,0:T(8,128)(2,1)} custom-call(bf16[8,16,512]{2,1,0:T(8,128)(2,1)} %all_to_all.25.terms_ref, s32[1,16]{1,0:T(1,128)} %copy-done.12, bf16[64,80,128]{2,1,0:T(8,128)(2,1)} %copy-done), custom_call_target="tpu_custom_call", output_to_operand_aliasing={{}: (2, {})} | custom-call | tf_op jit(solution)/shard_map/send_heads/pack_negs/pallas_call | solution.py:214
  82.4 6.4 %all-to-all-start.3 = ((bf16[64,80,128]{2,1,0:T(8,128)(2,1)}), bf16[64,80,128]{2,1,0:T(8,128)(2,1)S(1)}, u32[]{:S(2)}, u32[]{:S(2)}) async-start(bf16[64,80,128]{2,1,0:T(8,128)(2,1)} %pack_negs.1), calls=%async_computation.3 | async-start | bytes 2621440 | tf_op jit(solution)/shard_map/send_heads/all_to_all | solution.py:382
  88.8 1.2 convert_add_fusion
  90.0 1.0 copy-done.21
  91.0 3.1 %collective-permute-start.12 = (bf16[256,512]{1,0:T(8,128)(2,1)S(1)}, bf16[256,512]{1,0:T(8,128)(2,1)S(1)}, u32[]{:S(2)}, u32[]{:S(2)}) collective-permute-start(bf16[256,512]{1,0:T(8,128)(2,1)S(1)} %fusion.3), channel_id=1, source_target_pairs={{0,192},{64,128},{128,64},{192,0},{1,193},{65,129},{129,65},{193,1... | collective-permute-start | bytes 786440 | tf_op jit(solution)/shard_map/rel_column/ppermute | solution.py:19
  94.1 6.6 %collective-permute-done.12 = bf16[256,512]{1,0:T(8,128)(2,1)S(1)} collective-permute-done((bf16[256,512]{1,0:T(8,128)(2,1)S(1)}, bf16[256,512]{1,0:T(8,128)(2,1)S(1)}, u32[]{:S(2)}, u32[]{:S(2)}) %collective-permute-start.12) | collective-permute-done | bytes 262176 | tf_op jit(solution)/shard_map/rel_column/ppermute | solution.py:19
  100.7 1.3 bitcast_add_fusion
  102.6 2.6 %collective-permute-start.15 = (f32[8,8,512]{2,1,0:T(8,128)S(1)}, f32[8,8,512]{2,1,0:T(8,128)S(1)}, u32[]{:S(2)}, u32[]{:S(2)}) collective-permute-start(f32[8,8,512]{2,1,0:T(8,128)S(1)} %get-tuple-element.53), channel_id=1, source_target_pairs={{0,4},{2,6},{4,0},{6,2},{1,5},{3,7},{5,1},{7,3},{8,12},{10,14},{12... | collective-permute-start | bytes 393224 | tf_op jit(solution)/shard_map/rel_column/ppermute | solution.py:19
  105.7 4.4 %collective-permute-done.13 = f32[8,8,512]{2,1,0:T(8,128)S(1)} collective-permute-done((f32[8,8,512]{2,1,0:T(8,128)S(1)}, f32[8,8,512]{2,1,0:T(8,128)S(1)}, u32[]{:S(2)}, u32[]{:S(2)}) %collective-permute-start.13) | collective-permute-done | bytes 131104 | tf_op jit(solution)/shard_map/rel_column/ppermute | solution.py:19
  110.1 5.6 %collective-permute-done.15 = f32[8,8,512]{2,1,0:T(8,128)S(1)} collective-permute-done((f32[8,8,512]{2,1,0:T(8,128)S(1)}, f32[8,8,512]{2,1,0:T(8,128)S(1)}, u32[]{:S(2)}, u32[]{:S(2)}) %collective-permute-start.15) | collective-permute-done | bytes 131104 | tf_op jit(solution)/shard_map/rel_column/ppermute | solution.py:19
  115.8 1.8 %collective-permute-done.14 = f32[8,8,512]{2,1,0:T(8,128)} collective-permute-done((f32[8,8,512]{2,1,0:T(8,128)S(1)}, f32[8,8,512]{2,1,0:T(8,128)}, u32[]{:S(2)}, u32[]{:S(2)}) %collective-permute-start.14) | collective-permute-done | bytes 131104 | tf_op jit(solution)/shard_map/rel_column/ppermute | solution.py:19
  117.5 1.6 %fusion.13 = f32[8,8,512]{2,1,0:T(8,128)} fusion(f32[8,8,512]{2,1,0:T(8,128)S(1)} %collective-permute-done.15, f32[8,8,512]{2,1,0:T(8,128)} %collective-permute-done.14, f32[8,8,512]{2,1,0:T(8,128)S(1)} %collective-permute-done.13, f32[8,4,8,512]{3,2,1,0:T(8,128)S(1)} %bitcast.38, s32[]{:T(128)S(6)} %select_n.47), kind=kLoop, calls=%fused_computation.22 | loop fusion | flops 98304 | bytes 655364 | tf_op jit(solution)/shard_map/rel_column/add | solution.py:33
  119.1 4.0 %all-to-all-done.3.got_ref = bf16[64,80,128]{2,1,0:T(8,128)(2,1)S(1)} async-done(((bf16[64,80,128]{2,1,0:T(8,128)(2,1)}), bf16[64,80,128]{2,1,0:T(8,128)(2,1)S(1)}, u32[]{:S(2)}, u32[]{:S(2)}) %all-to-all-start.3) | async-done | bytes 1310752 | tf_op jit(solution)/shard_map/send_heads/all_to_all | solution.py:382
  123.2 3.4 %all-to-all-start.4 = ((f32[8,8,512]{2,1,0:T(8,128)}), f32[8,8,512]{2,1,0:T(8,128)S(1)}, u32[]{:S(2)}, u32[]{:S(2)}) async-start(f32[8,8,512]{2,1,0:T(8,128)} %fusion.13), calls=%async_computation.4 | async-start | bytes 262144 | tf_op jit(solution)/shard_map/rel_end/all_to_all | solution.py:387
  126.5 7.7 %combine.1 = f32[2048,512]{1,0:T(8,128)} custom-call(bf16[1024,512]{1,0:T(8,128)(2,1)S(1)} %bitcast.31, bf16[64,80,128]{2,1,0:T(8,128)(2,1)S(1)} %all-to-all-done.3.got_ref), custom_call_target="tpu_custom_call" | custom-call | flops 8000000000 | bytes 8388608 | tf_op jit(solution)/shard_map/combine/combine/pallas_call | solution.py:313
  134.3 1.3 all-to-all-done.4
  (64 shorter events, 7.0 us)
Async XLA Ops:
  2.0 17.6 %all-to-all-start = ((bf16[8,16,512]{2,1,0:T(8,128)(2,1)}), bf16[8,16,512]{2,1,0:T(8,128)(2,1)S(1)}, u32[]{:S(2)}, u32[]{:S(2)}) async-start(bf16[8,16,512]{2,1,0:T(8,128)(2,1)} %broadcast_in_dim.4), calls=%async_computation | async-start | bytes 262144 | tf_op jit(solution)/shard_map/gather_negatives/all_to_all | solution.py:347
  12.9 1.6 %copy-start.1 = (bf16[4,512,512]{2,1,0:T(8,128)(2,1)S(1)}, bf16[4,512,512]{2,1,0:T(8,128)(2,1)}, u32[]{:S(2)}) copy-start(bf16[4,512,512]{2,1,0:T(8,128)(2,1)} %relations_ref.3) | copy-start | bytes 6291460
  14.5 1.0 copy-start.13
  15.5 0.7 copy-start.18
  16.2 8.1 %copy-start.16 = (s32[512]{0:T(512)S(1)}, s32[512]{0:T(512)}, u32[]{:S(2)}) copy-start(s32[512]{0:T(512)} %param.16) | copy-start | bytes 6148
  16.2 8.1 %copy-start.17 = (s32[512]{0:T(512)S(1)}, s32[512]{0:T(512)}, u32[]{:S(2)}) copy-start(s32[512]{0:T(512)} %param.18) | copy-start | bytes 6148
  16.2 8.1 %copy-start.20 = (s32[16]{0:T(128)S(1)}, s32[16]{0:T(128)}, u32[]{:S(2)}) copy-start(s32[16]{0:T(128)} %param.21) | copy-start | bytes 196
  17.5 9.0 %copy-start.4 = (bf16[512,512]{1,0:T(8,128)(2,1)}, bf16[512,512]{1,0:T(8,128)(2,1)S(1)}, u32[]{:S(2)}) copy-start(bf16[512,512]{1,0:T(8,128)(2,1)S(1)} %get-tuple-element.26.query_ref) | copy-start | bytes 1572868
  19.6 8.7 %collective-permute-start.2 = (bf16[128,512]{1,0:T(8,128)(2,1)S(1)}, bf16[128,512]{1,0:T(8,128)(2,1)S(1)}, u32[]{:S(2)}, u32[]{:S(2)}) collective-permute-start(bf16[128,512]{1,0:T(8,128)(2,1)S(1)} %bitcast.40), channel_id=1, source_target_pairs={{0,4},{2,6},{4,0},{6,2},{1,5},{3,7},{5,1},{7,3},{8,12},{10,14},{12... | collective-permute-start | bytes 393224 | tf_op jit(solution)/shard_map/gather_negatives/ppermute | solution.py:19
  21.7 6.5 %collective-permute-start.1 = (bf16[128,512]{1,0:T(8,128)(2,1)S(1)}, bf16[128,512]{1,0:T(8,128)(2,1)S(1)}, u32[]{:S(2)}, u32[]{:S(2)}) collective-permute-start(bf16[128,512]{1,0:T(8,128)(2,1)S(1)} %bitcast.41), channel_id=1, source_target_pairs={{0,6},{2,4},{4,2},{6,0},{1,7},{3,5},{5,3},{7,1},{8,14},{10,12},{12... | collective-permute-start | bytes 393224 | tf_op jit(solution)/shard_map/gather_negatives/ppermute | solution.py:19
  21.7 6.5 %collective-permute-start = (bf16[128,512]{1,0:T(8,128)(2,1)S(1)}, bf16[128,512]{1,0:T(8,128)(2,1)S(1)}, u32[]{:S(2)}, u32[]{:S(2)}) collective-permute-start(bf16[128,512]{1,0:T(8,128)(2,1)S(1)} %bitcast.42), channel_id=1, source_target_pairs={{0,2},{2,0},{4,6},{6,4},{1,3},{3,1},{5,7},{7,5},{8,10},{10,8},{12,... | collective-permute-start | bytes 393224 | tf_op jit(solution)/shard_map/gather_negatives/ppermute | solution.py:19
  25.3 0.7 copy-start.8
  26.0 0.5 copy-start.12
  28.3 9.9 %collective-permute-start.3 = (bf16[512,512]{1,0:T(8,128)(2,1)S(1)}, bf16[512,512]{1,0:T(8,128)(2,1)S(1)}, u32[]{:S(2)}, u32[]{:S(2)}) collective-permute-start(bf16[512,512]{1,0:T(8,128)(2,1)S(1)} %pad_maximum_fusion.near_ref), channel_id=1, source_target_pairs={{0,1},{1,0},{2,3},{3,2},{4,5},{5,4},{6,7},{7,6},{8,9},{9,8},{10,11... | collective-permute-start | bytes 1572872 | tf_op jit(solution)/shard_map/gather_negatives/ppermute | solution.py:19
  28.4 16.9 %copy-start.19 = (s32[512]{0:T(512)S(1)}, s32[512]{0:T(512)}, u32[]{:S(2)}) copy-start(s32[512]{0:T(512)} %param.14) | copy-start | bytes 6148
  28.4 37.9 %all-to-all-start.1 = ((bf16[64,16,512]{2,1,0:T(8,128)(2,1)}), bf16[64,16,512]{2,1,0:T(8,128)(2,1)S(1)}, u32[]{:S(2)}, u32[]{:S(2)}) async-start(bf16[64,16,512]{2,1,0:T(8,128)(2,1)} %bitcast.9), calls=%async_computation.1 | async-start | bytes 2097152 | tf_op jit(solution)/shard_map/send_tails/all_to_all | solution.py:353
  38.2 0.8 copy-start.6
  39.0 1.0 copy-start.3
  40.0 1.0 copy-start.5
  41.1 1.0 copy-start.7
  44.5 0.7 copy-start.10
  45.2 7.8 %copy-start.14 = (bf16[512,512]{1,0:T(8,128)(2,1)S(1)}, bf16[512,512]{1,0:T(8,128)(2,1)}, u32[]{:S(2)}) copy-start(bf16[512,512]{1,0:T(8,128)(2,1)} %heads_ref.1) | copy-start | bytes 1572868
  45.2 2.3 %collective-permute-start.4 = (bf16[512,512]{1,0:T(8,128)(2,1)}, bf16[512,512]{1,0:T(8,128)(2,1)}, u32[]{:S(2)}, u32[]{:S(2)}) collective-permute-start(bf16[512,512]{1,0:T(8,128)(2,1)} %get-tuple-element.30), channel_id=1, source_target_pairs={{0,1},{1,0},{2,3},{3,2},{4,5},{5,4},{6,7},{7,6},{8,9},{9,8},{10,11... | collective-permute-start | bytes 1572872 | tf_op jit(solution)/shard_map/neg_sum/ppermute | solution.py:19
  45.3 12.3 %collective-permute-start.9 = (s32[512]{0:T(512)S(1)}, s32[512]{0:T(512)S(1)}, u32[]{:S(2)}, u32[]{:S(2)}) collective-permute-start(s32[512]{0:T(512)S(1)} %copy-done.19), channel_id=1, source_target_pairs={{0,1},{1,0},{2,3},{3,2},{4,5},{5,4},{6,7},{7,6},{8,9},{9,8},{10,11... | collective-permute-start | bytes 6152 | tf_op jit(solution)/shard_map/rel_heads/ppermute | solution.py:19
  45.7 6.7 %collective-permute-start.8 = (bf16[512,512]{1,0:T(8,128)(2,1)}, bf16[512,512]{1,0:T(8,128)(2,1)}, u32[]{:S(2)}, u32[]{:S(2)}) collective-permute-start(bf16[512,512]{1,0:T(8,128)(2,1)} %heads_ref.1), channel_id=1, source_target_pairs={{0,1},{1,0},{2,3},{3,2},{4,5},{5,4},{6,7},{7,6},{8,9},{9,8},{10,11... | collective-permute-start | bytes 1572872 | tf_op jit(solution)/shard_map/rel_heads/ppermute | solution.py:19
  45.8 11.7 %collective-permute-start.10 = (bf16[512,512]{1,0:T(8,128)(2,1)S(1)}, bf16[512,512]{1,0:T(8,128)(2,1)S(1)}, u32[]{:S(2)}, u32[]{:S(2)}) collective-permute-start(bf16[512,512]{1,0:T(8,128)(2,1)S(1)} %get-tuple-element.32.dquery_ref), channel_id=1, source_target_pairs={{0,1},{1,0},{2,3},{3,2},{4,5},{5,4},{6,7},{7,6},{8,9},{9,8},{10,11... | collective-permute-start | bytes 1572872 | tf_op jit(solution)/shard_map/rel_sum/ppermute | solution.py:19
  48.7 5.8 %copy-start.2 = (bf16[4,512,512]{2,1,0:T(8,128)(2,1)S(1)}, bf16[4,512,512]{2,1,0:T(8,128)(2,1)}, u32[]{:S(2)}) copy-start(bf16[4,512,512]{2,1,0:T(8,128)(2,1)} %relations_ref.3) | copy-start | bytes 6291460
  48.7 5.8 %copy-start.9 = (s32[512,1]{1,0:T(8,128)S(1)}, s32[512,1]{1,0:T(8,128)}, u32[]{:S(2)}) copy-start(s32[512,1]{1,0:T(8,128)} %copy-done.8) | copy-start | bytes 6148
  48.7 5.8 %copy-start.11 = (f32[512,1]{1,0:T(8,128)S(1)}, f32[512,1]{1,0:T(8,128)}, u32[]{:S(2)}) copy-start(f32[512,1]{1,0:T(8,128)} %copy-done.10) | copy-start | bytes 6148
  48.7 11.4 %collective-permute-start.7 = (bf16[8,16,512]{2,1,0:T(8,128)(2,1)S(1)}, bf16[8,16,512]{2,1,0:T(8,128)(2,1)S(1)}, u32[]{:S(2)}, u32[]{:S(2)}) collective-permute-start(bf16[8,16,512]{2,1,0:T(8,128)(2,1)S(1)} %bitcast.46), channel_id=1, source_target_pairs={{0,4},{2,6},{4,0},{6,2},{1,5},{3,7},{5,1},{7,3},{8,12},{10,14},{12... | collective-permute-start | bytes 393224 | tf_op jit(solution)/shard_map/neg_sum/ppermute | solution.py:19
  50.9 11.1 %collective-permute-start.5 = (bf16[8,16,512]{2,1,0:T(8,128)(2,1)S(1)}, bf16[8,16,512]{2,1,0:T(8,128)(2,1)S(1)}, u32[]{:S(2)}, u32[]{:S(2)}) collective-permute-start(bf16[8,16,512]{2,1,0:T(8,128)(2,1)S(1)} %bitcast.45), channel_id=1, source_target_pairs={{0,2},{2,0},{4,6},{6,4},{1,3},{3,1},{5,7},{7,5},{8,10},{10,8},{12,... | collective-permute-start | bytes 393224 | tf_op jit(solution)/shard_map/neg_sum/ppermute | solution.py:19
  52.3 11.5 %collective-permute-start.6 = (bf16[8,16,512]{2,1,0:T(8,128)(2,1)S(1)}, bf16[8,16,512]{2,1,0:T(8,128)(2,1)S(1)}, u32[]{:S(2)}, u32[]{:S(2)}) collective-permute-start(bf16[8,16,512]{2,1,0:T(8,128)(2,1)S(1)} %bitcast.44), channel_id=1, source_target_pairs={{0,6},{2,4},{4,2},{6,0},{1,7},{3,5},{5,3},{7,1},{8,14},{10,12},{12... | collective-permute-start | bytes 393224 | tf_op jit(solution)/shard_map/neg_sum/ppermute | solution.py:19
  56.5 1.1 copy-start
  59.3 0.8 copy-start.15
  66.3 14.1 %collective-permute-start.11 = (bf16[2,256,512]{2,1,0:T(8,128)(2,1)}, bf16[2,256,512]{2,1,0:T(8,128)(2,1)}, u32[]{:S(2)}, u32[]{:S(2)}) collective-permute-start(bf16[2,256,512]{2,1,0:T(8,128)(2,1)} %copy-done.15), channel_id=1, source_target_pairs={{0,64},{64,0},{128,192},{192,128},{1,65},{65,1},{129,193},{193,129... | collective-permute-start | bytes 1572872 | tf_op jit(solution)/shard_map/rel_halves/ppermute | solution.py:19
  82.4 40.8 %all-to-all-start.3 = ((bf16[64,80,128]{2,1,0:T(8,128)(2,1)}), bf16[64,80,128]{2,1,0:T(8,128)(2,1)S(1)}, u32[]{:S(2)}, u32[]{:S(2)}) async-start(bf16[64,80,128]{2,1,0:T(8,128)(2,1)} %pack_negs.1), calls=%async_computation.3 | async-start | bytes 2621440 | tf_op jit(solution)/shard_map/send_heads/all_to_all | solution.py:382
  90.0 1.0 copy-start.21
  91.0 9.7 %collective-permute-start.12 = (bf16[256,512]{1,0:T(8,128)(2,1)S(1)}, bf16[256,512]{1,0:T(8,128)(2,1)S(1)}, u32[]{:S(2)}, u32[]{:S(2)}) collective-permute-start(bf16[256,512]{1,0:T(8,128)(2,1)S(1)} %fusion.3), channel_id=1, source_target_pairs={{0,192},{64,128},{128,64},{192,0},{1,193},{65,129},{129,65},{193,1... | collective-permute-start | bytes 786440 | tf_op jit(solution)/shard_map/rel_column/ppermute | solution.py:19
  102.1 8.0 %collective-permute-start.13 = (f32[8,8,512]{2,1,0:T(8,128)S(1)}, f32[8,8,512]{2,1,0:T(8,128)S(1)}, u32[]{:S(2)}, u32[]{:S(2)}) collective-permute-start(f32[8,8,512]{2,1,0:T(8,128)S(1)} %get-tuple-element.52), channel_id=1, source_target_pairs={{0,2},{2,0},{4,6},{6,4},{1,3},{3,1},{5,7},{7,5},{8,10},{10,8},{12,... | collective-permute-start | bytes 393224 | tf_op jit(solution)/shard_map/rel_column/ppermute | solution.py:19
  102.6 13.2 %collective-permute-start.15 = (f32[8,8,512]{2,1,0:T(8,128)S(1)}, f32[8,8,512]{2,1,0:T(8,128)S(1)}, u32[]{:S(2)}, u32[]{:S(2)}) collective-permute-start(f32[8,8,512]{2,1,0:T(8,128)S(1)} %get-tuple-element.53), channel_id=1, source_target_pairs={{0,4},{2,6},{4,0},{6,2},{1,5},{3,7},{5,1},{7,3},{8,12},{10,14},{12... | collective-permute-start | bytes 393224 | tf_op jit(solution)/shard_map/rel_column/ppermute | solution.py:19
  105.1 12.4 %collective-permute-start.14 = (f32[8,8,512]{2,1,0:T(8,128)S(1)}, f32[8,8,512]{2,1,0:T(8,128)}, u32[]{:S(2)}, u32[]{:S(2)}) collective-permute-start(f32[8,8,512]{2,1,0:T(8,128)S(1)} %get-tuple-element.54), channel_id=1, source_target_pairs={{0,6},{2,4},{4,2},{6,0},{1,7},{3,5},{5,3},{7,1},{8,14},{10,12},{12... | collective-permute-start | bytes 393224 | tf_op jit(solution)/shard_map/rel_column/ppermute | solution.py:19
  123.2 12.4 %all-to-all-start.4 = ((f32[8,8,512]{2,1,0:T(8,128)}), f32[8,8,512]{2,1,0:T(8,128)S(1)}, u32[]{:S(2)}, u32[]{:S(2)}) async-start(f32[8,8,512]{2,1,0:T(8,128)} %fusion.13), calls=%async_computation.4 | async-start | bytes 262144 | tf_op jit(solution)/shard_map/rel_end/all_to_all | solution.py:387
